TPU v7x, 32 devices: a whole 2x2x4 slice. The times are simulated.
32 devices in a mesh: ctx: 16 (over z, y, x), wt: 2 (over core).
Axes of the slice: x: 2, y: 2, z: 4, core: 2. Of those that a mesh axis runs over, the one named last changes fastest.
Arguments:
- tokens: bfloat16 [2, 2048, 2048], P('wt', 'ctx'), may hold values from -6 to 6
- gain_attn: bfloat16 [2048], P('wt'), may hold values from 0.5 to 1.5
- w_query: bfloat16 [2048, 3072], P('wt'), may hold values from -0.125 to 0.125
- w_kv_down: bfloat16 [2048, 576], P('wt'), may hold values from -0.125 to 0.125
- gain_kv: bfloat16 [512], P('wt'), may hold values from 0.5 to 1.5
- w_kv_up: bfloat16 [512, 4096], P('wt'), may hold values from -0.25 to 0.25
- w_out: bfloat16 [2048, 2048], P('wt'), may hold values from -1 to 1
- gain_mlp: bfloat16 [2048], P('wt'), may hold values from 0.5 to 1.5
- w_shared_gate: bfloat16 [2048, 2816], P('wt'), may hold values from -0.125 to 0.125
- w_shared_up: bfloat16 [2048, 2816], P('wt'), may hold values from -0.125 to 0.125
- w_shared_down: bfloat16 [2816, 2048], P('wt'), may hold values from -0.109375 to 0.109375
- w_expert_gate: bfloat16 [16, 2048, 1408], P('ctx', 'wt'), may hold values from -0.125 to 0.125
- w_expert_up: bfloat16 [16, 2048, 1408], P('ctx', 'wt'), may hold values from -0.125 to 0.125
- w_expert_down: bfloat16 [16, 1408, 2048], P('ctx', 'wt'), may hold values from -0.21875 to 0.21875
- block_deal: int32 [32], replicated, may hold values from 0 to 31, as said below
- lengths: int32 [2, 4], P('wt'), may hold values from 1 to 1536, 2048 in all within a row
- routes: int32 [2, 2048, 6], P('wt', 'ctx'), may hold values from 0 to 15, all different within a row; in each aligned block of 128 rows (0 to 127, 128 to 255, ..., all dimensions but the last counted through in order) at most 64 rows name the same one
- gate_weights: float32 [2, 2048, 6], P('wt', 'ctx'), may hold values from 0.16 to 0.64
- cotangent: bfloat16 [2, 2048, 2048], P('wt', 'ctx'), may hold values from -6 to 6
Outputs:
- mixed_out: bfloat16 [2, 2048, 2048], P('wt', 'ctx')
- grad_tokens: float32 [2, 2048, 2048], P('wt', 'ctx')
- grad_gain_attn: float32 [2048], P(('ctx', 'wt'))
- grad_w_query: float32 [2048, 3072], P(None, ('ctx', 'wt'))
- grad_w_kv_down: float32 [2048, 576], P(('ctx', 'wt'))
- grad_gain_kv: float32 [512], P(('ctx', 'wt'))
- grad_w_kv_up: float32 [512, 4096], P(None, ('ctx', 'wt'))
- grad_w_out: float32 [2048, 2048], P(None, ('ctx', 'wt'))
- grad_gain_mlp: float32 [2048], P(('ctx', 'wt'))
- grad_w_shared_gate: float32 [2048, 2816], P(('ctx', 'wt'))
- grad_w_shared_up: float32 [2048, 2816], P(('ctx', 'wt'))
- grad_w_shared_down: float32 [2816, 2048], P(None, ('ctx', 'wt'))
- grad_w_expert_gate: float32 [16, 2048, 1408], P('ctx', 'wt')
- grad_w_expert_up: float32 [16, 2048, 1408], P('ctx', 'wt')
- grad_w_expert_down: float32 [16, 1408, 2048], P('ctx', 'wt')
Inputs may be any that keep to these rules, and one draw needn't show every extreme that they name: Index i of ctx holds the group's blocks block_deal[2i] and block_deal[2i+1], which sum to 31; every block is dealt once. `lengths`: each row sums to 2048, and its largest entry is exactly 1536. `routes`: A token names 6 different experts. In the rows of one device no expert is named by more than 64 rows, a bound that some block reaches.
All inputs are finite; a program needn't handle non-finite values.
Results may differ from a plain program's by a relative error of at most 0.02.
Values may be sent and summed in bfloat16 or wider, within the bound.
No kernel may reach another device: no remote copies, remote signals or barrier semaphores. Data moves between devices by JAX's collectives and lax.ppermute only.
A program may use at most 384 MiB of HBM per device.

v0:
```python
import math

import jax
import jax.numpy as jnp
from jax import lax
from jax.sharding import PartitionSpec as P

D = 2048
H = 16
DN = 128
DR = 64
DV = 128
R = 512
TOP = 6


EPS = 1e-06


def rms_norm(values, gain_in, reduce_axis):
    return (
        values
        * lax.rsqrt(jnp.mean(values * values, axis=reduce_axis, keepdims=True) + EPS)
        * gain_in
    )


def rope_angles(position, rope_width):
    half_width = rope_width // 2
    frequency = jnp.exp(
        jnp.arange(half_width, dtype=jnp.float32) * (-2.0 * math.log(10000.0) / rope_width)
    )
    angles = position.astype(jnp.float32)[:, None] * frequency[None, :]
    return (jnp.cos(angles), jnp.sin(angles))


def rotate(values, cos_table, sin_table, rope_axis):
    half_width = values.shape[rope_axis] // 2
    first_half = lax.slice_in_dim(values, 0, half_width, axis=rope_axis)
    second_half = lax.slice_in_dim(values, half_width, 2 * half_width, axis=rope_axis)
    return jnp.concatenate(
        [
            first_half * cos_table - second_half * sin_table,
            first_half * sin_table + second_half * cos_table,
        ],
        axis=rope_axis,
    )


def gated(gate_in, up_in):
    return jax.nn.silu(gate_in) * up_in


def keep_same(current):
    return current


def contract(former, latter, former_dim, latter_dim):
    return lax.dot_general(
        former,
        latter,
        (((former_dim,), (latter_dim,)), ((), ())),
        preferred_element_type=jnp.float32,
    )


def token_layout(block_deal, lengths_row, first_row, row_count, block_rows):
    row_ids = first_row + jnp.arange(row_count, dtype=jnp.int32)
    blocks = row_ids // block_rows
    block_ids = jnp.arange(block_deal.shape[0], dtype=jnp.int32)
    picked = jnp.sum(
        jnp.where(blocks[:, None] == block_ids[None, :], block_deal[None, :], 0), axis=1
    )
    place_at = picked * block_rows + row_ids % block_rows
    seq_ends = jnp.cumsum(lengths_row)
    past_end = place_at[:, None] >= seq_ends[None, :]
    segment = jnp.sum(past_end.astype(jnp.int32), axis=1)
    seq_start = jnp.sum(jnp.where(past_end, lengths_row[None, :], 0), axis=1)
    return (place_at, segment, place_at - seq_start)


def per_device(
    tokens,
    gain_attn,
    w_query,
    w_kv_down,
    gain_kv,
    w_kv_up,
    w_out,
    gain_mlp,
    w_shared_gate,
    w_shared_up,
    w_shared_down,
    w_expert_gate,
    w_expert_up,
    w_expert_down,
    block_deal,
    lengths,
    routes,
    gate_weights,
    cotangent,
):
    ctx_count = lax.axis_size("ctx")
    token_count = tokens.shape[1]
    group_rows = token_count * ctx_count
    first_row = lax.axis_index("ctx") * token_count
    block_rows = token_count // 2
    score_scale = 1.0 / math.sqrt(DN + DR)
    key_block = min(256, group_rows)
    key_steps = group_rows // key_block
    capacity = min(token_count, 4 * token_count * TOP // (3 * ctx_count))
    lengths_row = lengths[0]
    inputs = tokens[0].astype(jnp.float32)
    grad_out = cotangent[0].astype(jnp.float32)
    route_rows = routes[0]
    gate_rows = gate_weights[0]
    gathered = (
        lax.all_gather(gain_attn, "wt", axis=0, tiled=True),
        lax.all_gather(w_query, "wt", axis=0, tiled=True),
        lax.all_gather(w_kv_down, "wt", axis=0, tiled=True),
        lax.all_gather(gain_kv, "wt", axis=0, tiled=True),
        lax.all_gather(w_kv_up, "wt", axis=0, tiled=True),
        lax.all_gather(w_out, "wt", axis=0, tiled=True),
        lax.all_gather(gain_mlp, "wt", axis=0, tiled=True),
        lax.all_gather(w_shared_gate, "wt", axis=0, tiled=True),
        lax.all_gather(w_shared_up, "wt", axis=0, tiled=True),
        lax.all_gather(w_shared_down, "wt", axis=0, tiled=True),
        lax.all_gather(w_expert_gate, "wt", axis=1, tiled=True),
        lax.all_gather(w_expert_up, "wt", axis=1, tiled=True),
        lax.all_gather(w_expert_down, "wt", axis=1, tiled=True),
    )
    (
        full_gain_attn,
        full_query,
        full_kv_down,
        full_gain_kv,
        full_kv_up,
        full_out,
        full_gain_mlp,
        full_shared_gate,
        full_shared_up,
        full_shared_down,
        full_expert_gate,
        full_expert_up,
        full_expert_down,
    ) = gathered
    gain_one = full_gain_attn.astype(jnp.float32)
    place_q, segment_q, position_q = token_layout(
        block_deal, lengths_row, first_row, token_count, block_rows
    )
    cos_table, sin_table = rope_angles(position_q, DR)
    normed_one = rms_norm(inputs, gain_one, 1).astype(jnp.bfloat16)
    query_all = jnp.dot(normed_one, full_query, preferred_element_type=jnp.float32).reshape(
        token_count, H, DN + DR
    )
    query_nope = query_all[:, :, :DN].astype(jnp.bfloat16)
    query_rope = rotate(
        query_all[:, :, DN:], cos_table[:, None, :], sin_table[:, None, :], 2
    ).astype(jnp.bfloat16)
    kv_up = full_kv_up.reshape(R, H, DN + DV)
    up_key = kv_up[:, :, :DN]
    up_value = kv_up[:, :, DN:]
    query_latent = jnp.einsum(
        "thd,rhd->thr", query_nope, up_key, preferred_element_type=jnp.float32
    ).astype(jnp.bfloat16)
    kv_columns = contract(full_kv_down, normed_one, 0, 1)
    latent_raw = kv_columns[:R]
    rope_raw = kv_columns[R:]
    gain_latent = full_gain_kv.astype(jnp.float32)[:, None]
    latent_cols = rms_norm(latent_raw, gain_latent, 0).astype(jnp.bfloat16)
    key_rope_cols = rotate(rope_raw, cos_table.T, sin_table.T, 0).astype(jnp.bfloat16)
    latent_all, key_rope_all = (
        lax.all_gather(latent_cols, "ctx", axis=1, tiled=True),
        lax.all_gather(key_rope_cols, "ctx", axis=1, tiled=True),
    )
    place_k, segment_k = token_layout(block_deal, lengths_row, 0, group_rows, block_rows)[:2]

    def key_slices(offset):
        return (
            lax.dynamic_slice_in_dim(latent_all, offset, key_block, 1),
            lax.dynamic_slice_in_dim(key_rope_all, offset, key_block, 1),
        )

    def visible_at(offset):
        place_blk = lax.dynamic_slice_in_dim(place_k, offset, key_block, 0)
        segment_blk = lax.dynamic_slice_in_dim(segment_k, offset, key_block, 0)
        same_seq = (segment_blk[None, :] == segment_q[:, None]) & (
            place_blk[None, :] <= place_q[:, None]
        )
        return same_seq[:, None, :]

    def scores_at(latent_blk, rope_blk):
        first_term = jnp.einsum(
            "thr,rk->thk", query_latent, latent_blk, preferred_element_type=jnp.float32
        )
        second_term = jnp.einsum(
            "thd,dk->thk", query_rope, rope_blk, preferred_element_type=jnp.float32
        )
        return (first_term + second_term) * score_scale

    def stats_step(running, block_number):
        offset = block_number * key_block
        visible = visible_at(offset)

        def stats_update(current):
            run_max, run_sum = current
            latent_blk, rope_blk = key_slices(offset)
            masked = jnp.where(visible, scores_at(latent_blk, rope_blk), -1e30)
            new_max = jnp.maximum(run_max, jnp.max(masked, axis=2))
            weights = jnp.where(visible, jnp.exp(masked - new_max[:, :, None]), 0.0)
            return (new_max, run_sum * jnp.exp(run_max - new_max) + jnp.sum(weights, axis=2))

        return (lax.cond(jnp.any(visible), stats_update, keep_same, running), None)

    stats_start = (
        jnp.full((token_count, H), -1e30, jnp.float32),
        jnp.zeros((token_count, H), jnp.float32),
    )
    run_max, run_sum = lax.scan(stats_step, stats_start, jnp.arange(key_steps))[0]
    log_total = run_max + jnp.log(run_sum)

    def output_step(running, block_number):
        offset = block_number * key_block
        visible = visible_at(offset)

        def output_update(current):
            latent_blk, rope_blk = key_slices(offset)
            probs = jnp.where(
                visible, jnp.exp(scores_at(latent_blk, rope_blk) - log_total[:, :, None]), 0.0
            ).astype(jnp.bfloat16)
            return current + jnp.einsum(
                "thk,rk->thr", probs, latent_blk, preferred_element_type=jnp.float32
            )

        return (lax.cond(jnp.any(visible), output_update, keep_same, running), None)

    out_latent = lax.scan(
        output_step, jnp.zeros((token_count, H, R), jnp.float32), jnp.arange(key_steps)
    )[0]
    latent_low = out_latent.astype(jnp.bfloat16)
    heads_out = (
        jnp.einsum("thr,rhv->thv", latent_low, up_value, preferred_element_type=jnp.float32)
        .reshape(token_count, H * DV)
        .astype(jnp.bfloat16)
    )
    residual = inputs + jnp.dot(heads_out, full_out, preferred_element_type=jnp.float32)
    gain_two = full_gain_mlp.astype(jnp.float32)
    normed_two = rms_norm(residual, gain_two, 1).astype(jnp.bfloat16)
    shared_gate = jnp.dot(normed_two, full_shared_gate, preferred_element_type=jnp.float32)
    shared_up = jnp.dot(normed_two, full_shared_up, preferred_element_type=jnp.float32)
    shared_hidden = gated(shared_gate, shared_up).astype(jnp.bfloat16)
    shared_out = jnp.dot(shared_hidden, full_shared_down, preferred_element_type=jnp.float32)
    expert_ids = jnp.arange(ctx_count, dtype=jnp.int32)
    flat_route = route_rows.reshape(token_count * TOP)
    onehot = (flat_route[:, None] == expert_ids[None, :]).astype(jnp.int32)
    earlier = jnp.cumsum(onehot, axis=0) - onehot
    slot_rank = jnp.sum(earlier * onehot, axis=1)
    slot_index = flat_route * capacity + slot_rank
    expanded = jnp.repeat(normed_two, TOP, axis=0)
    outgoing = (
        jnp.zeros((ctx_count * capacity, D), jnp.bfloat16)
        .at[slot_index]
        .set(expanded, unique_indices=True)
        .reshape(ctx_count, capacity, D)
    )
    gate_matrix = full_expert_gate[0]
    up_matrix = full_expert_up[0]
    down_matrix = full_expert_down[0]
    arrived = lax.all_to_all(outgoing, "ctx", split_axis=0, concat_axis=0, tiled=True)
    rows_in = arrived.reshape(-1, D)
    gate_pre = jnp.dot(rows_in, gate_matrix, preferred_element_type=jnp.float32)
    up_pre = jnp.dot(rows_in, up_matrix, preferred_element_type=jnp.float32)
    hidden = gated(gate_pre, up_pre).astype(jnp.bfloat16)
    produced = jnp.dot(hidden, down_matrix, preferred_element_type=jnp.float32).astype(jnp.bfloat16)
    expert_out = produced.reshape(arrived.shape)
    returned = lax.all_to_all(expert_out, "ctx", split_axis=0, concat_axis=0, tiled=True)
    picked_rows = (
        jnp.take(returned.reshape(-1, D), slot_index, axis=0)
        .astype(jnp.float32)
        .reshape(token_count, TOP, D)
    )
    routed = jnp.sum(gate_rows[:, :, None] * picked_rows, axis=1)
    mixed_out = (residual + shared_out + routed).astype(jnp.bfloat16)
    gathered = (
        lax.all_gather(gain_attn, "wt", axis=0, tiled=True),
        lax.all_gather(w_query, "wt", axis=0, tiled=True),
        lax.all_gather(w_kv_down, "wt", axis=0, tiled=True),
        lax.all_gather(gain_kv, "wt", axis=0, tiled=True),
        lax.all_gather(w_kv_up, "wt", axis=0, tiled=True),
        lax.all_gather(w_out, "wt", axis=0, tiled=True),
        lax.all_gather(gain_mlp, "wt", axis=0, tiled=True),
        lax.all_gather(w_shared_gate, "wt", axis=0, tiled=True),
        lax.all_gather(w_shared_up, "wt", axis=0, tiled=True),
        lax.all_gather(w_shared_down, "wt", axis=0, tiled=True),
        lax.all_gather(w_expert_gate, "wt", axis=1, tiled=True),
        lax.all_gather(w_expert_up, "wt", axis=1, tiled=True),
        lax.all_gather(w_expert_down, "wt", axis=1, tiled=True),
    )
    (
        full_gain_attn,
        full_query,
        full_kv_down,
        full_gain_kv,
        full_kv_up,
        full_out,
        full_gain_mlp,
        full_shared_gate,
        full_shared_up,
        full_shared_down,
        full_expert_gate,
        full_expert_up,
        full_expert_down,
    ) = gathered
    kv_up = full_kv_up.reshape(R, H, DN + DV)
    up_key = kv_up[:, :, :DN]
    up_value = kv_up[:, :, DN:]
    gate_matrix = full_expert_gate[0]
    up_matrix = full_expert_up[0]
    down_matrix = full_expert_down[0]
    grad_shared = grad_out.astype(jnp.bfloat16)
    grad_w_shared_down = contract(shared_hidden, grad_shared, 0, 0)
    grad_shared_hidden = contract(grad_shared, full_shared_down, 1, 1)
    shared_pull = jax.vjp(gated, shared_gate, shared_up)[1]
    grad_shared_gate, grad_shared_up = shared_pull(grad_shared_hidden)
    grad_shared_gate = grad_shared_gate.astype(jnp.bfloat16)
    grad_shared_up = grad_shared_up.astype(jnp.bfloat16)
    grad_w_shared_gate = contract(normed_two, grad_shared_gate, 0, 0)
    grad_w_shared_up = contract(normed_two, grad_shared_up, 0, 0)
    grad_normed_two = contract(grad_shared_gate, full_shared_gate, 1, 1) + contract(
        grad_shared_up, full_shared_up, 1, 1
    )
    slot_grads = (
        (gate_rows[:, :, None] * grad_out[:, None, :])
        .reshape(token_count * TOP, D)
        .astype(jnp.bfloat16)
    )
    outgoing_grads = (
        jnp.zeros((ctx_count * capacity, D), jnp.bfloat16)
        .at[slot_index]
        .set(slot_grads, unique_indices=True)
        .reshape(ctx_count, capacity, D)
    )
    arrived_grads = lax.all_to_all(outgoing_grads, "ctx", split_axis=0, concat_axis=0, tiled=True)
    rows_in = arrived.reshape(-1, D)
    rows_grad = arrived_grads.reshape(-1, D)
    expert_gate_pre = jnp.dot(rows_in, gate_matrix, preferred_element_type=jnp.float32)
    expert_up_pre = jnp.dot(rows_in, up_matrix, preferred_element_type=jnp.float32)
    expert_hidden = gated(expert_gate_pre, expert_up_pre).astype(jnp.bfloat16)
    grad_expert_down = contract(expert_hidden, rows_grad, 0, 0)
    grad_expert_hidden = contract(rows_grad, down_matrix, 1, 1)
    expert_pull = jax.vjp(gated, expert_gate_pre, expert_up_pre)[1]
    grad_expert_gate_pre, grad_expert_up_pre = expert_pull(grad_expert_hidden)
    grad_expert_gate_pre = grad_expert_gate_pre.astype(jnp.bfloat16)
    grad_expert_up_pre = grad_expert_up_pre.astype(jnp.bfloat16)
    grad_expert_gate = contract(rows_in, grad_expert_gate_pre, 0, 0)
    grad_expert_up = contract(rows_in, grad_expert_up_pre, 0, 0)
    grad_rows = (
        (
            contract(grad_expert_gate_pre, gate_matrix, 1, 1)
            + contract(grad_expert_up_pre, up_matrix, 1, 1)
        )
        .astype(jnp.bfloat16)
        .reshape(arrived.shape)
    )
    sent_back = lax.all_to_all(grad_rows, "ctx", split_axis=0, concat_axis=0, tiled=True)
    grad_routed = jnp.sum(
        jnp.take(sent_back.reshape(-1, D), slot_index, axis=0)
        .astype(jnp.float32)
        .reshape(token_count, TOP, D),
        axis=1,
    )
    grad_normed_two = grad_normed_two + grad_routed
    expert_sums = (
        lax.psum_scatter(
            grad_expert_gate[None].astype(jnp.bfloat16), "wt", scatter_dimension=1, tiled=True
        ).astype(jnp.float32),
        lax.psum_scatter(
            grad_expert_up[None].astype(jnp.bfloat16), "wt", scatter_dimension=1, tiled=True
        ).astype(jnp.float32),
        lax.psum_scatter(
            grad_expert_down[None].astype(jnp.bfloat16), "wt", scatter_dimension=1, tiled=True
        ).astype(jnp.float32),
    )
    norm_two_pull = jax.vjp(
        lambda values, gain_in: rms_norm(values, gain_in, 1), residual, gain_two
    )[1]
    grad_residual_part, grad_gain_mlp = norm_two_pull(grad_normed_two)
    grad_residual = grad_out + grad_residual_part
    grad_attn = grad_residual.astype(jnp.bfloat16)
    grad_w_out = contract(heads_out, grad_attn, 0, 0)
    grad_heads = (
        contract(grad_attn, full_out, 1, 1).astype(jnp.bfloat16).reshape(token_count, H, DV)
    )
    grad_up_value = jnp.einsum(
        "thr,thv->rhv", latent_low, grad_heads, preferred_element_type=jnp.float32
    )
    grad_latent_out = jnp.einsum(
        "thv,rhv->thr", grad_heads, up_value, preferred_element_type=jnp.float32
    ).astype(jnp.bfloat16)
    delta = jnp.sum(grad_latent_out.astype(jnp.float32) * out_latent, axis=2)

    def back_step(running, block_number):
        offset = block_number * key_block
        visible = visible_at(offset)

        def back_update(current):
            acc_latent, acc_rope, grad_latent_all, grad_rope_all = current
            latent_blk, rope_blk = key_slices(offset)
            probs = jnp.where(
                visible, jnp.exp(scores_at(latent_blk, rope_blk) - log_total[:, :, None]), 0.0
            )
            grad_probs = jnp.einsum(
                "thr,rk->thk", grad_latent_out, latent_blk, preferred_element_type=jnp.float32
            )
            grad_scores = (probs * (grad_probs - delta[:, :, None])).astype(jnp.bfloat16)
            acc_latent = acc_latent + score_scale * jnp.einsum(
                "thk,rk->thr", grad_scores, latent_blk, preferred_element_type=jnp.float32
            )
            acc_rope = acc_rope + score_scale * jnp.einsum(
                "thk,dk->thd", grad_scores, rope_blk, preferred_element_type=jnp.float32
            )
            latent_term = score_scale * jnp.einsum(
                "thk,thr->rk", grad_scores, query_latent, preferred_element_type=jnp.float32
            )
            latent_term = latent_term + jnp.einsum(
                "thk,thr->rk",
                probs.astype(jnp.bfloat16),
                grad_latent_out,
                preferred_element_type=jnp.float32,
            )
            rope_term = score_scale * jnp.einsum(
                "thk,thd->dk", grad_scores, query_rope, preferred_element_type=jnp.float32
            )
            grad_latent_all = lax.dynamic_update_slice_in_dim(
                grad_latent_all, latent_term, offset, 1
            )
            grad_rope_all = lax.dynamic_update_slice_in_dim(grad_rope_all, rope_term, offset, 1)
            return (acc_latent, acc_rope, grad_latent_all, grad_rope_all)

        return (lax.cond(jnp.any(visible), back_update, keep_same, running), None)

    back_start = (
        jnp.zeros((token_count, H, R), jnp.float32),
        jnp.zeros((token_count, H, DR), jnp.float32),
        jnp.zeros((R, group_rows), jnp.float32),
        jnp.zeros((DR, group_rows), jnp.float32),
    )
    acc_latent, acc_rope, grad_latent_all, grad_rope_all = lax.scan(
        back_step, back_start, jnp.arange(key_steps)
    )[0]
    grad_latent_mine, grad_rope_mine = (
        lax.psum_scatter(
            grad_latent_all.astype(jnp.bfloat16), "ctx", scatter_dimension=1, tiled=True
        ).astype(jnp.float32),
        lax.psum_scatter(
            grad_rope_all.astype(jnp.bfloat16), "ctx", scatter_dimension=1, tiled=True
        ).astype(jnp.float32),
    )
    grad_query_latent = acc_latent.astype(jnp.bfloat16)
    grad_up_key = jnp.einsum(
        "thr,thd->rhd", grad_query_latent, query_nope, preferred_element_type=jnp.float32
    )
    grad_query_nope = jnp.einsum(
        "thr,rhd->thd", grad_query_latent, up_key, preferred_element_type=jnp.float32
    )
    query_rope_pull = jax.vjp(
        lambda values: rotate(values, cos_table[:, None, :], sin_table[:, None, :], 2),
        query_all[:, :, DN:],
    )[1]
    grad_query_rope = query_rope_pull(acc_rope)[0]
    grad_query = (
        jnp.concatenate([grad_query_nope, grad_query_rope], axis=2)
        .reshape(token_count, H * (DN + DR))
        .astype(jnp.bfloat16)
    )
    grad_w_query = contract(normed_one, grad_query, 0, 0)
    grad_normed_one = contract(grad_query, full_query, 1, 1)
    latent_pull = jax.vjp(
        lambda values, gain_in: rms_norm(values, gain_in, 0), latent_raw, gain_latent
    )[1]
    grad_latent_raw, grad_gain_kv = latent_pull(grad_latent_mine)
    key_rope_pull = jax.vjp(lambda values: rotate(values, cos_table.T, sin_table.T, 0), rope_raw)[1]
    grad_rope_raw = key_rope_pull(grad_rope_mine)[0]
    grad_kv_columns = jnp.concatenate([grad_latent_raw, grad_rope_raw], axis=0).astype(jnp.bfloat16)
    grad_w_kv_down = contract(normed_one, grad_kv_columns, 0, 1)
    grad_normed_one = grad_normed_one + contract(grad_kv_columns, full_kv_down, 0, 1)
    grad_w_kv_up = jnp.concatenate([grad_up_key, grad_up_value], axis=2).reshape(R, H * (DN + DV))
    norm_one_pull = jax.vjp(lambda values, gain_in: rms_norm(values, gain_in, 1), inputs, gain_one)[
        1
    ]
    grad_inputs_part, grad_gain_attn = norm_one_pull(grad_normed_one)
    grad_tokens = grad_residual + grad_inputs_part
    grad_gain_kv = grad_gain_kv.reshape(R)
    dense_sums = (
        lax.psum_scatter(grad_gain_attn, ("ctx", "wt"), scatter_dimension=0, tiled=True),
        lax.psum_scatter(grad_w_query, ("ctx", "wt"), scatter_dimension=1, tiled=True),
        lax.psum_scatter(grad_w_kv_down, ("ctx", "wt"), scatter_dimension=0, tiled=True),
        lax.psum_scatter(grad_gain_kv, ("ctx", "wt"), scatter_dimension=0, tiled=True),
        lax.psum_scatter(grad_w_kv_up, ("ctx", "wt"), scatter_dimension=1, tiled=True),
        lax.psum_scatter(grad_w_out, ("ctx", "wt"), scatter_dimension=1, tiled=True),
        lax.psum_scatter(grad_gain_mlp, ("ctx", "wt"), scatter_dimension=0, tiled=True),
        lax.psum_scatter(grad_w_shared_gate, ("ctx", "wt"), scatter_dimension=0, tiled=True),
        lax.psum_scatter(grad_w_shared_up, ("ctx", "wt"), scatter_dimension=0, tiled=True),
        lax.psum_scatter(grad_w_shared_down, ("ctx", "wt"), scatter_dimension=1, tiled=True),
    )
    return (
        mixed_out[None],
        grad_tokens[None],
        dense_sums[0],
        dense_sums[1],
        dense_sums[2],
        dense_sums[3],
        dense_sums[4],
        dense_sums[5],
        dense_sums[6],
        dense_sums[7],
        dense_sums[8],
        dense_sums[9],
        expert_sums[0],
        expert_sums[1],
        expert_sums[2],
    )


def solution(mesh):
    placed = (
        P("wt", "ctx", None),
        P("wt"),
        P("wt", None),
        P("wt", None),
        P("wt"),
        P("wt", None),
        P("wt", None),
        P("wt"),
        P("wt", None),
        P("wt", None),
        P("wt", None),
        P("ctx", "wt", None),
        P("ctx", "wt", None),
        P("ctx", "wt", None),
        P(),
        P("wt", None),
        P("wt", "ctx", None),
        P("wt", "ctx", None),
        P("wt", "ctx", None),
    )
    return jax.shard_map(
        per_device,
        mesh=mesh,
        in_specs=placed,
        out_specs=(
            P("wt", "ctx", None),
            P("wt", "ctx", None),
            P(("ctx", "wt")),
            P(None, ("ctx", "wt")),
            P(("ctx", "wt"), None),
            P(("ctx", "wt")),
            P(None, ("ctx", "wt")),
            P(None, ("ctx", "wt")),
            P(("ctx", "wt")),
            P(("ctx", "wt"), None),
            P(("ctx", "wt"), None),
            P(None, ("ctx", "wt")),
            P("ctx", "wt", None),
            P("ctx", "wt", None),
            P("ctx", "wt", None),
        ),
        check_vma=False,
    )
```

profile of v0, /device:TPU:0, one launch (start us, length us, event | category | flops | bytes accessed | tf_op | source)
XLA Modules:
  0.0 2689.4 jit_solution(3145566084012189424)
XLA Ops:
  13.7 9.5 all-gather.13.cloned.1.call-done
  48.7 14.5 scatter_custom_fusion.1
  73.7 124.7 %all_gather.61 = bf16[64,2048]{1,0:T(8,128)(2,1)} all-gather(bf16[64,128]{1,0:T(8,128)(2,1)S(1)} %pad_maximum_fusion.5), channel_id=1, replica_groups=mesh['ctx'=16,'wt'=2] {'ctx'}, dimensions={1}, use_global_device_ids=true | all-gather | bytes 278528 | tf_op jit(solution)/shard_map/all_gather | solution.py:174
  202.6 16.9 copy.106
  231.5 51.5 %while.41 = (s32[]{:T(128)}, f32[128,16]{0,1:T(8,128)S(1)}, f32[128,16]{0,1:T(8,128)S(1)}, s32[8]{0:T(128)S(1)}, s32[2048]{0:T(1024)S(1)}, /*index=5*/s32[128]{0...) while((s32[]{:T(128)}, f32[128,16]{0,1:T(8,128)S(1)}, ...), condition=%wide.region_14.15_spmd, body=%wide.region_8.14_spmd.sunk | while | flops 607784960 | bytes 11255159 | solution.py:219
  285.7 97.7 %while.42 = (s32[]{:T(128)}, f32[128,16,512]{2,0,1:T(8,128)}, s32[8]{0:T(128)S(1)}, s32[2048]{0:T(1024)S(1)}, s32[128]{0:T(128)S(1)}, /*index=5*/s32[2048]{0:T(1...) while((s32[]{:T(128)}, f32[128,16,512]{2,0,1:T(8,128)}, ...), condition=%wide.region_19.20_spmd, body=%wide.region_15.19_spmd.sunk | while | flops 1144651776 | bytes 15581523 | solution.py:237
  405.7 10.6 scatter_custom_fusion
  416.4 12.3 all-to-all-start
  429.3 12.0 fusion.56
  441.3 62.5 %all-to-all-done = bf16[16,64,2048]{2,1,0:T(8,128)(2,1)} async-done(((bf16[16,64,2048]{2,1,0:T(8,128)(2,1)}), bf16[16,64,2048]{2,1,0:T(8,128)(2,1)}, u32[]{:S(2)}, u32[]{:S(2)}) %all-to-all-start) | async-done | bytes 4194336 | tf_op jit(solution)/shard_map/all_to_all | solution.py:269
  503.7 11.7 fusion.62
  515.4 16.1 fusion.55
  540.5 10.7 add_convert_fusion
  551.2 19.1 all-to-all-start.3
  571.0 10.9 fusion.69
  581.9 66.3 %all-to-all-done.3 = bf16[16,64,2048]{2,1,0:T(8,128)(2,1)} async-done(((bf16[16,64,2048]{2,1,0:T(8,128)(2,1)}), bf16[16,64,2048]{2,1,0:T(8,128)(2,1)}, u32[]{:S(2)}, u32[]{:S(2)}) %all-to-all-start.3) | async-done | bytes 4194336 | tf_op jit(solution)/shard_map/all_to_all | solution.py:365
  648.2 18.4 all-to-all-start.1
  679.8 10.0 multiply_convert_fusion.4
  699.0 9.5 gather_fusion.1
  708.5 36.5 %all-to-all-done.1 = bf16[16,64,2048]{2,1,0:T(8,128)(2,1)} async-done(((bf16[16,64,2048]{2,1,0:T(8,128)(2,1)}), bf16[16,64,2048]{2,1,0:T(8,128)(2,1)}, u32[]{:S(2)}, u32[]{:S(2)}) %all-to-all-start.1) | async-done | bytes 4194336 | tf_op jit(solution)/shard_map/all_to_all | solution.py:276
  745.0 9.8 gather_fusion
  801.5 169.1 %while.43 = (s32[]{:T(128)}, f32[128,16,512]{2,0,1:T(8,128)}, f32[128,16,64]{0,2,1:T(8,128)}, bf16[512,2048]{0,1:T(8,128)(2,1)}, bf16[64,2048]{1,0:T(8,128)(2,1)...) while((s32[]{:T(128)}, f32[128,16,512]{2,0,1:T(8,128)}, ...), condition=%wide.region_34.36_spmd, body=%wide.region_30.35_spmd.sunk | while | flops 2892791808 | bytes 78896720 | solution.py:448
  805.9 17.1 conditional.8
  827.2 17.1 conditional.8
  848.4 17.1 conditional.8
  869.6 17.1 conditional.8
  890.9 17.1 conditional.8
  912.1 17.1 conditional.8
  933.3 17.1 conditional.8
  954.6 16.1 conditional.8
  978.2 11.0 fusion.50
  991.0 11.2 fusion.51
  1004.1 10.7 fusion.52
  1015.0 48.1 %reduce-scatter.39.cloned.1.call-done = bf16[128,64]{1,0:T(8,128)(2,1)} async-done(((bf16[2048,64]{1,0:T(8,128)(2,1)}), bf16[128,64]{1,0:T(8,128)(2,1)}) %reduce-scatter.39.cloned.1.call-update) | async-done | bytes 16400
  1064.1 78.3 %reduce-scatter.37.cloned.1.call-done = bf16[128,512]{1,0:T(8,128)(2,1)} async-done(((bf16[2048,512]{1,0:T(8,128)(2,1)}), bf16[128,512]{1,0:T(8,128)(2,1)}) %reduce-scatter.37.cloned.1.call-update) | async-done | bytes 131088
  1169.6 9.6 fusion.182
  1180.3 11.9 fusion.183
  1193.5 9.5 fusion.118
  1208.6 10.4 fusion.124
  1244.3 10.1 fusion.181
  1275.0 37.8 %all-reduce.7 = (f32[2048]{0:T(1024)S(1)}, f32[512]{0:T(512)S(1)}, f32[2048]{0:T(1024)S(1)}) all-reduce(f32[2048]{0:T(1024)S(1)} %get-tuple-element.513, f32[512]{0:T(512)S(1)} %get-tuple-element.515, f32[2048]{0:T(1024)S(1)} %copy-done.57), channel_id=4, replica_groups=mesh['ctx'=16,'wt'=2] {'ctx','wt'}, use_global_device_ids=true, to_apply=%region_40.42.clone | all-reduce | flops 4608 | bytes 36864
  1317.0 21.1 reduce-scatter.19.cloned.1.call-done
  1338.1 147.4 %reduce-scatter.21.cloned.1.call-done = f32[512,128]{1,0:T(8,128)} async-done(((f32[512,4096]{1,0:T(8,128)}), f32[512,128]{1,0:T(8,128)}) %reduce-scatter.21.cloned.1.call-update) | async-done | bytes 262160 | tf_op jit(solution)/shard_map/reduce_scatter | solution.py:499
  1485.5 245.0 %reduce-scatter.25.cloned.1.call-done = f32[64,2816]{1,0:T(8,128)} async-done(((f32[2048,2816]{1,0:T(8,128)}), f32[64,2816]{1,0:T(8,128)}) %reduce-scatter.25.cloned.1.call-update) | async-done | bytes 720912 | tf_op jit(solution)/shard_map/reduce_scatter | solution.py:502
  1730.5 254.2 %reduce-scatter.27.cloned.1.call-done = f32[64,2816]{1,0:T(8,128)} async-done(((f32[2048,2816]{1,0:T(8,128)}), f32[64,2816]{1,0:T(8,128)}) %reduce-scatter.27.cloned.1.call-update) | async-done | bytes 720912 | tf_op jit(solution)/shard_map/reduce_scatter | solution.py:503
  1984.6 254.3 %reduce-scatter.29.cloned.1.call-done = f32[2816,64]{0,1:T(8,128)} async-done(((f32[2816,2048]{0,1:T(8,128)}), f32[2816,64]{0,1:T(8,128)}) %reduce-scatter.29.cloned.1.call-update) | async-done | bytes 720912 | tf_op jit(solution)/shard_map/reduce_scatter | solution.py:504
  2238.9 257.7 %reduce-scatter.17.cloned.1.call-done = f32[2048,96]{0,1:T(8,128)} async-done(((f32[2048,3072]{0,1:T(8,128)}), f32[2048,96]{0,1:T(8,128)}) %reduce-scatter.17.cloned.1.call-update) | async-done | bytes 786448 | tf_op jit(solution)/shard_map/reduce_scatter | solution.py:496
  2496.6 186.1 %reduce-scatter.23.cloned.1.call-done = f32[2048,64]{0,1:T(8,128)} async-done(((f32[2048,2048]{0,1:T(8,128)}), f32[2048,64]{0,1:T(8,128)}) %reduce-scatter.23.cloned.1.call-update) | async-done | bytes 524304 | tf_op jit(solution)/shard_map/reduce_scatter | solution.py:500
  (652 shorter events, 648.2 us)
Async XLA Ops:
  7.2 16.1 all-gather.13.cloned.1.call-start
  7.9 190.5 %all-gather.15.cloned.1.call-start = ((), (), s32[]{:S(2)}) async-start(), calls=%async_computation.17 | async-start | bytes 2228224 | tf_op jit(solution)/shard_map/all_gather | solution.py:173
  10.0 209.5 %copy-start.41 = (f32[2048]{0:T(1024)}, f32[2048]{0:T(1024)S(1)}, u32[]{:S(2)}) copy-start(f32[2048]{0:T(1024)S(1)} %convert_element_type.209) | copy-start | bytes 24580
  13.7 205.8 %copy-start.60 = (f32[128]{0:T(128)}, f32[128]{0:T(128)S(1)}, u32[]{:S(2)}) copy-start(f32[128]{0:T(128)S(1)} %fusion.169) | copy-start | bytes 1540
  26.0 47.6 %copy-start.22 = (f32[576,128]{1,0:T(8,128)}, f32[576,128]{1,0:T(8,128)S(1)}, u32[]{:S(2)}) copy-start(f32[576,128]{1,0:T(8,128)S(1)} %convolution_bitcast_fusion.5) | copy-start | bytes 884740
  26.9 175.7 %all-gather.17.cloned.1.call-start = ((), (), s32[]{:S(2)}) async-start(), calls=%async_computation.18 | async-start | bytes 18874368 | tf_op jit(solution)/shard_map/all_gather | solution.py:119
  27.6 201.2 %all-gather.19.cloned.1.call-start = ((), (), s32[]{:S(2)}) async-start(), calls=%async_computation.19 | async-start | bytes 6291456 | tf_op jit(solution)/shard_map/all_gather | solution.py:122
  30.2 360.4 %all-gather.21.cloned.1.call-start = ((), (), s32[]{:S(2)}) async-start(), calls=%async_computation.20 | async-start | bytes 12582912 | tf_op jit(solution)/shard_map/all_gather | solution.py:123
  30.8 398.5 %all-gather.33.cloned.1.call-start = ((), (), s32[]{:S(2)}) async-start(), calls=%async_computation.26 | async-start | bytes 8650752 | tf_op jit(solution)/shard_map/all_gather | solution.py:130
  31.4 409.9 %all-gather.31.cloned.1.call-start = ((), (), s32[]{:S(2)}) async-start(), calls=%async_computation.25 | async-start | bytes 8650752 | tf_op jit(solution)/shard_map/all_gather | solution.py:129
  32.1 483.3 %all-gather.29.cloned.1.call-start = ((), (), s32[]{:S(2)}) async-start(), calls=%async_computation.24 | async-start | bytes 8650752 | tf_op jit(solution)/shard_map/all_gather | solution.py:128
  63.3 353.1 %all-to-all-start.2 = ((bf16[16,64,2048]{2,1,0:T(8,128)(2,1)}), bf16[16,64,2048]{2,1,0:T(8,128)(2,1)}, u32[]{:S(2)}, u32[]{:S(2)}) async-start(bf16[16,64,2048]{2,1,0:T(8,128)(2,1)} %bitcast.279), calls=%async_computation.2 | async-start | bytes 8388608 | tf_op jit(solution)/shard_map/all_to_all | solution.py:343
  70.2 596.5 %all-gather.23.cloned.1.call-start = ((), (), s32[]{:S(2)}) async-start(), calls=%async_computation.21 | async-start | bytes 17301504 | tf_op jit(solution)/shard_map/all_gather | solution.py:125
  71.5 148.0 %copy-start.63 = (f32[128]{0:T(128)}, f32[128]{0:T(128)S(1)}, u32[]{:S(2)}) copy-start(f32[128]{0:T(128)S(1)} %subtract_convert_fusion.1) | copy-start | bytes 1540
  71.5 148.0 %copy-start.65 = (f32[32]{0:T(128)}, f32[32]{0:T(128)S(1)}, u32[]{:S(2)}) copy-start(f32[32]{0:T(128)S(1)} %multiply_exponential_fusion) | copy-start | bytes 388
  73.5 154.1 %copy-start.43 = (f32[128,32]{0,1:T(8,128)}, f32[128,32]{0,1:T(8,128)S(1)}, u32[]{:S(2)}) copy-start(f32[128,32]{0,1:T(8,128)S(1)} %get-tuple-element.630) | copy-start | bytes 49156
  73.6 154.1 %copy-start.45 = (f32[128,32]{0,1:T(8,128)}, f32[128,32]{0,1:T(8,128)S(1)}, u32[]{:S(2)}) copy-start(f32[128,32]{0,1:T(8,128)S(1)} %get-tuple-element.631) | copy-start | bytes 49156
  396.7 276.0 %copy-start.13 = (bf16[128,2048]{1,0:T(8,128)(2,1)}, bf16[128,2048]{1,0:T(8,128)(2,1)S(1)}, u32[]{:S(2)}) copy-start(bf16[128,2048]{1,0:T(8,128)(2,1)S(1)} %multiply_convert_fusion.6) | copy-start | bytes 1572868
  416.4 87.4 %all-to-all-start = ((bf16[16,64,2048]{2,1,0:T(8,128)(2,1)}), bf16[16,64,2048]{2,1,0:T(8,128)(2,1)}, u32[]{:S(2)}, u32[]{:S(2)}) async-start(bf16[16,64,2048]{2,1,0:T(8,128)(2,1)} %bitcast.280), calls=%async_computation | async-start | bytes 8388608 | tf_op jit(solution)/shard_map/all_to_all | solution.py:269
  428.7 244.0 %all-gather.25.cloned.1.call-start = ((), (), s32[]{:S(2)}) async-start(), calls=%async_computation.22 | async-start | bytes 17301504 | tf_op jit(solution)/shard_map/all_gather | solution.py:126
  551.2 97.0 %all-to-all-start.3 = ((bf16[16,64,2048]{2,1,0:T(8,128)(2,1)}), bf16[16,64,2048]{2,1,0:T(8,128)(2,1)}, u32[]{:S(2)}, u32[]{:S(2)}) async-start(bf16[16,64,2048]{2,1,0:T(8,128)(2,1)} %bitcast.291), calls=%async_computation.3 | async-start | bytes 8388608 | tf_op jit(solution)/shard_map/all_to_all | solution.py:365
  570.3 109.5 %all-gather.27.cloned.1.call-start = ((), (), s32[]{:S(2)}) async-start(), calls=%async_computation.23 | async-start | bytes 17301504 | tf_op jit(solution)/shard_map/all_gather | solution.py:127
  648.2 18.4 copy-start.54
  648.2 18.4 copy-start.56
  648.2 96.8 %all-to-all-start.1 = ((bf16[16,64,2048]{2,1,0:T(8,128)(2,1)}), bf16[16,64,2048]{2,1,0:T(8,128)(2,1)}, u32[]{:S(2)}, u32[]{:S(2)}) async-start(bf16[16,64,2048]{2,1,0:T(8,128)(2,1)} %bitcast.290), calls=%async_computation.1 | async-start | bytes 8388608 | tf_op jit(solution)/shard_map/all_to_all | solution.py:276
  666.6 396.5 %reduce-scatter.39.cloned.1.call-start = ((), (), s32[]{:S(2)}) async-start(), calls=%async_computation.38 | async-start | bytes 557056
  972.6 169.8 %reduce-scatter.37.cloned.1.call-start = ((), (), s32[]{:S(2)}) async-start(), calls=%async_computation.37 | async-start | bytes 2228224
  978.2 280.3 %reduce-scatter.31.cloned.1.call-start = ((), (), s32[]{:S(2)}) async-start(), calls=%async_computation.34 | async-start | bytes 8650752 | tf_op jit(solution)/shard_map/reduce_scatter | solution.py:374
  989.2 274.0 %reduce-scatter.33.cloned.1.call-start = ((), (), s32[]{:S(2)}) async-start(), calls=%async_computation.35 | async-start | bytes 8650752 | tf_op jit(solution)/shard_map/reduce_scatter | solution.py:377
  1002.3 265.7 %reduce-scatter.35.cloned.1.call-start = ((), (), s32[]{:S(2)}) async-start(), calls=%async_computation.36 | async-start | bytes 8650752 | tf_op jit(solution)/shard_map/reduce_scatter | solution.py:380
  1014.8 49.1 %copy-start.64 = (f32[128]{0:T(128)S(1)}, f32[128]{0:T(128)}, u32[]{:S(2)}) copy-start(f32[128]{0:T(128)} %copy-done.63) | copy-start | bytes 1540
  1014.8 49.1 %copy-start.66 = (f32[32]{0:T(128)S(1)}, f32[32]{0:T(128)}, u32[]{:S(2)}) copy-start(f32[32]{0:T(128)} %copy-done.65) | copy-start | bytes 388
  1014.8 128.6 %copy-start.23 = (f32[576,128]{1,0:T(8,128)S(1)}, f32[576,128]{1,0:T(8,128)}, u32[]{:S(2)}) copy-start(f32[576,128]{1,0:T(8,128)} %copy-done.22) | copy-start | bytes 884740
  1014.8 128.6 %copy-start.59 = (f32[2,1,256]{2,1,0:T(1,128)S(1)}, f32[2,1,256]{2,1,0:T(1,128)}, u32[]{:S(2)}) copy-start(f32[2,1,256]{2,1,0:T(1,128)} %copy-done.58) | copy-start | bytes 6148
  1014.8 128.6 %copy-start.68 = (f32[128]{0:T(128)S(1)}, f32[128]{0:T(128)}, u32[]{:S(2)}) copy-start(f32[128]{0:T(128)} %copy-done.67) | copy-start | bytes 1540
  1014.8 128.9 %copy-start.74 = (f32[128]{0:T(128)S(1)}, f32[128]{0:T(128)}, u32[]{:S(2)}) copy-start(f32[128]{0:T(128)} %copy-done.73) | copy-start | bytes 1540
  1014.8 129.0 %copy-start.9 = (bf16[1,128,2048]{2,1,0:T(8,128)(2,1)S(1)}, bf16[1,128,2048]{2,1,0:T(8,128)(2,1)}, u32[]{:S(2)}) copy-start(bf16[1,128,2048]{2,1,0:T(8,128)(2,1)} %param.33) | copy-start | bytes 1572868
  1014.9 129.0 %copy-start.42 = (f32[2048]{0:T(1024)S(1)}, f32[2048]{0:T(1024)}, u32[]{:S(2)}) copy-start(f32[2048]{0:T(1024)} %copy-done.41) | copy-start | bytes 24580
  1014.9 129.0 %copy-start.61 = (f32[128]{0:T(128)S(1)}, f32[128]{0:T(128)}, u32[]{:S(2)}) copy-start(f32[128]{0:T(128)} %copy-done.60) | copy-start | bytes 1540
  1014.9 323.2 %reduce-scatter.19.cloned.1.call-start = ((), (), s32[]{:S(2)}) async-start(), calls=%async_computation.28 | async-start | bytes 5406720 | tf_op jit(solution)/shard_map/reduce_scatter | solution.py:497
  1147.2 338.2 %reduce-scatter.21.cloned.1.call-start = ((), (), s32[]{:S(2)}) async-start(), calls=%async_computation.29 | async-start | bytes 8650752 | tf_op jit(solution)/shard_map/reduce_scatter | solution.py:499
  1168.0 562.5 %reduce-scatter.25.cloned.1.call-start = ((), (), s32[]{:S(2)}) async-start(), calls=%async_computation.31 | async-start | bytes 23789568 | tf_op jit(solution)/shard_map/reduce_scatter | solution.py:502
  1179.2 805.4 %reduce-scatter.27.cloned.1.call-start = ((), (), s32[]{:S(2)}) async-start(), calls=%async_computation.32 | async-start | bytes 23789568 | tf_op jit(solution)/shard_map/reduce_scatter | solution.py:503
  1192.2 1046.7 %reduce-scatter.29.cloned.1.call-start = ((), (), s32[]{:S(2)}) async-start(), calls=%async_computation.33 | async-start | bytes 23789568 | tf_op jit(solution)/shard_map/reduce_scatter | solution.py:504
  1203.0 1293.6 %reduce-scatter.17.cloned.1.call-start = ((), (), s32[]{:S(2)}) async-start(), calls=%async_computation.27 | async-start | bytes 25952256 | tf_op jit(solution)/shard_map/reduce_scatter | solution.py:496
  1219.0 1463.7 %reduce-scatter.23.cloned.1.call-start = ((), (), s32[]{:S(2)}) async-start(), calls=%async_computation.30 | async-start | bytes 17301504 | tf_op jit(solution)/shard_map/reduce_scatter | solution.py:500
  1236.6 17.8 slice-start.3
  1273.3 41.2 %copy-start.72 = (f32[128]{0:T(128)S(1)}, f32[128]{0:T(128)}, u32[]{:S(2)}) copy-start(f32[128]{0:T(128)} %copy-done.71) | copy-start | bytes 1540
  (88 other events, 447.8 us)
Sparse Core Ops, SparseCore 0:
  9.6 13.6 all-gather.12
  27.0 93.1 all-gather.14
  121.8 28.8 all-gather.16
  152.7 14.1 all-gather.18
  168.2 21.0 all-gather.20
  190.7 17.1 all-gather.32
  209.4 17.1 all-gather.30
  228.2 17.1 all-gather.28
  246.9 25.1 all-gather.22
  430.8 25.1 all-gather.24
  572.7 25.1 all-gather.26
  972.8 90.2 reduce-scatter.38
  1065.4 76.9 reduce-scatter.36
  1145.3 10.7 reduce-scatter.30
  1158.8 15.0 reduce-scatter.32
  1176.1 15.0 reduce-scatter.34
  1193.9 144.1 reduce-scatter.18
  1340.8 144.6 reduce-scatter.20
  1488.4 242.0 reduce-scatter.24
  1733.2 251.3 reduce-scatter.26
  1987.5 251.3 reduce-scatter.28
  2245.9 250.6 reduce-scatter.16
  2499.6 183.0 reduce-scatter.22
where the time goes:
time: 2700 us; the launch traced here: 2690 us
  waiting for transfers between devices  1670 us (62%)
  matrix products  453 us (17%)
  local copies, waits for them, and re-layouts  202 us (7%)
  blocking collectives  168 us (6%)
  other arithmetic  86.9 us (3%)
  starting transfers between devices  57.6 us (2%)
  loops' own time  33.6 us (1%)
    reduce_scatter x1, waiting for transfers between devices, per_device(): lax.psum_scatter(grad_w_query, ('ctx', 'wt'), scatter_dimension=1, tiled=...  258 us
    reduce_scatter x1, waiting for transfers between devices, per_device(): lax.psum_scatter(grad_w_shared_down, ('ctx', 'wt'), scatter_dimension=1,...  254 us
    reduce_scatter x1, waiting for transfers between devices, per_device(): lax.psum_scatter(grad_w_shared_up, ('ctx', 'wt'), scatter_dimension=0, ti...  254 us
    reduce_scatter x1, waiting for transfers between devices, per_device(): lax.psum_scatter(grad_w_shared_gate, ('ctx', 'wt'), scatter_dimension=0,...  245 us
    reduce_scatter x1, waiting for transfers between devices, per_device(): lax.psum_scatter(grad_w_out, ('ctx', 'wt'), scatter_dimension=1, tiled=True)  186 us
    dot_general x19, matrix products, contract(): lax.dot_general(former, latter, (((former_dim,), (latter_dim,)), ((), ())...  163 us
    reduce_scatter x1, waiting for transfers between devices, per_device(): lax.psum_scatter(grad_w_kv_up, ('ctx', 'wt'), scatter_dimension=1, tiled=...  147 us
    unnamed x25, waiting for transfers between devices  132 us
  transfers between devices with their start and end apart: 27, of which 13 were waited for; matrix products, arithmetic and copies ran while one was open for 19% of the time, Pallas kernels for 0%

commit v1 on v0

v1 whole, which is shorter than its diff:
```python
import functools
import math

import jax
import jax.numpy as jnp
from jax import lax
from jax.sharding import PartitionSpec as P

D = 2048
H = 16
DN = 128
DR = 64
DV = 128
R = 512
TOP = 6
DQ = DN + DR
KW = R + DR

EPS = 1e-06
SCALE = 1.0 / math.sqrt(DN + DR)
MASKED = -1e30
BF = jnp.bfloat16
F32 = jnp.float32


def contract(former, latter, former_dim, latter_dim):
    return lax.dot_general(
        former,
        latter,
        (((former_dim,), (latter_dim,)), ((), ())),
        preferred_element_type=F32,
    )


def wt_from(x, step):
    count = lax.axis_size("wt")
    return lax.ppermute(x, "wt", [((i + step) % count, i) for i in range(count)])


def wt_to(x, step):
    count = lax.axis_size("wt")
    return lax.ppermute(x, "wt", [(i, (i + step) % count) for i in range(count)])


def wt_rows(x):
    return jnp.concatenate(
        [x] + [wt_from(x, step) for step in range(1, lax.axis_size("wt"))], axis=0
    )


def in_order(parts, axis):
    count = len(parts)
    w = lax.axis_index("wt")
    if count == 2:
        return jnp.where(
            w == 0, jnp.concatenate(parts, axis), jnp.concatenate(parts[::-1], axis)
        )
    size = parts[0].shape[axis]
    return lax.dynamic_slice_in_dim(
        jnp.concatenate(parts + parts, axis), (count - w) % count * size, count * size, axis
    )


def wt_gather(x, axis):
    return in_order([x] + [wt_from(x, step) for step in range(1, lax.axis_size("wt"))], axis)


def part_of(x, index, axis):
    count = lax.axis_size("wt")
    size = x.shape[axis] // count
    if count == 2:
        return jnp.where(
            index == 0,
            lax.slice_in_dim(x, 0, size, axis=axis),
            lax.slice_in_dim(x, size, 2 * size, axis=axis),
        )
    return lax.dynamic_slice_in_dim(x, index * size, size, axis)


def my_part(x, axis):
    return part_of(x, lax.axis_index("wt"), axis)


def wt_sum_rows(x):
    count = lax.axis_size("wt")
    rows = x.shape[0] // count
    total = x[:rows]
    for step in range(1, count):
        total = total + wt_to(x[step * rows : (step + 1) * rows], step)
    return total


def wt_sum_part(x, axis):
    count = lax.axis_size("wt")
    w = lax.axis_index("wt")
    rows = x.shape[0] // count
    total = my_part(x, axis)
    for step in range(1, count):
        other = wt_to(part_of(x, (w + step) % count, axis), step)
        other = jnp.concatenate([other[step * rows :], other[: step * rows]], axis=0)
        total = total + other
    return total


def wt_own_rows(x):
    count = lax.axis_size("wt")
    rows = x.shape[0] // count
    parts = [x[:rows]]
    for step in range(1, count):
        back = count - step
        parts.append(
            lax.ppermute(
                x[back * rows : (back + 1) * rows],
                "wt",
                [((i + step) % count, i) for i in range(count)],
            )
        )
    return in_order(parts, 1)


def wt_all_columns(x):
    count = lax.axis_size("wt")
    rows = x.shape[0] // count
    parts = [x]
    for step in range(1, count):
        other = wt_from(x, step)
        parts.append(jnp.concatenate([other[-step * rows :], other[: -step * rows]], axis=0))
    return in_order(parts, 1)


def ctx_swap(x, mask):
    count = lax.axis_size("ctx")
    return lax.ppermute(x, "ctx", [(i, i ^ mask) for i in range(count)])


def spread_orders():
    bits = []
    bit = lax.axis_size("ctx") // 2
    while bit:
        bits.append(bit)
        bit //= 2
    return bits, bits[:-2] + [bits[-1], bits[-2]]


def masks_of(order):
    masks = [0]
    for bit in order:
        masks = masks + [m ^ bit for m in masks]
    return masks


def ctx_spread(x, order):
    for bit in order:
        x = jnp.concatenate([x, ctx_swap(x, bit)], axis=0)
    return x


def ctx_unspread(x, order):
    for bit in reversed(order):
        half = x.shape[0] // 2
        x = x[:half] + ctx_swap(x[half:].astype(BF), bit).astype(F32)
    return x


def ctx_reduce(x, order, sent=BF):
    c = lax.axis_index("ctx")
    count = x.shape[0]
    tail = x.shape[1:]
    dims = []
    bit = count // 2
    while bit:
        dims.append(bit)
        bit //= 2
    for number, bit in enumerate(order):
        place = dims.index(bit)
        before, after = 2**place, 2 ** (len(dims) - place - 1)
        view = x.reshape((before, 2, after) + tail)
        mine = (c // bit) % 2
        keep = lax.dynamic_index_in_dim(view, mine, 1, keepdims=False)
        send = lax.dynamic_index_in_dim(view, 1 - mine, 1, keepdims=False)
        got = ctx_swap(send, bit)
        total = keep.astype(F32) + got.astype(F32)
        dims.pop(place)
        x = total.reshape((before * after,) + tail)
        if number < len(order) - 1:
            x = x.astype(sent)
    return x.reshape(tail)


def query_parts(q, cos, sin, up_key):
    rows = q.shape[0]
    q = q.reshape(rows, H, DQ)
    nope = q[:, :, :DN].astype(BF)
    first, second = q[:, :, DN : DN + DR // 2], q[:, :, DN + DR // 2 :]
    cos, sin = cos[:, None], sin[:, None]
    latent = jnp.einsum("thd,rhd->htr", nope, up_key, preferred_element_type=F32).astype(BF)
    rotary = jnp.concatenate([first * cos - second * sin, first * sin + second * cos], axis=2)
    return nope, jnp.concatenate([latent, rotary.astype(BF).transpose(1, 0, 2)], axis=2)


def attend(query, keys, seen, up_value):
    scores = jnp.einsum("htr,kr->htk", query, keys, preferred_element_type=F32) * SCALE
    scores = jnp.where(seen, scores, MASKED)
    top = jnp.max(scores, axis=2, keepdims=True)
    probs = jnp.exp(scores - top)
    total = jnp.sum(probs, axis=2, keepdims=True)
    out = jnp.einsum("htk,kr->htr", probs.astype(BF), keys[:, :R], preferred_element_type=F32) / total
    heads = jnp.einsum("htr,rhv->thv", out.astype(BF), up_value, preferred_element_type=F32)
    return out, top + jnp.log(total), heads.reshape(heads.shape[0], H * DV).astype(BF)


def attend_back(query, keys, seen, up_key, up_value, out, log_total, grad_heads, cos, sin):
    rows = query.shape[1]
    scores = jnp.einsum("htr,kr->htk", query, keys, preferred_element_type=F32) * SCALE
    probs = jnp.exp(jnp.where(seen, scores, MASKED) - log_total)
    grad_out = jnp.einsum(
        "thv,rhv->htr", grad_heads.reshape(rows, H, DV), up_value, preferred_element_type=F32
    ).astype(BF)
    delta = jnp.sum(grad_out.astype(F32) * out, axis=2, keepdims=True)
    grad_probs = jnp.einsum("htr,kr->htk", grad_out, keys[:, :R], preferred_element_type=F32)
    grad_scores = (probs * (grad_probs - delta) * SCALE).astype(BF)
    grad_query = jnp.einsum("htk,kr->htr", grad_scores, keys, preferred_element_type=F32)
    grad_keys = jnp.einsum("htk,htr->kr", grad_scores, query, preferred_element_type=F32)
    values_part = jnp.einsum("htk,htr->kr", probs.astype(BF), grad_out, preferred_element_type=F32)
    grad_keys = grad_keys + jnp.pad(values_part, ((0, 0), (0, DR)))
    grad_latent = grad_query[:, :, :R].astype(BF)
    nope = jnp.einsum("htr,rhd->thd", grad_latent, up_key, preferred_element_type=F32)
    first, second = grad_query[:, :, R : R + DR // 2], grad_query[:, :, R + DR // 2 :]
    rotary = jnp.concatenate([first * cos + second * sin, second * cos - first * sin], axis=2)
    grad_q = jnp.concatenate([nope, rotary.transpose(1, 0, 2)], axis=2).reshape(rows, H * DQ)
    return grad_q.astype(BF), grad_latent, grad_keys


def rms_norm(values, gain):
    scale = lax.rsqrt(jnp.mean(values * values, axis=1, keepdims=True) + EPS)
    return values * scale * gain


def rms_back(values, gain, grad):
    scale = lax.rsqrt(jnp.mean(values * values, axis=1, keepdims=True) + EPS)
    scaled = grad * gain
    inner = jnp.mean(values * scaled, axis=1, keepdims=True)
    return scale * scaled - values * (scale * scale * scale * inner), jnp.sum(grad * values * scale, axis=0)


def silu_parts(v):
    sig = jax.nn.sigmoid(v)
    return v * sig, sig * (1.0 + v * (1.0 - sig))


def token_places(block_deal, lengths_row, first_block, rows, block):
    blocks = lax.dynamic_slice_in_dim(block_deal, first_block, 2, 0)
    place = (blocks[:, None] * block + jnp.arange(block, dtype=jnp.int32)[None, :]).reshape(rows)
    ends = jnp.cumsum(lengths_row)
    past = place[:, None] >= ends[None, :]
    start = jnp.sum(jnp.where(past, lengths_row[None, :], 0), axis=1)
    return place, start


def route_matrices(routes, gates, capacity):
    count = lax.axis_size("ctx")
    rows = routes.shape[0]
    experts = lax.axis_index("ctx") ^ jnp.arange(count // 2, dtype=jnp.int32)
    named = routes[:, :, None] == experts[None, None, :]
    chosen = jnp.any(named, axis=1)
    weight = jnp.sum(jnp.where(named, gates[:, :, None], 0.0), axis=1).T
    earlier = (jnp.arange(rows)[:, None] > jnp.arange(rows)[None, :]).astype(BF)
    rank = contract(chosen.astype(BF), earlier, 0, 1).astype(jnp.int32)
    slots = jnp.arange(capacity, dtype=jnp.int32)
    held = (rank[:, None, :] == slots[None, :, None]) & chosen.T[:, None, :]
    place = held.astype(BF).reshape(-1, rows)
    weighted = jnp.where(held, weight[:, None, :], 0.0).reshape(-1, rows)
    high = weighted.astype(BF)
    low = (weighted - high.astype(F32)).astype(BF)
    return place, high, low


def per_device(
    tokens,
    gain_attn,
    w_query,
    w_kv_down,
    gain_kv,
    w_kv_up,
    w_out,
    gain_mlp,
    w_shared_gate,
    w_shared_up,
    w_shared_down,
    w_expert_gate,
    w_expert_up,
    w_expert_down,
    block_deal,
    lengths,
    routes,
    gate_weights,
    cotangent,
):
    n_ctx = lax.axis_size("ctx")
    n_wt = lax.axis_size("wt")
    c = lax.axis_index("ctx")
    rows = tokens.shape[1]
    block = rows // 2
    half_ctx = n_ctx // 2
    capacity = min(rows, 4 * rows * TOP // (3 * n_ctx))
    order_a, order_b = spread_orders()
    reduce_a, reduce_b = order_a[::-1], order_b[::-1]

    tok = tokens[0]
    cot = cotangent[0]
    tok_all = wt_rows(tok)
    cot_all = wt_rows(cot)
    kv_down = wt_gather(w_kv_down, 0)
    kv_up = wt_gather(w_kv_up, 0)
    gains = jnp.stack(
        [gain_attn, gain_mlp, jnp.pad(gain_kv, (0, gain_attn.shape[0] - gain_kv.shape[0]))]
    ).astype(F32)
    gains = wt_gather(gains[None], 0)
    gain_one = gains[:, 0].reshape(1, D).astype(F32)
    gain_two = gains[:, 1].reshape(1, D).astype(F32)
    gain_latent = gains[:, 2, : gain_kv.shape[0]].reshape(1, R).astype(F32)

    place, start = token_places(block_deal, lengths[0], 2 * c, rows, block)
    position = place - start
    frequency = jnp.exp(
        jnp.arange(DR // 2, dtype=F32) * (-2.0 * math.log(10000.0) / DR)
    )
    angles = position.astype(F32)[:, None] * frequency[None, :]
    cos, sin = jnp.cos(angles), jnp.sin(angles)
    lo, hi = start[:, None], place[:, None]
    blocks = jnp.stack(
        [
            jnp.take(block_deal, 2 * (c ^ jnp.array(masks_of(order), jnp.int32)) + side)
            for side, order in ((0, order_a), (1, order_b))
        ]
    )

    inputs_all = tok_all.astype(F32)
    inputs = inputs_all[:rows]
    normed_one = rms_norm(inputs_all, gain_one).astype(BF)
    kv = contract(normed_one[:rows], kv_down, 1, 0)
    latent_raw = kv[:, :R]
    latent = rms_norm(latent_raw, gain_latent).astype(BF)
    first, second = kv[:, R : R + DR // 2], kv[:, R + DR // 2 :]
    own_keys = jnp.concatenate(
        [latent, (first * cos - second * sin).astype(BF), (first * sin + second * cos).astype(BF)],
        axis=1,
    )
    keys_a = ctx_spread(own_keys[:block], order_a)
    keys_b = ctx_spread(own_keys[block:], order_b)
    query = wt_sum_rows(contract(my_part(normed_one, 1), w_query, 1, 0))
    up3 = kv_up.reshape(R, H, DN + DV)
    up_key, up_value = up3[:, :, :DN], up3[:, :, DN:]
    query_nope, query_cat = query_parts(query, cos, sin, up_key)

    partner = functools.partial(ctx_swap, mask=half_ctx)
    route_own = routes[0]
    gate_own = gate_weights[0]
    place_own, high_own, low_own = route_matrices(route_own, gate_own, capacity)
    place_other, high_other, low_other = route_matrices(
        partner(route_own.astype(F32)).astype(jnp.int32), partner(gate_own), capacity
    )
    def swap_blocks(x):
        return jnp.concatenate([x[:1]] + [ctx_swap(x[j : j + 1], j) for j in range(1, half_ctx)], axis=0)

    def to_experts(own, other):
        both = jnp.concatenate(
            [own.reshape(half_ctx, capacity, D), other.reshape(half_ctx, capacity, D)], axis=1
        )
        return swap_blocks(both).reshape(-1, D)

    def from_experts(x):
        x = swap_blocks(x.reshape(half_ctx, 2 * capacity, D))
        return x[:, :capacity].reshape(-1, D), x[:, capacity:].reshape(-1, D)

    cot_other = partner(cot)
    rows_grad = to_experts(
        (contract(high_own, cot, 1, 0) + contract(low_own, cot, 1, 0)).astype(BF),
        (contract(high_other, cot_other, 1, 0) + contract(low_other, cot_other, 1, 0)).astype(BF),
    )

    keys = jnp.concatenate([keys_a, keys_b], axis=0)
    key_place = (blocks[:, :, None] * block + jnp.arange(block, dtype=jnp.int32)).reshape(1, -1)
    seen = (key_place >= lo) & (key_place <= hi)
    out_latent, log_total, heads_out = attend(query_cat, keys, seen, up_value)
    heads_all = wt_rows(heads_out)
    residual = inputs + wt_sum_rows(contract(my_part(heads_all, 1), w_out, 1, 0))
    normed_two = rms_norm(residual, gain_two).astype(BF)

    normed_other = partner(normed_two)
    rows_in = to_experts(
        contract(place_own, normed_two, 1, 0).astype(BF),
        contract(place_other, normed_other, 1, 0).astype(BF),
    )

    two_all = wt_rows(normed_two)
    two_part = my_part(two_all, 1)
    shared_gate = wt_sum_part(contract(two_part, w_shared_gate, 1, 0), 1)
    shared_up = wt_sum_part(contract(two_part, w_shared_up, 1, 0), 1)
    act, slope = silu_parts(shared_gate)
    hidden = (act * shared_up).astype(BF)
    shared_out = wt_sum_rows(contract(hidden, w_shared_down, 1, 0))
    grad_hidden = contract(cot_all, w_shared_down, 1, 1)
    grad_gate = wt_all_columns((grad_hidden * shared_up * slope).astype(BF))
    grad_up = wt_all_columns((grad_hidden * act).astype(BF))
    hidden_all = wt_all_columns(hidden)
    shared_back = wt_own_rows(
        contract(grad_gate, w_shared_gate, 1, 1) + contract(grad_up, w_shared_up, 1, 1)
    )

    def chosen_columns(x):
        wide = x.shape[1] // (n_ctx * n_wt)
        view = x.reshape(x.shape[0], n_ctx, n_wt, wide)
        return my_part(view, 2).reshape(x.shape[0], n_ctx * wide)

    def weight_grad(chunked, other, order):
        grad = contract(chosen_columns(chunked), other, 0, 0).astype(BF)
        return ctx_reduce(grad.reshape(n_ctx, -1, other.shape[1]), order)

    grad_w_shared_gate = weight_grad(two_all, grad_gate, reduce_a)
    grad_w_shared_up = weight_grad(two_all, grad_up, reduce_b)
    grad_w_shared_down = weight_grad(cot_all, hidden_all, reduce_b).T

    gate_matrix = lax.all_gather(w_expert_gate[0], "wt", axis=0, tiled=True)
    up_matrix = lax.all_gather(w_expert_up[0], "wt", axis=0, tiled=True)
    down_matrix = lax.all_gather(w_expert_down[0], "wt", axis=0, tiled=True)
    expert_gate = contract(rows_in, gate_matrix, 1, 0)
    expert_up = contract(rows_in, up_matrix, 1, 0)
    expert_act, expert_slope = silu_parts(expert_gate)
    expert_hidden = (expert_act * expert_up).astype(BF)
    grad_expert_hidden = contract(rows_grad, down_matrix, 1, 1)
    grad_expert_gate = (grad_expert_hidden * expert_up * expert_slope).astype(BF)
    grad_expert_up = (grad_expert_hidden * expert_act).astype(BF)
    grad_rows = (
        contract(grad_expert_gate, gate_matrix, 1, 1) + contract(grad_expert_up, up_matrix, 1, 1)
    ).astype(BF)
    back_own, back_other = from_experts(grad_rows)
    grad_routed = contract(place_own, back_own, 0, 0) + partner(
        contract(place_other, back_other, 0, 0).astype(BF)
    ).astype(F32)
    produced = contract(expert_hidden, down_matrix, 1, 0).astype(BF)
    out_own, out_other = from_experts(produced)
    routed = (
        contract(high_own, out_own, 0, 0)
        + contract(low_own, out_own, 0, 0)
        + partner(
            (contract(high_other, out_other, 0, 0) + contract(low_other, out_other, 0, 0)).astype(BF)
        ).astype(F32)
    )
    mixed_out = (residual + shared_out + routed).astype(BF)

    def expert_sum(grad):
        total = my_part(grad, 0)
        for step in range(1, n_wt):
            w = lax.axis_index("wt")
            total = total + wt_to(part_of(grad, (w + step) % n_wt, 0).astype(BF), step).astype(F32)
        return total[None]

    grad_w_expert_gate = expert_sum(contract(rows_in, grad_expert_gate, 0, 0))
    grad_w_expert_up = expert_sum(contract(rows_in, grad_expert_up, 0, 0))
    grad_w_expert_down = expert_sum(contract(expert_hidden, rows_grad, 0, 0))

    grad_two = shared_back + grad_routed
    grad_part, grad_gain_mlp = rms_back(residual, gain_two, grad_two)
    grad_residual = cot.astype(F32) + grad_part
    grad_attn = wt_rows(grad_residual.astype(BF))
    grad_heads = wt_own_rows(contract(grad_attn, w_out, 1, 1).astype(BF))
    grad_w_out = weight_grad(grad_attn, heads_all, reduce_a).T

    grad_query, grad_query_latent, grad_keys = attend_back(
        query_cat, keys, seen, up_key, up_value, out_latent, log_total, grad_heads, cos, sin
    )
    grad_keys_a, grad_keys_b = jnp.split(grad_keys, 2, axis=0)
    grad_keys = jnp.concatenate(
        [ctx_unspread(grad_keys_a, order_a), ctx_unspread(grad_keys_b, order_b)], axis=0
    )
    grad_up_key = jnp.einsum(
        "thd,htr->hdr", query_nope, grad_query_latent, preferred_element_type=F32
    )
    grad_up_value = jnp.einsum(
        "thv,htr->hvr", grad_heads.reshape(rows, H, DV), out_latent.astype(BF), preferred_element_type=F32
    )
    up_grads = jnp.concatenate([grad_up_key, grad_up_value], axis=1).astype(BF)
    up_grads = up_grads.reshape(n_ctx, n_wt, -1, R)
    own_up = my_part(up_grads, 1).astype(F32)
    for step in range(1, n_wt):
        w = lax.axis_index("wt")
        own_up = own_up + wt_to(part_of(up_grads, (w + step) % n_wt, 1), step).astype(F32)
    grad_w_kv_up = ctx_reduce(own_up.astype(BF).reshape(n_ctx, -1, R), reduce_b).T

    query_all = wt_rows(grad_query)
    query_columns = chosen_columns(query_all)
    grad_w_query = jnp.concatenate(
        [
            ctx_reduce(
                contract(query_columns, normed_one[:, part * (D // 2) : (part + 1) * (D // 2)], 0, 0)
                .astype(BF)
                .reshape(n_ctx, -1, D // 2),
                order,
            ).T
            for part, order in ((0, reduce_a), (1, reduce_b))
        ],
        axis=0,
    )
    one_part = contract(query_all, w_query, 1, 1)

    grad_latent, grad_gain_kv = rms_back(latent_raw, gain_latent, grad_keys[:, :R])
    first, second = grad_keys[:, R : R + DR // 2], grad_keys[:, R + DR // 2 :]
    grad_kv = jnp.concatenate(
        [grad_latent, first * cos + second * sin, second * cos - first * sin], axis=1
    ).astype(BF)
    grad_kv_all = wt_rows(grad_kv)
    grad_w_kv_down = weight_grad(normed_one, grad_kv_all, reduce_a)
    grad_one = wt_own_rows(one_part + contract(grad_kv_all, w_kv_down, 1, 1))
    grad_inputs, grad_gain_attn = rms_back(inputs, gain_one, grad_one)
    grad_tokens = grad_residual + grad_inputs

    gain_grads = jnp.concatenate(
        [
            g.reshape(n_ctx, n_wt, -1)
            for g in (grad_gain_attn, grad_gain_mlp, grad_gain_kv)
        ],
        axis=2,
    )
    own_gain = my_part(gain_grads, 1)
    for step in range(1, n_wt):
        w = lax.axis_index("wt")
        own_gain = own_gain + wt_to(part_of(gain_grads, (w + step) % n_wt, 1), step)
    gain_total = ctx_reduce(own_gain.reshape(n_ctx, 1, -1), reduce_b, F32)[0]
    wide = D // (n_ctx * n_wt)

    return (
        mixed_out[None],
        grad_tokens[None],
        gain_total[:wide],
        grad_w_query,
        grad_w_kv_down,
        gain_total[2 * wide :],
        grad_w_kv_up,
        grad_w_out,
        gain_total[wide : 2 * wide],
        grad_w_shared_gate,
        grad_w_shared_up,
        grad_w_shared_down,
        grad_w_expert_gate,
        grad_w_expert_up,
        grad_w_expert_down,
    )


def solution(mesh):
    placed = (
        P("wt", "ctx", None),
        P("wt"),
        P("wt", None),
        P("wt", None),
        P("wt"),
        P("wt", None),
        P("wt", None),
        P("wt"),
        P("wt", None),
        P("wt", None),
        P("wt", None),
        P("ctx", "wt", None),
        P("ctx", "wt", None),
        P("ctx", "wt", None),
        P(),
        P("wt", None),
        P("wt", "ctx", None),
        P("wt", "ctx", None),
        P("wt", "ctx", None),
    )
    return jax.shard_map(
        per_device,
        mesh=mesh,
        in_specs=placed,
        out_specs=(
            P("wt", "ctx", None),
            P("wt", "ctx", None),
            P(("ctx", "wt")),
            P(None, ("ctx", "wt")),
            P(("ctx", "wt"), None),
            P(("ctx", "wt")),
            P(None, ("ctx", "wt")),
            P(None, ("ctx", "wt")),
            P(("ctx", "wt")),
            P(("ctx", "wt"), None),
            P(("ctx", "wt"), None),
            P(None, ("ctx", "wt")),
            P("ctx", "wt", None),
            P("ctx", "wt", None),
            P("ctx", "wt", None),
        ),
        check_vma=False,
    )
```

time: 2700 us -> 1090 us (0.40)
  waiting for transfers between devices: 1670 us -> 469 us
  matrix products: 453 us -> 252 us
  blocking collectives: 168 us -> 0 us
  local copies, waits for them, and re-layouts: 202 us -> 115 us
  starting transfers between devices: 57.6 us -> 99.5 us
  other arithmetic: 86.9 us -> 127 us
  loops' own time: 33.6 us -> 0 us
    reduce_scatter x10 -> x0, waiting for transfers between devices: 1370 us -> none  [the longest x1 258 us: per_device(): lax.psum_scatter(grad_w_query, ('ctx', 'wt'), scatter_dimension=1, tiled=...]
    ppermute x0 -> x112, waiting for transfers between devices: none -> 468 us  [the longest x86 466 us: ctx_swap(): return lax.ppermute(x, 'ctx', [(i, i ^ mask) for i in range(count)])]
    dot_general x110 -> x12, matrix products: 290 us -> 67.4 us  [the longest x1 13.6 us: attend_back(): jnp.einsum('htr,kr->htk', grad_out, keys[:, :R], preferred_element_type=F32)]
    all_to_all x4 -> x0, waiting for transfers between devices: 165 us -> none  [the longest x1 66.3 us: per_device(): lax.all_to_all(grad_rows, 'ctx', split_axis=0, concat_axis=0, tiled=True)]
    unnamed x25 -> x3, waiting for transfers between devices: 132 us -> 1.39 us
    all_gather x4 -> x0, blocking collectives: 130 us -> none  [the longest x1 125 us: per_device(): lax.all_gather(key_rope_cols, 'ctx', axis=1, tiled=True)]
    ppermute x0 -> x112, starting transfers between devices: none -> 99.4 us  [the longest x86 95.5 us: ctx_swap(): return lax.ppermute(x, 'ctx', [(i, i ^ mask) for i in range(count)])]
    all_to_all x4 -> x0, starting transfers between devices: 56.6 us -> none  [the longest x1 19.1 us: per_device(): lax.all_to_all(grad_rows, 'ctx', split_axis=0, concat_axis=0, tiled=True)]
  transfers between devices with their start and end apart: 27 -> 115, of which waited for: 13 -> 49; matrix products, arithmetic and copies ran while one was open for 19% -> 44% of each run, Pallas kernels for 0% -> 0%
where the time goes in v1:
time: 1090 us; the launch traced here: 1080 us
  waiting for transfers between devices  469 us (43%)
  matrix products  252 us (23%)
  other arithmetic  127 us (12%)
  local copies, waits for them, and re-layouts  115 us (11%)
  starting transfers between devices  99.5 us (9%)
  between operations  17.4 us (2%)
    ppermute x86, waiting for transfers between devices, ctx_swap(): return lax.ppermute(x, 'ctx', [(i, i ^ mask) for i in range(count)])  466 us
    dot_general x42, matrix products, contract(): lax.dot_general(former, latter, (((former_dim,), (latter_dim,)), ((), ())...  185 us
    ppermute x86, starting transfers between devices, ctx_swap(): return lax.ppermute(x, 'ctx', [(i, i ^ mask) for i in range(count)])  95.5 us
    unnamed x341, local copies, waits for them, and re-layouts  50 us
    convert_element_type x24, other arithmetic, ctx_reduce(): x = x.astype(sent)  23.5 us
    broadcast_in_dim x3, other arithmetic, expert_sum(): return total[None]  23.1 us
  transfers between devices with their start and end apart: 115, of which 49 were waited for; matrix products, arithmetic and copies ran while one was open for 44% of the time, Pallas kernels for 0%

profile of v1, /device:TPU:0, one launch (start us, length us, event | category | flops | bytes accessed | tf_op | source)
XLA Modules:
  0.0 1080.0 jit_solution(17963764836140985452)
XLA Ops:
  29.5 6.8 collective-permute-done.19
  69.9 7.4 collective-permute-done.5
  140.2 10.6 fusion.3
  150.8 7.0 fusion.6
  184.1 11.5 %collective-permute-done.47 = bf16[1,128,2048]{2,1,0:T(8,128)(2,1)S(1)} collective-permute-done((bf16[1,128,2048]{2,1,0:T(8,128)(2,1)}, bf16[1,128,2048]{2,1,0:T(8,128)(2,1)S(1)}, u32[]{:S(2)}, u32[]{:S(2)}) %collective-permute-start.47) | collective-permute-done | bytes 524320 | tf_op jit(solution)/shard_map/ppermute | solution.py:133
  196.4 9.9 collective-permute-done.48
  210.4 23.0 %collective-permute-done.20 = bf16[128,2048]{1,0:T(8,128)(2,1)S(1)} collective-permute-done((bf16[128,2048]{1,0:T(8,128)(2,1)S(1)}, bf16[128,2048]{1,0:T(8,128)(2,1)S(1)}, u32[]{:S(2)}, u32[]{:S(2)}) %collective-permute-start.20) | collective-permute-done | bytes 524320 | tf_op jit(solution)/shard_map/ppermute | solution.py:133
  260.1 19.2 %collective-permute-done.23 = bf16[1,128,2048]{2,1,0:T(8,128)(2,1)} collective-permute-done((bf16[1,128,2048]{2,1,0:T(8,128)(2,1)}, bf16[1,128,2048]{2,1,0:T(8,128)(2,1)}, u32[]{:S(2)}, u32[]{:S(2)}) %collective-permute-start.23) | collective-permute-done | bytes 524320 | tf_op jit(solution)/shard_map/ppermute | solution.py:133
  286.5 8.0 collective-permute-done.27
  295.3 11.8 %fusion.19 = f32[1024,1408]{1,0:T(8,128)} fusion(bf16[1024,2048]{1,0:T(8,128)(2,1)} %bitcast.572, bf16[1,1408,2048]{2,1,0:T(8,128)(2,1)} %all-gather.11.cloned.1.call-done), kind=kOutput, calls=%fused_computation.55 | convolution fusion | flops 5905580032 | bytes 15728640 | tf_op jit(solution)/shard_map/dot_general | solution.py:27
  307.0 11.7 %fusion.25 = f32[1024,1408]{1,0:T(8,128)} fusion(bf16[1024,2048]{1,0:T(8,128)(2,1)} %bitcast.574, bf16[1,2048,1408]{2,1,0:T(8,128)(2,1)} %all-gather.9.cloned.1.call-done), kind=kOutput, calls=%fused_computation.61 | convolution fusion | flops 5905580032 | bytes 15728640 | tf_op jit(solution)/shard_map/dot_general | solution.py:27
  318.7 16.6 %multiply_convert_fusion.2 = (bf16[1024,1408]{1,0:T(8,128)(2,1)}, bf16[1024,1408]{1,0:T(8,128)(2,1)}, bf16[1024,1408]{1,0:T(8,128)(2,1)S(1)}) fusion(f32[1024,1408]{1,0:T(8,128)} %fusion.19, f32[1024,1408]{1,0:T(8,128)} %fusion.25, bf16[1024,2048]{1,0:T(8,128)(2,1)} %bitcast.575, bf16[1,2048,1408]{2,1,0:T(8,128)(2,1)} %all-gather.7.cloned.1.call-done), kind=kOutput, calls=%fused_computation.74 | convolution fusion | flops 5927206912 | bytes 30146560 | tf_op jit(solution)/shard_map/dot_general | solution.py:27
  335.4 6.3 fusion.268
  341.6 10.9 %fusion.33 = bf16[1024,2048]{1,0:T(8,128)(2,1)S(1)} fusion(bf16[1024,1408]{1,0:T(8,128)(2,1)S(1)} %get-tuple-element.96, bf16[1,1408,2048]{2,1,0:T(8,128)(2,1)} %all-gather.11.cloned.1.call-done), kind=kOutput, calls=%fused_computation.93 | convolution fusion | flops 5907677184 | bytes 12845056 | tf_op jit(solution)/shard_map/dot_general | solution.py:27
  357.0 9.8 fusion.266
  366.8 9.6 fusion.267
  376.4 8.9 fusion.23
  385.3 11.2 %add_convert_fusion = bf16[1024,2048]{1,0:T(8,128)(2,1)S(1)} fusion(f32[1024,2048]{1,0:T(8,128)} %fusion.23, bf16[1024,1408]{1,0:T(8,128)(2,1)} %get-tuple-element.94, bf16[1,2048,1408]{2,1,0:T(8,128)(2,1)} %all-gather.7.cloned.1.call-done), kind=kOutput, calls=%fused_computation.13 | convolution fusion | flops 5909774336 | bytes 21233664 | tf_op jit(solution)/shard_map/dot_general | solution.py:27
  398.5 6.4 select_convert_fusion.2
  411.4 6.6 select_convert_fusion.1
  448.1 9.1 collective-permute-done.33
  457.4 11.1 %collective-permute-done.34 = bf16[1,128,2048]{2,1,0:T(8,128)(2,1)S(1)} collective-permute-done((bf16[1,128,2048]{2,1,0:T(8,128)(2,1)S(1)}, bf16[1,128,2048]{2,1,0:T(8,128)(2,1)S(1)}, u32[]{:S(2)}, u32[]{:S(2)}) %collective-permute-start.34) | collective-permute-done | bytes 524320 | tf_op jit(solution)/shard_map/ppermute | solution.py:133
  471.2 14.3 %collective-permute-done.50 = bf16[1,128,2048]{2,1,0:T(8,128)(2,1)S(1)} collective-permute-done((bf16[1,128,2048]{2,1,0:T(8,128)(2,1)S(1)}, bf16[1,128,2048]{2,1,0:T(8,128)(2,1)S(1)}, u32[]{:S(2)}, u32[]{:S(2)}) %collective-permute-start.50) | collective-permute-done | bytes 524320 | tf_op jit(solution)/shard_map/ppermute | solution.py:133
  490.1 12.0 %collective-permute-done.54 = bf16[1,128,2048]{2,1,0:T(8,128)(2,1)S(1)} collective-permute-done((bf16[1,128,2048]{2,1,0:T(8,128)(2,1)S(1)}, bf16[1,128,2048]{2,1,0:T(8,128)(2,1)S(1)}, u32[]{:S(2)}, u32[]{:S(2)}) %collective-permute-start.54) | collective-permute-done | bytes 524320 | tf_op jit(solution)/shard_map/ppermute | solution.py:133
  502.2 7.5 collective-permute-done.55
  513.9 6.6 convolution_convert_fusion.1
  523.3 6.5 convolution_convert_fusion.2
  529.8 6.5 convolution_add_fusion.1
  539.5 6.7 convolution_convert_fusion
  560.0 15.3 %collective-permute-done.36 = bf16[128,2048]{1,0:T(8,128)(2,1)S(1)} collective-permute-done((bf16[128,2048]{1,0:T(8,128)(2,1)}, bf16[128,2048]{1,0:T(8,128)(2,1)S(1)}, u32[]{:S(2)}, u32[]{:S(2)}) %collective-permute-start.36) | collective-permute-done | bytes 524320 | tf_op jit(solution)/shard_map/ppermute | solution.py:133
  597.3 10.0 fusion.36
  607.3 13.6 %multiply_convert_fusion = bf16[16,128,2048]{2,1,0:T(8,128)(2,1)} fusion(f32[16,128,2048]{2,1,0:T(8,128)} %copy-done.10, f32[16,128]{1,0:T(8,128)S(1)} %get-tuple-element.183, f32[16,128]{1,0:T(8,128)S(1)} %copy-done.109, pred[128,2048]{1,0:T(8,128)(4,1)S(1)} %copy-done.59, bf16[16,128,512]{2,1,0:T(8,128)(2,1)} %copy-done.136, ...), kind=kOutput, calls=%fused_computation.2 | convolution fusion | flops 4324327424 | bytes 29638656 | tf_op jit(solution)/shard_map/htr,kr->htk/dot_general | solution.py:220
  621.0 7.6 fusion.56
  631.7 7.7 fusion.261
  644.8 10.7 collective-permute-done.60
  667.6 8.6 add_bitcast_fusion.2
  677.1 8.4 add_bitcast_fusion.1
  685.5 41.4 %collective-permute-done.65 = bf16[256,576]{0,1:T(8,128)(2,1)S(1)} collective-permute-done((bf16[256,576]{0,1:T(8,128)(2,1)S(1)}, bf16[256,576]{0,1:T(8,128)(2,1)S(1)}, u32[]{:S(2)}, u32[]{:S(2)}) %collective-permute-start.65) | collective-permute-done | bytes 294944 | tf_op jit(solution)/shard_map/ppermute | solution.py:133
  739.5 9.0 collective-permute-done.67
  781.1 11.5 %collective-permute-done.105 = bf16[4,2,64,2816]{3,2,0,1:T(8,128)(2,1)} collective-permute-done((bf16[4,2,64,2816]{3,2,0,1:T(8,128)(2,1)}, bf16[4,2,64,2816]{3,2,0,1:T(8,128)(2,1)}, u32[]{:S(2)}, u32[]{:S(2)}) %collective-permute-start.105) | collective-permute-done | bytes 2883616 | tf_op jit(solution)/shard_map/ppermute | solution.py:133
  806.5 17.8 %collective-permute-done.71 = f32[4,2,1,144]{3,2,1,0:T(1,128)S(1)} collective-permute-done((f32[4,2,1,144]{3,2,1,0:T(1,128)S(1)}, f32[4,2,1,144]{3,2,1,0:T(1,128)S(1)}, u32[]{:S(2)}, u32[]{:S(2)}) %collective-permute-start.71) | collective-permute-done | bytes 4640 | tf_op jit(solution)/shard_map/ppermute | solution.py:133
  840.8 8.7 collective-permute-done.83
  854.5 27.6 %collective-permute-done.84 = bf16[4,1,64,576]{3,2,0,1:T(8,128)(2,1)S(1)} collective-permute-done((bf16[4,1,64,576]{3,2,0,1:T(8,128)(2,1)S(1)}, bf16[4,1,64,576]{3,2,0,1:T(8,128)(2,1)S(1)}, u32[]{:S(2)}, u32[]{:S(2)}) %collective-permute-start.84) | collective-permute-done | bytes 294944 | tf_op jit(solution)/shard_map/ppermute | solution.py:133
  901.9 14.9 %collective-permute-done.93 = bf16[4,1,64,2048]{3,2,0,1:T(8,128)(2,1)S(1)} collective-permute-done((bf16[4,1,64,2048]{3,2,0,1:T(8,128)(2,1)S(1)}, bf16[4,1,64,2048]{3,2,0,1:T(8,128)(2,1)S(1)}, u32[]{:S(2)}, u32[]{:S(2)}) %collective-permute-start.93) | collective-permute-done | bytes 1048608 | tf_op jit(solution)/shard_map/ppermute | solution.py:133
  921.3 26.1 %collective-permute-done.106 = bf16[4,1,64,2816]{3,2,0,1:T(8,128)(2,1)S(1)} collective-permute-done((bf16[4,1,64,2816]{3,2,0,1:T(8,128)(2,1)S(1)}, bf16[4,1,64,2816]{3,2,0,1:T(8,128)(2,1)S(1)}, u32[]{:S(2)}, u32[]{:S(2)}) %collective-permute-start.106) | collective-permute-done | bytes 1441824 | tf_op jit(solution)/shard_map/ppermute | solution.py:133
  959.8 53.3 %collective-permute-done.81 = bf16[2,1,96,1024]{3,2,1,0:T(8,128)(2,1)S(1)} collective-permute-done((bf16[2,1,96,1024]{3,2,1,0:T(8,128)(2,1)S(1)}, bf16[2,1,96,1024]{3,2,1,0:T(8,128)(2,1)S(1)}, u32[]{:S(2)}, u32[]{:S(2)}) %collective-permute-start.81) | collective-permute-done | bytes 393248 | tf_op jit(solution)/shard_map/ppermute | solution.py:133
  1022.6 10.4 collective-permute-done.95
  1045.8 20.6 %collective-permute-done.91 = bf16[1,1,128,512]{3,2,0,1:T(8,128)(2,1)S(1)} collective-permute-done((bf16[1,1,128,512]{3,2,0,1:T(8,128)(2,1)S(1)}, bf16[1,1,128,512]{3,2,0,1:T(8,128)(2,1)S(1)}, u32[]{:S(2)}, u32[]{:S(2)}) %collective-permute-start.91) | collective-permute-done | bytes 131104 | tf_op jit(solution)/shard_map/ppermute | solution.py:133
  (818 shorter events, 445.6 us)
Async XLA Ops:
  7.2 288.1 %all-gather.11.cloned.1.call-start = ((), (), s32[]{:S(2)}) async-start(), calls=%async_computation.2 | async-start | bytes 8650752 | tf_op jit(solution)/shard_map/all_gather | solution.py:426
  7.9 299.1 %all-gather.9.cloned.1.call-start = ((), (), s32[]{:S(2)}) async-start(), calls=%async_computation.1 | async-start | bytes 8650752 | tf_op jit(solution)/shard_map/all_gather | solution.py:425
  8.7 310.0 %all-gather.7.cloned.1.call-start = ((), (), s32[]{:S(2)}) async-start(), calls=%async_computation | async-start | bytes 8650752 | tf_op jit(solution)/shard_map/all_gather | solution.py:424
  8.8 43.9 %collective-permute-start.41 = (bf16[128,2048]{1,0:T(8,128)(2,1)S(1)}, bf16[128,2048]{1,0:T(8,128)(2,1)}, u32[]{:S(2)}, u32[]{:S(2)}) collective-permute-start(bf16[128,2048]{1,0:T(8,128)(2,1)S(1)} %bitcast.485), channel_id=1, source_target_pairs={{0,16},{2,18},{4,20},{6,22},{8,24},{10,26},{12,28},{14,30},{16,0},... | collective-permute-start | bytes 1572872 | tf_op jit(solution)/shard_map/ppermute | solution.py:133
  12.9 71.5 %collective-permute-start.37 = (bf16[128,2048]{1,0:T(8,128)(2,1)S(1)}, bf16[128,2048]{1,0:T(8,128)(2,1)}, u32[]{:S(2)}, u32[]{:S(2)}) collective-permute-start(bf16[128,2048]{1,0:T(8,128)(2,1)S(1)} %bitcast.486), channel_id=1, source_target_pairs={{1,0},{0,1},{3,2},{2,3},{5,4},{4,5},{7,6},{6,7},{9,8},{8,9},{11,10... | collective-permute-start | bytes 1572872 | tf_op jit(solution)/shard_map/ppermute | solution.py:37
  20.1 87.5 %collective-permute-start.1 = (bf16[256,4096]{0,1:T(8,128)(2,1)}, bf16[256,4096]{0,1:T(8,128)(2,1)}, u32[]{:S(2)}, u32[]{:S(2)}) collective-permute-start(bf16[256,4096]{0,1:T(8,128)(2,1)} %copy.218), channel_id=1, source_target_pairs={{1,0},{0,1},{3,2},{2,3},{5,4},{4,5},{7,6},{6,7},{9,8},{8,9},{11,10... | collective-permute-start | bytes 6291464 | tf_op jit(solution)/shard_map/ppermute | solution.py:37
  51.8 60.0 %collective-permute-start.3 = (f32[128,3072]{1,0:T(8,128)}, f32[128,3072]{1,0:T(8,128)}, u32[]{:S(2)}, u32[]{:S(2)}) collective-permute-start(f32[128,3072]{1,0:T(8,128)} %slice.635), channel_id=1, source_target_pairs={{0,1},{1,0},{2,3},{3,2},{4,5},{5,4},{6,7},{7,6},{8,9},{9,8},{10,11... | collective-permute-start | bytes 4718600 | tf_op jit(solution)/shard_map/ppermute | solution.py:42
  84.3 83.1 %collective-permute-start.42 = (bf16[1,128,2048]{2,1,0:T(8,128)(2,1)}, bf16[1,128,2048]{2,1,0:T(8,128)(2,1)}, u32[]{:S(2)}, u32[]{:S(2)}) collective-permute-start(bf16[1,128,2048]{2,1,0:T(8,128)(2,1)} %get-tuple-element.114), channel_id=1, source_target_pairs={{0,2},{2,0},{4,6},{6,4},{8,10},{10,8},{12,14},{14,12},{16,18},{18,... | collective-permute-start | bytes 1572872 | tf_op jit(solution)/shard_map/ppermute | solution.py:133
  97.0 73.4 %collective-permute-start.43 = (bf16[1,128,2048]{2,1,0:T(8,128)(2,1)}, bf16[1,128,2048]{2,1,0:T(8,128)(2,1)}, u32[]{:S(2)}, u32[]{:S(2)}) collective-permute-start(bf16[1,128,2048]{2,1,0:T(8,128)(2,1)} %get-tuple-element.115), channel_id=1, source_target_pairs={{0,4},{2,6},{4,0},{6,2},{8,12},{10,14},{12,8},{14,10},{16,20},{18,... | collective-permute-start | bytes 1572872 | tf_op jit(solution)/shard_map/ppermute | solution.py:133
  102.8 76.2 %collective-permute-start.44 = (bf16[1,128,2048]{2,1,0:T(8,128)(2,1)}, bf16[1,128,2048]{2,1,0:T(8,128)(2,1)}, u32[]{:S(2)}, u32[]{:S(2)}) collective-permute-start(bf16[1,128,2048]{2,1,0:T(8,128)(2,1)} %get-tuple-element.116), channel_id=1, source_target_pairs={{0,6},{2,4},{4,2},{6,0},{8,14},{10,12},{12,10},{14,8},{16,22},{18,... | collective-permute-start | bytes 1572872 | tf_op jit(solution)/shard_map/ppermute | solution.py:133
  133.4 47.5 %collective-permute-start.45 = (bf16[1,128,2048]{2,1,0:T(8,128)(2,1)}, bf16[1,128,2048]{2,1,0:T(8,128)(2,1)}, u32[]{:S(2)}, u32[]{:S(2)}) collective-permute-start(bf16[1,128,2048]{2,1,0:T(8,128)(2,1)} %get-tuple-element.117), channel_id=1, source_target_pairs={{0,8},{2,10},{4,12},{6,14},{8,0},{10,2},{12,4},{14,6},{16,24},{18,... | collective-permute-start | bytes 1572872 | tf_op jit(solution)/shard_map/ppermute | solution.py:133
  238.5 40.9 %collective-permute-start.23 = (bf16[1,128,2048]{2,1,0:T(8,128)(2,1)}, bf16[1,128,2048]{2,1,0:T(8,128)(2,1)}, u32[]{:S(2)}, u32[]{:S(2)}) collective-permute-start(bf16[1,128,2048]{2,1,0:T(8,128)(2,1)} %get-tuple-element.131), channel_id=1, source_target_pairs={{0,6},{2,4},{4,2},{6,0},{8,14},{10,12},{12,10},{14,8},{16,22},{18,... | collective-permute-start | bytes 1572872 | tf_op jit(solution)/shard_map/ppermute | solution.py:133
  240.3 41.1 %collective-permute-start.24 = (bf16[1,128,2048]{2,1,0:T(8,128)(2,1)}, bf16[1,128,2048]{2,1,0:T(8,128)(2,1)}, u32[]{:S(2)}, u32[]{:S(2)}) collective-permute-start(bf16[1,128,2048]{2,1,0:T(8,128)(2,1)} %get-tuple-element.132), channel_id=1, source_target_pairs={{0,8},{2,10},{4,12},{6,14},{8,0},{10,2},{12,4},{14,6},{16,24},{18,... | collective-permute-start | bytes 1572872 | tf_op jit(solution)/shard_map/ppermute | solution.py:133
  240.3 43.4 %collective-permute-start.25 = (bf16[1,128,2048]{2,1,0:T(8,128)(2,1)}, bf16[1,128,2048]{2,1,0:T(8,128)(2,1)}, u32[]{:S(2)}, u32[]{:S(2)}) collective-permute-start(bf16[1,128,2048]{2,1,0:T(8,128)(2,1)} %get-tuple-element.133), channel_id=1, source_target_pairs={{0,10},{2,8},{4,14},{6,12},{8,2},{10,0},{12,6},{14,4},{16,26},{18,... | collective-permute-start | bytes 1572872 | tf_op jit(solution)/shard_map/ppermute | solution.py:133
  251.9 33.7 %collective-permute-start.26 = (bf16[1,128,2048]{2,1,0:T(8,128)(2,1)}, bf16[1,128,2048]{2,1,0:T(8,128)(2,1)S(1)}, u32[]{:S(2)}, u32[]{:S(2)}) collective-permute-start(bf16[1,128,2048]{2,1,0:T(8,128)(2,1)} %get-tuple-element.134), channel_id=1, source_target_pairs={{0,12},{2,14},{4,8},{6,10},{8,4},{10,6},{12,0},{14,2},{16,28},{18,... | collective-permute-start | bytes 1572872 | tf_op jit(solution)/shard_map/ppermute | solution.py:133
  255.4 39.1 %collective-permute-start.27 = (bf16[1,128,2048]{2,1,0:T(8,128)(2,1)}, bf16[1,128,2048]{2,1,0:T(8,128)(2,1)S(1)}, u32[]{:S(2)}, u32[]{:S(2)}) collective-permute-start(bf16[1,128,2048]{2,1,0:T(8,128)(2,1)} %get-tuple-element.127), channel_id=1, source_target_pairs={{0,14},{2,12},{4,10},{6,8},{8,6},{10,4},{12,2},{14,0},{16,30},{18,... | collective-permute-start | bytes 1572872 | tf_op jit(solution)/shard_map/ppermute | solution.py:133
  279.4 138.7 %collective-permute-start.16 = (f32[256,1408]{1,0:T(8,128)}, f32[256,1408]{1,0:T(8,128)}, u32[]{:S(2)}, u32[]{:S(2)}) collective-permute-start(f32[256,1408]{1,0:T(8,128)} %slice_select_fusion.1), channel_id=1, source_target_pairs={{0,1},{1,0},{2,3},{3,2},{4,5},{5,4},{6,7},{7,6},{8,9},{9,8},{10,11... | collective-permute-start | bytes 4325384 | tf_op jit(solution)/shard_map/ppermute | solution.py:42
  281.3 138.4 %collective-permute-start.17 = (f32[256,1408]{1,0:T(8,128)S(1)}, f32[256,1408]{1,0:T(8,128)}, u32[]{:S(2)}, u32[]{:S(2)}) collective-permute-start(f32[256,1408]{1,0:T(8,128)S(1)} %slice_select_fusion), channel_id=1, source_target_pairs={{0,1},{1,0},{2,3},{3,2},{4,5},{5,4},{6,7},{7,6},{8,9},{9,8},{10,11... | collective-permute-start | bytes 4325384 | tf_op jit(solution)/shard_map/ppermute | solution.py:42
  443.6 41.9 %collective-permute-start.50 = (bf16[1,128,2048]{2,1,0:T(8,128)(2,1)S(1)}, bf16[1,128,2048]{2,1,0:T(8,128)(2,1)S(1)}, u32[]{:S(2)}, u32[]{:S(2)}) collective-permute-start(bf16[1,128,2048]{2,1,0:T(8,128)(2,1)S(1)} %copy-done.67), channel_id=1, source_target_pairs={{0,4},{2,6},{4,0},{6,2},{8,12},{10,14},{12,8},{14,10},{16,20},{18,... | collective-permute-start | bytes 1572872 | tf_op jit(solution)/shard_map/ppermute | solution.py:133
  445.6 43.1 %collective-permute-start.51 = (bf16[1,128,2048]{2,1,0:T(8,128)(2,1)S(1)}, bf16[1,128,2048]{2,1,0:T(8,128)(2,1)S(1)}, u32[]{:S(2)}, u32[]{:S(2)}) collective-permute-start(bf16[1,128,2048]{2,1,0:T(8,128)(2,1)S(1)} %copy-done.66), channel_id=1, source_target_pairs={{0,6},{2,4},{4,2},{6,0},{8,14},{10,12},{12,10},{14,8},{16,22},{18,... | collective-permute-start | bytes 1572872 | tf_op jit(solution)/shard_map/ppermute | solution.py:133
  469.3 32.8 %collective-permute-start.54 = (bf16[1,128,2048]{2,1,0:T(8,128)(2,1)S(1)}, bf16[1,128,2048]{2,1,0:T(8,128)(2,1)S(1)}, u32[]{:S(2)}, u32[]{:S(2)}) collective-permute-start(bf16[1,128,2048]{2,1,0:T(8,128)(2,1)S(1)} %copy-done.63), channel_id=1, source_target_pairs={{0,12},{2,14},{4,8},{6,10},{8,4},{10,6},{12,0},{14,2},{16,28},{18,... | collective-permute-start | bytes 1572872 | tf_op jit(solution)/shard_map/ppermute | solution.py:133
  488.6 176.9 %collective-permute-start.109 = (bf16[1024,1408]{1,0:T(8,128)(2,1)}, bf16[1024,1408]{1,0:T(8,128)(2,1)}, u32[]{:S(2)}, u32[]{:S(2)}) collective-permute-start(bf16[1024,1408]{1,0:T(8,128)(2,1)} %select_convert_fusion.2), channel_id=1, source_target_pairs={{0,1},{1,0},{2,3},{3,2},{4,5},{5,4},{6,7},{7,6},{8,9},{9,8},{10,11... | collective-permute-start | bytes 8650760 | tf_op jit(solution)/shard_map/ppermute | solution.py:42
  488.8 187.4 %collective-permute-start.110 = (bf16[1024,1408]{1,0:T(8,128)(2,1)}, bf16[1024,1408]{1,0:T(8,128)(2,1)}, u32[]{:S(2)}, u32[]{:S(2)}) collective-permute-start(bf16[1024,1408]{1,0:T(8,128)(2,1)} %select_convert_fusion.1), channel_id=1, source_target_pairs={{0,1},{1,0},{2,3},{3,2},{4,5},{5,4},{6,7},{7,6},{8,9},{9,8},{10,11... | collective-permute-start | bytes 8650760 | tf_op jit(solution)/shard_map/ppermute | solution.py:42
  490.0 49.3 %collective-permute-start.104 = (bf16[256,1408]{1,0:T(8,128)(2,1)S(1)}, bf16[256,1408]{1,0:T(8,128)(2,1)S(1)}, u32[]{:S(2)}, u32[]{:S(2)}) collective-permute-start(bf16[256,1408]{1,0:T(8,128)(2,1)S(1)} %get-tuple-element.145), channel_id=1, source_target_pairs={{1,0},{0,1},{3,2},{2,3},{5,4},{4,5},{7,6},{6,7},{9,8},{8,9},{11,10... | collective-permute-start | bytes 2162696 | tf_op jit(solution)/shard_map/ppermute | solution.py:37
  502.1 73.1 %collective-permute-start.18 = (f32[128,2048]{1,0:T(8,128)}, f32[128,2048]{1,0:T(8,128)}, u32[]{:S(2)}, u32[]{:S(2)}) collective-permute-start(f32[128,2048]{1,0:T(8,128)} %slice.668), channel_id=1, source_target_pairs={{0,1},{1,0},{2,3},{3,2},{4,5},{5,4},{6,7},{7,6},{8,9},{9,8},{10,11... | collective-permute-start | bytes 3145736 | tf_op jit(solution)/shard_map/ppermute | solution.py:42
  655.5 101.6 %collective-permute-start.111 = (bf16[704,2048]{1,0:T(8,128)(2,1)}, bf16[704,2048]{1,0:T(8,128)(2,1)}, u32[]{:S(2)}, u32[]{:S(2)}) collective-permute-start(bf16[704,2048]{1,0:T(8,128)(2,1)} %select_convert_fusion), channel_id=1, source_target_pairs={{0,1},{1,0},{2,3},{3,2},{4,5},{5,4},{6,7},{7,6},{8,9},{9,8},{10,11... | collective-permute-start | bytes 8650760 | tf_op jit(solution)/shard_map/ppermute | solution.py:42
  656.5 141.7 %collective-permute-start.96 = (bf16[8,1,64,2816]{3,2,0,1:T(8,128)(2,1)}, bf16[8,1,64,2816]{3,2,0,1:T(8,128)(2,1)}, u32[]{:S(2)}, u32[]{:S(2)}) collective-permute-start(bf16[8,1,64,2816]{3,2,0,1:T(8,128)(2,1)} %dynamic-slice_bitcast_fusion), channel_id=1, source_target_pairs={{0,2},{2,0},{4,6},{6,4},{8,10},{10,8},{12,14},{14,12},{16,18},{18,... | collective-permute-start | bytes 8650760 | tf_op jit(solution)/shard_map/ppermute | solution.py:133
  657.8 118.8 %collective-permute-start.100 = (bf16[4,2,64,2816]{3,2,0,1:T(8,128)(2,1)}, bf16[4,2,64,2816]{3,2,0,1:T(8,128)(2,1)}, u32[]{:S(2)}, u32[]{:S(2)}) collective-permute-start(bf16[4,2,64,2816]{3,2,0,1:T(8,128)(2,1)} %bitcast.469), channel_id=1, source_target_pairs={{0,4},{2,6},{4,0},{6,2},{8,12},{10,14},{12,8},{14,10},{16,20},{18,... | collective-permute-start | bytes 8650760 | tf_op jit(solution)/shard_map/ppermute | solution.py:133
  666.3 60.6 %collective-permute-start.65 = (bf16[256,576]{0,1:T(8,128)(2,1)S(1)}, bf16[256,576]{0,1:T(8,128)(2,1)S(1)}, u32[]{:S(2)}, u32[]{:S(2)}) collective-permute-start(bf16[256,576]{0,1:T(8,128)(2,1)S(1)} %slice.1103), channel_id=1, source_target_pairs={{0,2},{2,0},{4,6},{6,4},{8,10},{10,8},{12,14},{14,12},{16,18},{18,... | collective-permute-start | bytes 884744 | tf_op jit(solution)/shard_map/ppermute | solution.py:133
  676.2 52.5 %collective-permute-start.61 = (bf16[256,576]{0,1:T(8,128)(2,1)S(1)}, bf16[256,576]{0,1:T(8,128)(2,1)}, u32[]{:S(2)}, u32[]{:S(2)}) collective-permute-start(bf16[256,576]{0,1:T(8,128)(2,1)S(1)} %slice.1104), channel_id=1, source_target_pairs={{0,4},{2,6},{4,0},{6,2},{8,12},{10,14},{12,8},{14,10},{16,20},{18,... | collective-permute-start | bytes 884744 | tf_op jit(solution)/shard_map/ppermute | solution.py:133
  726.9 65.7 %collective-permute-start.105 = (bf16[4,2,64,2816]{3,2,0,1:T(8,128)(2,1)}, bf16[4,2,64,2816]{3,2,0,1:T(8,128)(2,1)}, u32[]{:S(2)}, u32[]{:S(2)}) collective-permute-start(bf16[4,2,64,2816]{3,2,0,1:T(8,128)(2,1)} %bitcast.534), channel_id=1, source_target_pairs={{0,4},{2,6},{4,0},{6,2},{8,12},{10,14},{12,8},{14,10},{16,20},{18,... | collective-permute-start | bytes 8650760 | tf_op jit(solution)/shard_map/ppermute | solution.py:133
  754.6 95.5 %collective-permute-start.92 = (bf16[8,1,64,2048]{3,2,0,1:T(8,128)(2,1)}, bf16[8,1,64,2048]{3,2,0,1:T(8,128)(2,1)}, u32[]{:S(2)}, u32[]{:S(2)}) collective-permute-start(bf16[8,1,64,2048]{3,2,0,1:T(8,128)(2,1)} %dynamic-slice_bitcast_fusion.1), channel_id=1, source_target_pairs={{0,2},{2,0},{4,6},{6,4},{8,10},{10,8},{12,14},{14,12},{16,18},{18,... | collective-permute-start | bytes 6291464 | tf_op jit(solution)/shard_map/ppermute | solution.py:133
  763.4 120.8 %collective-permute-start.87 = (bf16[16,1,128,512]{3,2,0,1:T(8,128)(2,1)}, bf16[16,1,128,512]{3,2,0,1:T(8,128)(2,1)}, u32[]{:S(2)}, u32[]{:S(2)}) collective-permute-start(bf16[16,1,128,512]{3,2,0,1:T(8,128)(2,1)} %broadcast_select_fusion), channel_id=1, source_target_pairs={{0,1},{1,0},{2,3},{3,2},{4,5},{5,4},{6,7},{7,6},{8,9},{9,8},{10,11... | collective-permute-start | bytes 6291464 | tf_op jit(solution)/shard_map/ppermute | solution.py:42
  776.6 114.0 %collective-permute-start.79 = (bf16[4,2,96,1024]{3,2,0,1:T(8,128)(2,1)}, bf16[4,2,96,1024]{3,2,0,1:T(8,128)(2,1)}, u32[]{:S(2)}, u32[]{:S(2)}) collective-permute-start(bf16[4,2,96,1024]{3,2,0,1:T(8,128)(2,1)} %bitcast.470), channel_id=1, source_target_pairs={{0,4},{2,6},{4,0},{6,2},{8,12},{10,14},{12,8},{14,10},{16,20},{18,... | collective-permute-start | bytes 4718600 | tf_op jit(solution)/shard_map/ppermute | solution.py:133
  792.6 100.6 %collective-permute-start.75 = (bf16[8,1,96,1024]{3,2,0,1:T(8,128)(2,1)}, bf16[8,1,96,1024]{3,2,0,1:T(8,128)(2,1)}, u32[]{:S(2)}, u32[]{:S(2)}) collective-permute-start(bf16[8,1,96,1024]{3,2,0,1:T(8,128)(2,1)} %dynamic-slice_bitcast_fusion.2), channel_id=1, source_target_pairs={{0,2},{2,0},{4,6},{6,4},{8,10},{10,8},{12,14},{14,12},{16,18},{18,... | collective-permute-start | bytes 4718600 | tf_op jit(solution)/shard_map/ppermute | solution.py:133
  849.5 69.1 %collective-permute-start.97 = (bf16[4,1,64,2816]{3,2,0,1:T(8,128)(2,1)S(1)}, bf16[4,1,64,2816]{3,2,0,1:T(8,128)(2,1)S(1)}, u32[]{:S(2)}, u32[]{:S(2)}) collective-permute-start(bf16[4,1,64,2816]{3,2,0,1:T(8,128)(2,1)S(1)} %dynamic-slice_bitcast_fusion.3), channel_id=1, source_target_pairs={{0,4},{2,6},{4,0},{6,2},{8,12},{10,14},{12,8},{14,10},{16,20},{18,... | collective-permute-start | bytes 4325384 | tf_op jit(solution)/shard_map/ppermute | solution.py:133
  850.2 31.9 %collective-permute-start.84 = (bf16[4,1,64,576]{3,2,0,1:T(8,128)(2,1)S(1)}, bf16[4,1,64,576]{3,2,0,1:T(8,128)(2,1)S(1)}, u32[]{:S(2)}, u32[]{:S(2)}) collective-permute-start(bf16[4,1,64,576]{3,2,0,1:T(8,128)(2,1)S(1)} %dynamic-slice_bitcast_fusion.14), channel_id=1, source_target_pairs={{0,4},{2,6},{4,0},{6,2},{8,12},{10,14},{12,8},{14,10},{16,20},{18,... | collective-permute-start | bytes 884744 | tf_op jit(solution)/shard_map/ppermute | solution.py:133
  882.0 38.0 %collective-permute-start.101 = (bf16[4,1,64,2816]{3,2,0,1:T(8,128)(2,1)S(1)}, bf16[4,1,64,2816]{3,2,0,1:T(8,128)(2,1)S(1)}, u32[]{:S(2)}, u32[]{:S(2)}) collective-permute-start(bf16[4,1,64,2816]{3,2,0,1:T(8,128)(2,1)S(1)} %constant_dynamic-slice_fusion.5), channel_id=1, source_target_pairs={{0,2},{2,0},{4,6},{6,4},{8,10},{10,8},{12,14},{14,12},{16,18},{18,... | collective-permute-start | bytes 4325384 | tf_op jit(solution)/shard_map/ppermute | solution.py:133
  889.9 57.6 %collective-permute-start.106 = (bf16[4,1,64,2816]{3,2,0,1:T(8,128)(2,1)S(1)}, bf16[4,1,64,2816]{3,2,0,1:T(8,128)(2,1)S(1)}, u32[]{:S(2)}, u32[]{:S(2)}) collective-permute-start(bf16[4,1,64,2816]{3,2,0,1:T(8,128)(2,1)S(1)} %constant_dynamic-slice_fusion.1), channel_id=1, source_target_pairs={{0,2},{2,0},{4,6},{6,4},{8,10},{10,8},{12,14},{14,12},{16,18},{18,... | collective-permute-start | bytes 4325384 | tf_op jit(solution)/shard_map/ppermute | solution.py:133
  899.6 49.0 %collective-permute-start.88 = (bf16[4,2,128,512]{3,2,1,0:T(8,128)(2,1)S(1)}, bf16[4,2,128,512]{3,2,1,0:T(8,128)(2,1)S(1)}, u32[]{:S(2)}, u32[]{:S(2)}) collective-permute-start(bf16[4,2,128,512]{3,2,1,0:T(8,128)(2,1)S(1)} %dynamic-slice_bitcast_fusion.5), channel_id=1, source_target_pairs={{0,4},{2,6},{4,0},{6,2},{8,12},{10,14},{12,8},{14,10},{16,20},{18,... | collective-permute-start | bytes 3145736 | tf_op jit(solution)/shard_map/ppermute | solution.py:133
  916.8 39.1 %collective-permute-start.80 = (bf16[4,1,96,1024]{3,2,0,1:T(8,128)(2,1)S(1)}, bf16[4,1,96,1024]{3,2,0,1:T(8,128)(2,1)S(1)}, u32[]{:S(2)}, u32[]{:S(2)}) collective-permute-start(bf16[4,1,96,1024]{3,2,0,1:T(8,128)(2,1)S(1)} %constant_dynamic-slice_fusion.14), channel_id=1, source_target_pairs={{0,2},{2,0},{4,6},{6,4},{8,10},{10,8},{12,14},{14,12},{16,18},{18,... | collective-permute-start | bytes 2359304 | tf_op jit(solution)/shard_map/ppermute | solution.py:133
  918.6 38.5 %collective-permute-start.76 = (bf16[4,1,96,1024]{3,2,0,1:T(8,128)(2,1)S(1)}, bf16[4,1,96,1024]{3,2,0,1:T(8,128)(2,1)S(1)}, u32[]{:S(2)}, u32[]{:S(2)}) collective-permute-start(bf16[4,1,96,1024]{3,2,0,1:T(8,128)(2,1)S(1)} %dynamic-slice_bitcast_fusion.6), channel_id=1, source_target_pairs={{0,4},{2,6},{4,0},{6,2},{8,12},{10,14},{12,8},{14,10},{16,20},{18,... | collective-permute-start | bytes 2359304 | tf_op jit(solution)/shard_map/ppermute | solution.py:133
  920.1 38.6 %collective-permute-start.94 = (bf16[2,1,64,2048]{3,2,0,1:T(8,128)(2,1)S(1)}, bf16[2,1,64,2048]{3,2,0,1:T(8,128)(2,1)S(1)}, u32[]{:S(2)}, u32[]{:S(2)}) collective-permute-start(bf16[2,1,64,2048]{3,2,0,1:T(8,128)(2,1)S(1)} %dynamic-slice_bitcast_fusion.11), channel_id=1, source_target_pairs={{0,8},{2,10},{4,12},{6,14},{8,0},{10,2},{12,4},{14,6},{16,24},{18,... | collective-permute-start | bytes 1572872 | tf_op jit(solution)/shard_map/ppermute | solution.py:133
  947.4 86.5 %collective-permute-start.98 = (bf16[2,1,64,2816]{3,2,0,1:T(8,128)(2,1)S(1)}, bf16[2,1,64,2816]{3,2,0,1:T(8,128)(2,1)S(1)}, u32[]{:S(2)}, u32[]{:S(2)}) collective-permute-start(bf16[2,1,64,2816]{3,2,0,1:T(8,128)(2,1)S(1)} %dynamic-slice_bitcast_fusion.9), channel_id=1, source_target_pairs={{0,8},{2,10},{4,12},{6,14},{8,0},{10,2},{12,4},{14,6},{16,24},{18,... | collective-permute-start | bytes 2162696 | tf_op jit(solution)/shard_map/ppermute | solution.py:133
  948.6 87.3 %collective-permute-start.102 = (bf16[2,1,64,2816]{3,2,0,1:T(8,128)(2,1)S(1)}, bf16[2,1,64,2816]{3,2,0,1:T(8,128)(2,1)S(1)}, u32[]{:S(2)}, u32[]{:S(2)}) collective-permute-start(bf16[2,1,64,2816]{3,2,0,1:T(8,128)(2,1)S(1)} %dynamic-slice_bitcast_fusion.8), channel_id=1, source_target_pairs={{0,8},{2,10},{4,12},{6,14},{8,0},{10,2},{12,4},{14,6},{16,24},{18,... | collective-permute-start | bytes 2162696 | tf_op jit(solution)/shard_map/ppermute | solution.py:133
  955.9 81.5 %collective-permute-start.107 = (bf16[2,1,64,2816]{3,2,0,1:T(8,128)(2,1)S(1)}, bf16[2,1,64,2816]{3,2,0,1:T(8,128)(2,1)S(1)}, u32[]{:S(2)}, u32[]{:S(2)}) collective-permute-start(bf16[2,1,64,2816]{3,2,0,1:T(8,128)(2,1)S(1)} %dynamic-slice_bitcast_fusion.7), channel_id=1, source_target_pairs={{0,8},{2,10},{4,12},{6,14},{8,0},{10,2},{12,4},{14,6},{16,24},{18,... | collective-permute-start | bytes 2162696 | tf_op jit(solution)/shard_map/ppermute | solution.py:133
  957.1 56.0 %collective-permute-start.81 = (bf16[2,1,96,1024]{3,2,1,0:T(8,128)(2,1)S(1)}, bf16[2,1,96,1024]{3,2,1,0:T(8,128)(2,1)S(1)}, u32[]{:S(2)}, u32[]{:S(2)}) collective-permute-start(bf16[2,1,96,1024]{3,2,1,0:T(8,128)(2,1)S(1)} %dynamic-slice_bitcast_fusion.12), channel_id=1, source_target_pairs={{0,8},{2,10},{4,12},{6,14},{8,0},{10,2},{12,4},{14,6},{16,24},{18,... | collective-permute-start | bytes 1179656 | tf_op jit(solution)/shard_map/ppermute | solution.py:133
  958.7 58.8 %collective-permute-start.77 = (bf16[2,1,96,1024]{3,2,0,1:T(8,128)(2,1)S(1)}, bf16[2,1,96,1024]{3,2,0,1:T(8,128)(2,1)S(1)}, u32[]{:S(2)}, u32[]{:S(2)}) collective-permute-start(bf16[2,1,96,1024]{3,2,0,1:T(8,128)(2,1)S(1)} %dynamic-slice_bitcast_fusion.13), channel_id=1, source_target_pairs={{0,8},{2,10},{4,12},{6,14},{8,0},{10,2},{12,4},{14,6},{16,24},{18,... | collective-permute-start | bytes 1179656 | tf_op jit(solution)/shard_map/ppermute | solution.py:133
  (219 other events, 3531.9 us)
Sparse Core Ops, SparseCore 0:
  9.6 18.9 all-gather.10
  30.1 16.8 all-gather.8
  48.6 17.1 all-gather.6

commit v2 on v1

--- a/solution.py
+++ b/solution.py
@@ -68,7 +68,7 @@
 def part_of(x, index, axis):
     count = lax.axis_size("wt")
     size = x.shape[axis] // count
-    if count == 2:
+    if count == 2 and axis > 0:
         return jnp.where(
             index == 0,
             lax.slice_in_dim(x, 0, size, axis=axis),
@@ -81,25 +81,25 @@
     return part_of(x, lax.axis_index("wt"), axis)
 
 
-def wt_sum_rows(x):
+def wt_sum_rows(x, sent=F32):
     count = lax.axis_size("wt")
     rows = x.shape[0] // count
     total = x[:rows]
     for step in range(1, count):
-        total = total + wt_to(x[step * rows : (step + 1) * rows], step)
+        total = total + wt_to(x[step * rows : (step + 1) * rows].astype(sent), step).astype(F32)
     return total
 
 
-def wt_sum_part(x, axis):
+def wt_sum_parts(arrays):
     count = lax.axis_size("wt")
     w = lax.axis_index("wt")
-    rows = x.shape[0] // count
-    total = my_part(x, axis)
+    rows = arrays[0].shape[0] // count
+    total = jnp.concatenate([my_part(x, 1) for x in arrays], axis=1)
     for step in range(1, count):
-        other = wt_to(part_of(x, (w + step) % count, axis), step)
-        other = jnp.concatenate([other[step * rows :], other[: step * rows]], axis=0)
-        total = total + other
-    return total
+        sent = jnp.concatenate([part_of(x, (w + step) % count, 1) for x in arrays], axis=1)
+        other = wt_to(sent.astype(BF), step).astype(F32)
+        total = total + jnp.concatenate([other[step * rows :], other[: step * rows]], axis=0)
+    return jnp.split(total, len(arrays), axis=1)
 
 
 def wt_own_rows(x):
@@ -118,14 +118,18 @@
     return in_order(parts, 1)
 
 
-def wt_all_columns(x):
+def wt_all_columns(arrays):
     count = lax.axis_size("wt")
-    rows = x.shape[0] // count
-    parts = [x]
+    rows = arrays[0].shape[0] // count
+    wide = arrays[0].shape[1]
+    merged = jnp.concatenate(arrays, axis=1)
+    parts = [[x] for x in arrays]
     for step in range(1, count):
-        other = wt_from(x, step)
-        parts.append(jnp.concatenate([other[-step * rows :], other[: -step * rows]], axis=0))
-    return in_order(parts, 1)
+        other = wt_from(merged, step)
+        other = jnp.concatenate([other[-step * rows :], other[: -step * rows]], axis=0)
+        for number, part in enumerate(parts):
+            part.append(other[:, number * wide : (number + 1) * wide])
+    return [in_order(part, 1) for part in parts]
 
 
 def ctx_swap(x, mask):
@@ -160,6 +164,58 @@
         half = x.shape[0] // 2
         x = x[:half] + ctx_swap(x[half:].astype(BF), bit).astype(F32)
     return x
+
+
+class Order:
+    def __init__(self):
+        self.signs = []
+
+    def __call__(self, x, *others):
+        signs = tuple(lax.slice(o, (0,) * o.ndim, (1,) * o.ndim).reshape(()).astype(F32) for o in others)
+        held = lax.optimization_barrier((x,) + signs)
+        self.signs += held[1:]
+        return held[0]
+
+    def seal(self, x):
+        return x + 0.0 * sum(self.signs)
+
+
+class Reduction:
+    def __init__(self, x, order, after):
+        self.x = x
+        self.after = after
+        self.tail = x.shape[1:]
+        self.order = list(order)
+        self.dims = sorted(order, reverse=True)
+        self.kept = None
+        self.got = None
+
+    def send(self, *others):
+        bit = self.order.pop(0)
+        place = self.dims.index(bit)
+        before, behind = 2**place, 2 ** (len(self.dims) - place - 1)
+        self.dims.pop(place)
+        view = self.x.reshape((before, 2, behind) + self.tail)
+        mine = (lax.axis_index("ctx") // bit) % 2
+        self.kept = lax.dynamic_index_in_dim(view, mine, 1, keepdims=False)
+        sent = lax.dynamic_index_in_dim(view, 1 - mine, 1, keepdims=False)
+        self.got = ctx_swap(self.after(sent, *others) if others else sent, bit)
+        return self
+
+    def take(self, *others):
+        got = self.after(self.got, *others) if others else self.got
+        total = self.kept.astype(F32) + got.astype(F32)
+        self.x = total.reshape((-1,) + self.tail)
+        if self.order:
+            self.x = self.x.astype(BF)
+        return self
+
+    def result(self, *others):
+        if self.got is not None:
+            self.take(*others)
+        while self.order:
+            self.send().take()
+        return self.x.reshape(self.tail)
 
 
 def ctx_reduce(x, order, sent=BF):
@@ -209,7 +265,7 @@
     return out, top + jnp.log(total), heads.reshape(heads.shape[0], H * DV).astype(BF)
 
 
-def attend_back(query, keys, seen, up_key, up_value, out, log_total, grad_heads, cos, sin):
+def attend_back(query, keys, seen, up_key, up_value, out, log_total, grad_heads, cos, sin, beside):
     rows = query.shape[1]
     scores = jnp.einsum("htr,kr->htk", query, keys, preferred_element_type=F32) * SCALE
     probs = jnp.exp(jnp.where(seen, scores, MASKED) - log_total)
@@ -222,13 +278,14 @@
     grad_query = jnp.einsum("htk,kr->htr", grad_scores, keys, preferred_element_type=F32)
     grad_keys = jnp.einsum("htk,htr->kr", grad_scores, query, preferred_element_type=F32)
     values_part = jnp.einsum("htk,htr->kr", probs.astype(BF), grad_out, preferred_element_type=F32)
+    values_part, beside = lax.optimization_barrier((values_part, beside))
     grad_keys = grad_keys + jnp.pad(values_part, ((0, 0), (0, DR)))
     grad_latent = grad_query[:, :, :R].astype(BF)
     nope = jnp.einsum("htr,rhd->thd", grad_latent, up_key, preferred_element_type=F32)
     first, second = grad_query[:, :, R : R + DR // 2], grad_query[:, :, R + DR // 2 :]
     rotary = jnp.concatenate([first * cos + second * sin, second * cos - first * sin], axis=2)
     grad_q = jnp.concatenate([nope, rotary.transpose(1, 0, 2)], axis=2).reshape(rows, H * DQ)
-    return grad_q.astype(BF), grad_latent, grad_keys
+    return grad_q.astype(BF), grad_latent, grad_keys, beside
 
 
 def rms_norm(values, gain):
@@ -260,7 +317,8 @@
 def route_matrices(routes, gates, capacity):
     count = lax.axis_size("ctx")
     rows = routes.shape[0]
-    experts = lax.axis_index("ctx") ^ jnp.arange(count // 2, dtype=jnp.int32)
+    half = count // 2
+    experts = lax.axis_index("ctx") // half * half + jnp.arange(half, dtype=jnp.int32)
     named = routes[:, :, None] == experts[None, None, :]
     chosen = jnp.any(named, axis=1)
     weight = jnp.sum(jnp.where(named, gates[:, :, None], 0.0), axis=1).T
@@ -303,15 +361,13 @@
     block = rows // 2
     half_ctx = n_ctx // 2
     capacity = min(rows, 4 * rows * TOP // (3 * n_ctx))
+    after = Order()
     order_a, order_b = spread_orders()
     reduce_a, reduce_b = order_a[::-1], order_b[::-1]
 
     tok = tokens[0]
     cot = cotangent[0]
-    tok_all = wt_rows(tok)
-    cot_all = wt_rows(cot)
-    kv_down = wt_gather(w_kv_down, 0)
-    kv_up = wt_gather(w_kv_up, 0)
+    kv_down = wt_gather(w_kv_down.T, 1)
     gains = jnp.stack(
         [gain_attn, gain_mlp, jnp.pad(gain_kv, (0, gain_attn.shape[0] - gain_kv.shape[0]))]
     ).astype(F32)
@@ -335,10 +391,9 @@
         ]
     )
 
-    inputs_all = tok_all.astype(F32)
-    inputs = inputs_all[:rows]
-    normed_one = rms_norm(inputs_all, gain_one).astype(BF)
-    kv = contract(normed_one[:rows], kv_down, 1, 0)
+    inputs = tok.astype(F32)
+    one_own = rms_norm(inputs, gain_one).astype(BF)
+    kv = contract(one_own, kv_down, 1, 1)
     latent_raw = kv[:, :R]
     latent = rms_norm(latent_raw, gain_latent).astype(BF)
     first, second = kv[:, R : R + DR // 2], kv[:, R + DR // 2 :]
@@ -348,7 +403,11 @@
     )
     keys_a = ctx_spread(own_keys[:block], order_a)
     keys_b = ctx_spread(own_keys[block:], order_b)
-    query = wt_sum_rows(contract(my_part(normed_one, 1), w_query, 1, 0))
+    tok_all = wt_rows(after(tok, own_keys))
+    cot_all = wt_rows(after(cot, own_keys))
+    kv_up = wt_gather(after(w_kv_up, own_keys), 0)
+    one_part = my_part(rms_norm(tok_all.astype(F32), gain_one).astype(BF), 1)
+    query = wt_sum_rows(contract(one_part, w_query, 1, 0), BF)
     up3 = kv_up.reshape(R, H, DN + DV)
     up_key, up_value = up3[:, :, :DN], up3[:, :, DN:]
     query_nope, query_cat = query_parts(query, cos, sin, up_key)
@@ -360,24 +419,23 @@
     place_other, high_other, low_other = route_matrices(
         partner(route_own.astype(F32)).astype(jnp.int32), partner(gate_own), capacity
     )
+    groups = [list(range(half_ctx)), list(range(half_ctx, n_ctx))]
+
     def swap_blocks(x):
-        return jnp.concatenate([x[:1]] + [ctx_swap(x[j : j + 1], j) for j in range(1, half_ctx)], axis=0)
-
-    def to_experts(own, other):
-        both = jnp.concatenate(
-            [own.reshape(half_ctx, capacity, D), other.reshape(half_ctx, capacity, D)], axis=1
-        )
-        return swap_blocks(both).reshape(-1, D)
-
-    def from_experts(x):
-        x = swap_blocks(x.reshape(half_ctx, 2 * capacity, D))
-        return x[:, :capacity].reshape(-1, D), x[:, capacity:].reshape(-1, D)
+        return lax.all_to_all(x, "ctx", 0, 0, axis_index_groups=groups, tiled=True)
+
+    def slots(x):
+        return x.astype(BF).reshape(half_ctx, capacity, D)
 
     cot_other = partner(cot)
-    rows_grad = to_experts(
-        (contract(high_own, cot, 1, 0) + contract(low_own, cot, 1, 0)).astype(BF),
-        (contract(high_other, cot_other, 1, 0) + contract(low_other, cot_other, 1, 0)).astype(BF),
-    )
+    rows_grad = jnp.concatenate(
+        [
+            slots(contract(high_own, cot, 1, 0) + contract(low_own, cot, 1, 0)),
+            slots(contract(high_other, cot_other, 1, 0) + contract(low_other, cot_other, 1, 0)),
+        ],
+        axis=1,
+    )
+    rows_grad = swap_blocks(after(rows_grad, keys_a, keys_b))
 
     keys = jnp.concatenate([keys_a, keys_b], axis=0)
     key_place = (blocks[:, :, None] * block + jnp.arange(block, dtype=jnp.int32)).reshape(1, -1)
@@ -386,60 +444,112 @@
     heads_all = wt_rows(heads_out)
     residual = inputs + wt_sum_rows(contract(my_part(heads_all, 1), w_out, 1, 0))
     normed_two = rms_norm(residual, gain_two).astype(BF)
-
+    normed_two, rows_grad = lax.optimization_barrier((normed_two, rows_grad))
+    grad_own, grad_other = rows_grad[:, :capacity].reshape(-1, D), rows_grad[:, capacity:].reshape(-1, D)
+
+    rows_own = swap_blocks(slots(contract(place_own, normed_two, 1, 0))).reshape(-1, D)
     normed_other = partner(normed_two)
-    rows_in = to_experts(
-        contract(place_own, normed_two, 1, 0).astype(BF),
-        contract(place_other, normed_other, 1, 0).astype(BF),
-    )
+    rows_other = swap_blocks(slots(contract(place_other, normed_other, 1, 0))).reshape(-1, D)
 
     two_all = wt_rows(normed_two)
     two_part = my_part(two_all, 1)
-    shared_gate = wt_sum_part(contract(two_part, w_shared_gate, 1, 0), 1)
-    shared_up = wt_sum_part(contract(two_part, w_shared_up, 1, 0), 1)
+    shared_gate, shared_up = wt_sum_parts(
+        [contract(two_part, w_shared_gate, 1, 0), contract(two_part, w_shared_up, 1, 0)]
+    )
     act, slope = silu_parts(shared_gate)
     hidden = (act * shared_up).astype(BF)
     shared_out = wt_sum_rows(contract(hidden, w_shared_down, 1, 0))
     grad_hidden = contract(cot_all, w_shared_down, 1, 1)
-    grad_gate = wt_all_columns((grad_hidden * shared_up * slope).astype(BF))
-    grad_up = wt_all_columns((grad_hidden * act).astype(BF))
-    hidden_all = wt_all_columns(hidden)
+    grad_gate, grad_up, hidden_all = wt_all_columns(
+        [(grad_hidden * shared_up * slope).astype(BF), (grad_hidden * act).astype(BF), hidden]
+    )
     shared_back = wt_own_rows(
         contract(grad_gate, w_shared_gate, 1, 1) + contract(grad_up, w_shared_up, 1, 1)
     )
 
-    def chosen_columns(x):
-        wide = x.shape[1] // (n_ctx * n_wt)
-        view = x.reshape(x.shape[0], n_ctx, n_wt, wide)
-        return my_part(view, 2).reshape(x.shape[0], n_ctx * wide)
-
-    def weight_grad(chunked, other, order):
-        grad = contract(chosen_columns(chunked), other, 0, 0).astype(BF)
-        return ctx_reduce(grad.reshape(n_ctx, -1, other.shape[1]), order)
-
-    grad_w_shared_gate = weight_grad(two_all, grad_gate, reduce_a)
-    grad_w_shared_up = weight_grad(two_all, grad_up, reduce_b)
-    grad_w_shared_down = weight_grad(cot_all, hidden_all, reduce_b).T
+    def pair_send(chunked, other, bit, *others):
+        mine = (c // bit) % 2
+        view = chunked.reshape(rows, half_ctx // bit, 2, -1)
+        keep = jnp.where(mine == 0, view[:, :, 0], view[:, :, 1]).reshape(rows, -1)
+        sent = jnp.where(mine == 0, view[:, :, 1], view[:, :, 0]).reshape(rows, -1)
+        got = ctx_swap(after(jnp.concatenate([sent, other], axis=1), *others), bit)
+        return jnp.concatenate([jnp.concatenate([keep, other], axis=1), got], axis=0), keep.shape[1]
+
+    def pair_grad(sent, *others):
+        both, wide = sent
+        both = wt_rows(after(both, *others))
+        columns, partners = both[:, :wide], both[:, wide:]
+        columns = my_part(columns.reshape(-1, half_ctx, n_wt, wide // (half_ctx * n_wt)), 2).reshape(-1, wide // n_wt)
+        grad = contract(columns, partners, 0, 0).astype(BF)
+        return grad.reshape(half_ctx, -1, partners.shape[1])
+
+    def scatter_sum(x, bit):
+        sides = [[i for i in range(n_ctx) if i // bit % 2 == side] for side in range(2)]
+        return lax.psum_scatter(x, "ctx", scatter_dimension=0, axis_index_groups=sides, tiled=True)[0].astype(F32)
 
     gate_matrix = lax.all_gather(w_expert_gate[0], "wt", axis=0, tiled=True)
     up_matrix = lax.all_gather(w_expert_up[0], "wt", axis=0, tiled=True)
     down_matrix = lax.all_gather(w_expert_down[0], "wt", axis=0, tiled=True)
-    expert_gate = contract(rows_in, gate_matrix, 1, 0)
-    expert_up = contract(rows_in, up_matrix, 1, 0)
-    expert_act, expert_slope = silu_parts(expert_gate)
-    expert_hidden = (expert_act * expert_up).astype(BF)
-    grad_expert_hidden = contract(rows_grad, down_matrix, 1, 1)
-    grad_expert_gate = (grad_expert_hidden * expert_up * expert_slope).astype(BF)
-    grad_expert_up = (grad_expert_hidden * expert_act).astype(BF)
-    grad_rows = (
-        contract(grad_expert_gate, gate_matrix, 1, 1) + contract(grad_expert_up, up_matrix, 1, 1)
-    ).astype(BF)
-    back_own, back_other = from_experts(grad_rows)
+
+    def expert(rows_in, rows_grad):
+        gate = contract(rows_in, gate_matrix, 1, 0)
+        up = contract(rows_in, up_matrix, 1, 0)
+        gate_act, gate_slope = silu_parts(gate)
+        grad_inner = contract(rows_grad, down_matrix, 1, 1)
+        grad_gate_pre = (grad_inner * up * gate_slope).astype(BF)
+        grad_up_pre = (grad_inner * gate_act).astype(BF)
+        grad_in = contract(grad_gate_pre, gate_matrix, 1, 1) + contract(grad_up_pre, up_matrix, 1, 1)
+        return (gate_act * up).astype(BF), grad_gate_pre, grad_up_pre, slots(grad_in)
+
+    hidden_1, grad_gate_1, grad_up_1, grad_in_1 = expert(rows_own, grad_own)
+    back_own = swap_blocks(grad_in_1).reshape(-1, D)
+    hidden_2, grad_gate_2, grad_up_2, grad_in_2 = expert(after(rows_other, grad_in_1), grad_other)
+    sent_gate_up = pair_send(
+        normed_two, jnp.concatenate([grad_gate[:rows], grad_up[:rows]], axis=1), reduce_a[0], grad_in_1
+    )
+    sent_down = pair_send(cot, hidden_all[:rows], reduce_b[0], grad_in_1)
+    grad_in_2, back_own = lax.optimization_barrier((grad_in_2, back_own))
+    back_other = swap_blocks(grad_in_2).reshape(-1, D)
+    grads_gate_up = pair_grad(sent_gate_up, grad_in_2)
+    grads_down = pair_grad(sent_down, grad_in_2)
+    sums_gate_up = scatter_sum(grads_gate_up, reduce_a[0])
+    sums_down = scatter_sum(grads_down, reduce_b[0])
+    produced = jnp.concatenate(
+        [slots(contract(after(x, grad_in_2), down_matrix, 1, 0)) for x in (hidden_1, hidden_2)], axis=1
+    )
     grad_routed = contract(place_own, back_own, 0, 0) + partner(
         contract(place_other, back_other, 0, 0).astype(BF)
     ).astype(F32)
-    produced = contract(expert_hidden, down_matrix, 1, 0).astype(BF)
-    out_own, out_other = from_experts(produced)
+
+    def expert_sum(grad):
+        total = my_part(grad, 0)
+        for step in range(1, n_wt):
+            w = lax.axis_index("wt")
+            total = total + wt_to(part_of(grad, (w + step) % n_wt, 0).astype(BF), step).astype(F32)
+        return total[None]
+
+    grad_two = shared_back + grad_routed
+    grad_part, grad_gain_mlp = rms_back(residual, gain_two, grad_two)
+    grad_residual = cot.astype(F32) + grad_part
+    grad_attn_own = grad_residual.astype(BF)
+    grad_attn = wt_rows(grad_attn_own)
+    grad_heads = wt_own_rows(contract(grad_attn, w_out, 1, 1).astype(BF))
+    sent_out = pair_send(grad_attn_own, heads_out, reduce_b[0], grad_heads)
+
+    out_rows = swap_blocks(after(produced, grad_routed))
+
+    grad_query, grad_query_latent, grad_keys, out_rows = attend_back(
+        query_cat, keys, seen, up_key, up_value, out_latent, log_total, grad_heads, cos, sin, out_rows
+    )
+    out_own, out_other = out_rows[:, :capacity].reshape(-1, D), out_rows[:, capacity:].reshape(-1, D)
+    grad_keys_a, grad_keys_b = jnp.split(grad_keys, 2, axis=0)
+    sent_query = [
+        pair_send(grad_query, one_own[:, part * (D // 2) : (part + 1) * (D // 2)], order[0], grad_keys_a)
+        for part, order in ((0, reduce_a), (1, reduce_b))
+    ]
+    grad_keys = jnp.concatenate(
+        [ctx_unspread(grad_keys_a, order_a), ctx_unspread(grad_keys_b, order_b)], axis=0
+    )
     routed = (
         contract(high_own, out_own, 0, 0)
         + contract(low_own, out_own, 0, 0)
@@ -448,32 +558,16 @@
         ).astype(F32)
     )
     mixed_out = (residual + shared_out + routed).astype(BF)
-
-    def expert_sum(grad):
-        total = my_part(grad, 0)
-        for step in range(1, n_wt):
-            w = lax.axis_index("wt")
-            total = total + wt_to(part_of(grad, (w + step) % n_wt, 0).astype(BF), step).astype(F32)
-        return total[None]
-
-    grad_w_expert_gate = expert_sum(contract(rows_in, grad_expert_gate, 0, 0))
-    grad_w_expert_up = expert_sum(contract(rows_in, grad_expert_up, 0, 0))
+    rows_own, rows_other, grad_own, grad_other = (
+        after(x, grad_keys_a) for x in (rows_own, rows_other, grad_own, grad_other)
+    )
+    rows_in = jnp.concatenate([rows_own, rows_other], axis=0)
+    expert_hidden = jnp.concatenate([hidden_1, hidden_2], axis=0)
+    rows_grad = jnp.concatenate([grad_own, grad_other], axis=0)
+    grad_w_expert_gate = expert_sum(contract(rows_in, jnp.concatenate([grad_gate_1, grad_gate_2], axis=0), 0, 0))
+    grad_w_expert_up = expert_sum(contract(rows_in, jnp.concatenate([grad_up_1, grad_up_2], axis=0), 0, 0))
     grad_w_expert_down = expert_sum(contract(expert_hidden, rows_grad, 0, 0))
 
-    grad_two = shared_back + grad_routed
-    grad_part, grad_gain_mlp = rms_back(residual, gain_two, grad_two)
-    grad_residual = cot.astype(F32) + grad_part
-    grad_attn = wt_rows(grad_residual.astype(BF))
-    grad_heads = wt_own_rows(contract(grad_attn, w_out, 1, 1).astype(BF))
-    grad_w_out = weight_grad(grad_attn, heads_all, reduce_a).T
-
-    grad_query, grad_query_latent, grad_keys = attend_back(
-        query_cat, keys, seen, up_key, up_value, out_latent, log_total, grad_heads, cos, sin
-    )
-    grad_keys_a, grad_keys_b = jnp.split(grad_keys, 2, axis=0)
-    grad_keys = jnp.concatenate(
-        [ctx_unspread(grad_keys_a, order_a), ctx_unspread(grad_keys_b, order_b)], axis=0
-    )
     grad_up_key = jnp.einsum(
         "thd,htr->hdr", query_nope, grad_query_latent, preferred_element_type=F32
     )
@@ -486,23 +580,16 @@
     for step in range(1, n_wt):
         w = lax.axis_index("wt")
         own_up = own_up + wt_to(part_of(up_grads, (w + step) % n_wt, 1), step).astype(F32)
-    grad_w_kv_up = ctx_reduce(own_up.astype(BF).reshape(n_ctx, -1, R), reduce_b).T
+    sum_kv_up = Reduction(own_up.astype(BF).reshape(n_ctx, -1, R), reduce_a, after)
 
     query_all = wt_rows(grad_query)
-    query_columns = chosen_columns(query_all)
-    grad_w_query = jnp.concatenate(
-        [
-            ctx_reduce(
-                contract(query_columns, normed_one[:, part * (D // 2) : (part + 1) * (D // 2)], 0, 0)
-                .astype(BF)
-                .reshape(n_ctx, -1, D // 2),
-                order,
-            ).T
-            for part, order in ((0, reduce_a), (1, reduce_b))
-        ],
-        axis=0,
-    )
-    one_part = contract(query_all, w_query, 1, 1)
+    sum_out = Reduction(pair_grad(sent_out, grad_keys_a), reduce_b[1:], after).send()
+    sums_query = [
+        Reduction(pair_grad(sent, grad_keys), order[1:], after).send()
+        for sent, order in zip(sent_query, (reduce_a, reduce_b))
+    ]
+    sum_kv_up.send(grad_keys)
+    one_back = contract(query_all, w_query, 1, 1)
 
     grad_latent, grad_gain_kv = rms_back(latent_raw, gain_latent, grad_keys[:, :R])
     first, second = grad_keys[:, R : R + DR // 2], grad_keys[:, R + DR // 2 :]
@@ -510,8 +597,8 @@
         [grad_latent, first * cos + second * sin, second * cos - first * sin], axis=1
     ).astype(BF)
     grad_kv_all = wt_rows(grad_kv)
-    grad_w_kv_down = weight_grad(normed_one, grad_kv_all, reduce_a)
-    grad_one = wt_own_rows(one_part + contract(grad_kv_all, w_kv_down, 1, 1))
+    sum_kv_down = Reduction(pair_grad(pair_send(one_own, grad_kv, reduce_b[0], grad_kv)), reduce_b[1:], after)
+    grad_one = wt_own_rows(one_back + contract(grad_kv_all, w_kv_down, 1, 1))
     grad_inputs, grad_gain_attn = rms_back(inputs, gain_one, grad_one)
     grad_tokens = grad_residual + grad_inputs
 
@@ -526,8 +613,14 @@
     for step in range(1, n_wt):
         w = lax.axis_index("wt")
         own_gain = own_gain + wt_to(part_of(gain_grads, (w + step) % n_wt, 1), step)
-    gain_total = ctx_reduce(own_gain.reshape(n_ctx, 1, -1), reduce_b, F32)[0]
+    gain_total = after.seal(ctx_reduce(own_gain.reshape(n_ctx, 1, -1), reduce_b, F32)[0])
     wide = D // (n_ctx * n_wt)
+    grad_w_kv_down = sum_kv_down.result()
+    grad_w_query = jnp.concatenate([part.result().T for part in sums_query], axis=0)
+    grad_w_kv_up = sum_kv_up.result().T
+    grad_w_shared_gate, grad_w_shared_up = jnp.split(sums_gate_up, 2, axis=1)
+    grad_w_shared_down = sums_down.T
+    grad_w_out = sum_out.result().T
 
     return (
         mixed_out[None],

time: 1090 us -> 879 us (0.81)
  waiting for transfers between devices: 469 us -> 201 us
  local copies, waits for them, and re-layouts: 115 us -> 144 us
  starting transfers between devices: 99.5 us -> 116 us
  other arithmetic: 127 us -> 113 us
  between operations: 17.4 us -> 29.5 us
  matrix products: 252 us -> 264 us
    ppermute x86 -> x48, waiting for transfers between devices: 466 us -> 169 us  [ctx_swap(): return lax.ppermute(x, 'ctx', [(i, i ^ mask) for i in range(count)])]
    convert_element_type x32 -> x17, other arithmetic: 45.5 us -> 7.91 us  [the longest x11 4.46 us: take(): self.x = self.x.astype(BF)]
    all_to_all x0 -> x6, starting transfers between devices: none -> 30.2 us  [swap_blocks(): return lax.all_to_all(x, 'ctx', 0, 0, axis_index_groups=groups, tiled=True)]
    all_to_all x0 -> x6, waiting for transfers between devices: none -> 29.3 us  [swap_blocks(): return lax.all_to_all(x, 'ctx', 0, 0, axis_index_groups=groups, tiled=True)]
    slice x10 -> x28, local copies, waits for them, and re-layouts: 9.51 us -> 32.1 us  [the longest x7 9.66 us: pair_grad(): columns, partners = (both[:, :wide], both[:, wide:])]
    concatenate x4 -> x18, other arithmetic: 5.78 us -> 26.5 us  [the longest x6 11.5 us: pair_send(): jnp.concatenate([jnp.concatenate([keep, other], axis=1), got], axis=0)]
    ppermute x86 -> x48, starting transfers between devices: 95.5 us -> 80.5 us  [ctx_swap(): return lax.ppermute(x, 'ctx', [(i, i ^ mask) for i in range(count)])]
    dot_general x42 -> x47, matrix products: 185 us -> 196 us  [contract(): lax.dot_general(former, latter, (((former_dim,), (latter_dim,)), ((), ())...]
  transfers between devices with their start and end apart: 115 -> 88, of which waited for: 49 -> 33; matrix products, arithmetic and copies ran while one was open for 44% -> 57% of each run, Pallas kernels for 0% -> 0%
where the time goes in v2:
time: 879 us; the launch traced here: 867 us
  matrix products  264 us (30%)
  waiting for transfers between devices  201 us (23%)
  local copies, waits for them, and re-layouts  144 us (16%)
  starting transfers between devices  116 us (13%)
  other arithmetic  113 us (13%)
  between operations  29.5 us (3%)
    dot_general x47, matrix products, contract(): lax.dot_general(former, latter, (((former_dim,), (latter_dim,)), ((), ())...  196 us
    ppermute x48, waiting for transfers between devices, ctx_swap(): return lax.ppermute(x, 'ctx', [(i, i ^ mask) for i in range(count)])  169 us
    ppermute x48, starting transfers between devices, ctx_swap(): return lax.ppermute(x, 'ctx', [(i, i ^ mask) for i in range(count)])  80.5 us
    unnamed x417, local copies, waits for them, and re-layouts  42.2 us
    all_to_all x6, starting transfers between devices, swap_blocks(): return lax.all_to_all(x, 'ctx', 0, 0, axis_index_groups=groups, tiled=True)  30.2 us
    all_to_all x6, waiting for transfers between devices, swap_blocks(): return lax.all_to_all(x, 'ctx', 0, 0, axis_index_groups=groups, tiled=True)  29.3 us
    broadcast_in_dim x3, other arithmetic, expert_sum(): return total[None]  17.6 us
  transfers between devices with their start and end apart: 88, of which 33 were waited for; matrix products, arithmetic and copies ran while one was open for 57% of the time, Pallas kernels for 0%

profile of v2, /device:TPU:0, one launch (start us, length us, event | category | flops | bytes accessed | tf_op | source)
XLA Modules:
  0.0 867.4 jit_solution(8603315006928173039)
XLA Ops:
  19.5 9.1 %collective-permute-done.16 = f32[128,6]{0,1:T(8,128)S(1)} collective-permute-done((f32[128,6]{0,1:T(8,128)S(1)}, f32[128,6]{0,1:T(8,128)S(1)}, u32[]{:S(2)}, u32[]{:S(2)}) %collective-permute-start.16) | collective-permute-done | bytes 3104 | tf_op jit(solution)/shard_map/ppermute | solution.py:137
  40.4 9.0 %collective-permute-done.9 = bf16[64,576]{0,1:T(8,128)(2,1)S(1)} collective-permute-done((bf16[64,576]{0,1:T(8,128)(2,1)S(1)}, bf16[64,576]{0,1:T(8,128)(2,1)S(1)}, u32[]{:S(2)}, u32[]{:S(2)}) %collective-permute-start.9) | collective-permute-done | bytes 73760 | tf_op jit(solution)/shard_map/ppermute | solution.py:137
  99.4 4.9 concatenate.293
  126.5 8.2 fusion.3
  140.4 6.7 fusion.6
  176.2 5.3 all-to-all-start.2
  181.6 8.5 fusion.37
  190.1 5.1 fusion.39
  209.0 5.4 fusion.196
  238.9 5.3 all-to-all-start.1
  244.3 7.6 fusion.23
  251.9 8.8 %multiply_convert_fusion.2 = (bf16[512,1408]{1,0:T(8,128)(2,1)}, bf16[512,1408]{1,0:T(8,128)(2,1)S(1)}, bf16[512,1408]{1,0:T(8,128)(2,1)S(1)}) fusion(f32[512,1408]{1,0:T(8,128)} %fusion.23, f32[512,1408]{1,0:T(8,128)} %fusion.37, bf16[512,2048]{1,0:T(8,128)(2,1)S(1)} %bitcast.449, bf16[1,2048,1408]{2,1,0:T(8,128)(2,1)} %all-gather.9.cloned.1.call-done), kind=kOutput, calls=%fused_computation.90 | convolution fusion | flops 2963603456 | bytes 17956864 | tf_op jit(solution)/shard_map/dot_general | solution.py:27
  287.1 6.5 fusion.19
  293.6 8.7 %multiply_convert_fusion.1 = (bf16[512,1408]{1,0:T(8,128)(2,1)}, bf16[512,1408]{1,0:T(8,128)(2,1)S(1)}, bf16[512,1408]{1,0:T(8,128)(2,1)S(1)}) fusion(f32[512,1408]{1,0:T(8,128)S(1)} %fusion.19, f32[512,1408]{1,0:T(8,128)S(1)} %copy-done.174, bf16[512,2048]{1,0:T(8,128)(2,1)} %bitcast.36, bf16[1,2048,1408]{2,1,0:T(8,128)(2,1)} %all-gather.9.cloned.1.call-done), kind=kOutput, calls=%fused_computation.89 | convolution fusion | flops 2963603456 | bytes 17956864 | tf_op jit(solution)/shard_map/dot_general | solution.py:27
  313.3 27.2 %all-to-all-done.3 = bf16[8,64,2048]{2,1,0:T(8,128)(2,1)S(1)} async-done(((bf16[8,64,2048]{2,1,0:T(8,128)(2,1)}), bf16[8,64,2048]{2,1,0:T(8,128)(2,1)S(1)}, u32[]{:S(2)}, u32[]{:S(2)}) %all-to-all-start.3) | async-done | bytes 2097184 | tf_op jit(solution)/shard_map/all_to_all | solution.py:425
  342.3 5.0 convolution_add_fusion
  366.3 5.0 convolution_convert_fusion.1
  371.4 6.6 fusion.52
  378.0 6.5 fusion.55
  403.0 24.7 %collective-permute-done.25 = bf16[128,2048]{1,0:T(8,128)(2,1)} collective-permute-done((bf16[128,2048]{1,0:T(8,128)(2,1)}, bf16[128,2048]{1,0:T(8,128)(2,1)}, u32[]{:S(2)}, u32[]{:S(2)}) %collective-permute-start.25) | collective-permute-done | bytes 524320 | tf_op jit(solution)/shard_map/ppermute | solution.py:137
  432.3 4.9 convolution_convert_fusion
  438.7 6.7 all-to-all-start.5
  456.3 5.2 multiply_reduce_fusion
  461.5 11.8 %multiply_convert_fusion = bf16[16,128,2048]{2,1,0:T(8,128)(2,1)S(1)} fusion(f32[16,128,2048]{2,1,0:T(8,128)} %copy-done.8, f32[16,128]{1,0:T(8,128)S(1)} %get-tuple-element.293, f32[16,128]{1,0:T(8,128)S(1)} %copy-done.143, pred[128,2048]{1,0:T(8,128)(4,1)S(1)} %copy-done.85, bf16[16,128,512]{2,1,0:T(8,128)(2,1)} %get-tuple-element.294, ...), kind=kOutput, calls=%fused_computation.2 | convolution fusion | flops 4324327424 | bytes 29638656 | tf_op jit(solution)/shard_map/htr,kr->htk/dot_general | solution.py:276
  473.3 5.1 fusion.82
  491.9 10.1 %fusion.45 = f32[2048,512]{1,0:T(8,128)} fusion(bf16[16,128,512]{2,1,0:T(8,128)(2,1)} %get-tuple-element.294, f32[16,128,2048]{2,1,0:T(8,128)S(1)} %bitcast.441, f32[16,128]{1,0:T(8,128)S(1)} %copy-done.143, pred[128,2048]{1,0:T(8,128)(4,1)S(1)} %copy-done.85), kind=kOutput, calls=%fused_computation.70 | convolution fusion | flops 4311744512 | bytes 23339008 | tf_op jit(solution)/shard_map/htk,htr->kr/dot_general | solution.py:280
  509.1 7.7 collective-permute-done.47
  527.2 5.3 copy.326
  532.6 9.6 %fusion.277 = (bf16[2048,576]{0,1:T(8,128)(2,1)S(1)}, f32[2048,576]{0,1:T(8,128)S(1)}) fusion(f32[2048,512]{0,1:T(8,128)} %copy.326, bf16[16,128,2048]{2,1,0:T(8,128)(2,1)} %copy-done.169, bf16[16,128,64]{2,1,0:T(8,128)(2,1)S(1)} %copy-done.99, bf16[16,128,512]{2,1,0:T(8,128)(2,1)} %copy-done.67), kind=kOutput, calls=%fused_computation.543 | convolution fusion | flops 4838916096 | bytes 22020096 | tf_op jit(solution)/shard_map/htk,htr->kr/dot_general | solution.py:279
  546.9 6.8 fusion.63
  553.7 11.3 %fusion.59 = f32[2048,1408]{1,0:T(8,128)S(1)} fusion(bf16[1024,2048]{1,0:T(8,128)(2,1)S(1)} %constant_dynamic-update-slice_fusion.12, bf16[512,1408]{1,0:T(8,128)(2,1)} %copy-done.180, bf16[512,1408]{1,0:T(8,128)(2,1)} %copy-done.179), kind=kOutput, calls=%fused_computation.78 | convolution fusion | flops 5911347200 | bytes 18612224 | tf_op jit(solution)/shard_map/dot_general | solution.py:27
  580.9 16.9 %collective-permute-start.30 = (bf16[512,576]{0,1:T(8,128)(2,1)}, bf16[512,576]{0,1:T(8,128)(2,1)}, u32[]{:S(2)}, u32[]{:S(2)}) collective-permute-start(bf16[512,576]{0,1:T(8,128)(2,1)} %get-tuple-element.233), channel_id=1, source_target_pairs={{0,2},{2,0},{4,6},{6,4},{8,10},{10,8},{12,14},{14,12},{16,18},{18,... | collective-permute-start | bytes 1769480 | tf_op jit(solution)/shard_map/ppermute | solution.py:137
  599.0 9.2 %fusion.41 = f32[1408,2048]{1,0:T(8,128)} fusion(bf16[512,2048]{1,0:T(8,128)(2,1)S(1)} %bitcast.500, bf16[512,2048]{1,0:T(8,128)(2,1)S(1)} %bitcast.502, bf16[512,1408]{1,0:T(8,128)(2,1)S(1)} %copy-done.173, bf16[512,1408]{1,0:T(8,128)(2,1)S(1)} %copy-done.171), kind=kOutput, calls=%fused_computation.59 | convolution fusion | flops 5919735808 | bytes 18612224 | tf_op jit(solution)/shard_map/dot_general | solution.py:27
  628.4 9.8 %collective-permute-done.49 = bf16[128,2560]{0,1:T(8,128)(2,1)S(1)} collective-permute-done((bf16[128,2560]{0,1:T(8,128)(2,1)S(1)}, bf16[128,2560]{0,1:T(8,128)(2,1)S(1)}, u32[]{:S(2)}, u32[]{:S(2)}) %collective-permute-start.49) | collective-permute-done | bytes 655392 | tf_op jit(solution)/shard_map/ppermute | solution.py:137
  646.7 5.0 collective-permute-done.32
  651.8 5.2 collective-permute-done.36
  658.7 8.1 collective-permute-done.33
  667.4 6.7 collective-permute-done.37
  688.3 4.9 fusion.114
  693.3 5.9 collective-permute-done.59
  718.7 6.2 collective-permute-done.28
  730.5 12.0 %collective-permute-done.64 = bf16[8,1,128,512]{3,2,0,1:T(8,128)(2,1)S(1)} collective-permute-done((bf16[8,1,128,512]{3,2,0,1:T(8,128)(2,1)S(1)}, bf16[8,1,128,512]{3,2,0,1:T(8,128)(2,1)S(1)}, u32[]{:S(2)}, u32[]{:S(2)}) %collective-permute-start.64) | collective-permute-done | bytes 1048608 | tf_op jit(solution)/shard_map/ppermute | solution.py:137
  758.8 13.9 %collective-permute-done.69 = bf16[4,1,64,2048]{3,2,0,1:T(8,128)(2,1)S(1)} collective-permute-done((bf16[4,1,64,2048]{3,2,0,1:T(8,128)(2,1)}, bf16[4,1,64,2048]{3,2,0,1:T(8,128)(2,1)S(1)}, u32[]{:S(2)}, u32[]{:S(2)}) %collective-permute-start.69) | collective-permute-done | bytes 1048608 | tf_op jit(solution)/shard_map/ppermute | solution.py:137
  775.0 6.5 collective-permute-done.61
  797.7 7.1 add_bitcast_fusion.1
  817.2 5.7 add_bitcast_fusion
  835.6 7.5 collective-permute-done.53
  851.0 5.8 collective-permute-done.54
  (865 shorter events, 442.6 us)
Async XLA Ops:
  7.3 174.3 %all-gather.7.cloned.1.call-start = ((), (), s32[]{:S(2)}) async-start(), calls=%async_computation.10 | async-start | bytes 8650752 | tf_op jit(solution)/shard_map/all_gather | solution.py:492
  8.0 236.2 %all-gather.11.cloned.1.call-start = ((), (), s32[]{:S(2)}) async-start(), calls=%async_computation.12 | async-start | bytes 8650752 | tf_op jit(solution)/shard_map/all_gather | solution.py:490
  8.2 22.1 %collective-permute-start = (f32[1,3,1024]{2,0,1:T(1,128)S(1)}, f32[1,3,1024]{2,0,1:T(1,128)S(1)}, u32[]{:S(2)}, u32[]{:S(2)}) collective-permute-start(f32[1,3,1024]{2,0,1:T(1,128)S(1)} %maximum_convert_fusion.1), channel_id=1, source_target_pairs={{1,0},{0,1},{3,2},{2,3},{5,4},{4,5},{7,6},{6,7},{9,8},{8,9},{11,10... | collective-permute-start | bytes 36872 | tf_op jit(solution)/shard_map/ppermute | solution.py:37
  8.7 22.5 %collective-permute-start.1 = (bf16[576,1024]{1,0:T(8,128)(2,1)}, bf16[576,1024]{1,0:T(8,128)(2,1)}, u32[]{:S(2)}, u32[]{:S(2)}) collective-permute-start(bf16[576,1024]{1,0:T(8,128)(2,1)} %bitcast.1), channel_id=1, source_target_pairs={{1,0},{0,1},{3,2},{2,3},{5,4},{4,5},{7,6},{6,7},{9,8},{8,9},{11,10... | collective-permute-start | bytes 3538952 | tf_op jit(solution)/shard_map/ppermute | solution.py:37
  12.9 46.7 %collective-permute-start.17 = (bf16[128,2048]{1,0:T(8,128)(2,1)S(1)}, bf16[128,2048]{1,0:T(8,128)(2,1)}, u32[]{:S(2)}, u32[]{:S(2)}) collective-permute-start(bf16[128,2048]{1,0:T(8,128)(2,1)S(1)} %bitcast.442), channel_id=1, source_target_pairs={{0,16},{2,18},{4,20},{6,22},{8,24},{10,26},{12,28},{14,30},{16,0},... | collective-permute-start | bytes 1572872 | tf_op jit(solution)/shard_map/ppermute | solution.py:137
  52.1 20.7 %collective-permute-start.3 = (bf16[128,2048]{1,0:T(8,128)(2,1)S(1)}, bf16[128,2048]{1,0:T(8,128)(2,1)}, u32[]{:S(2)}, u32[]{:S(2)}) collective-permute-start(bf16[128,2048]{1,0:T(8,128)(2,1)S(1)} %bitcast.437), channel_id=1, source_target_pairs={{1,0},{0,1},{3,2},{2,3},{5,4},{4,5},{7,6},{6,7},{9,8},{8,9},{11,10... | collective-permute-start | bytes 1572872 | tf_op jit(solution)/shard_map/ppermute | solution.py:37
  67.5 46.7 %collective-permute-start.2 = (bf16[256,4096]{0,1:T(8,128)(2,1)}, bf16[256,4096]{0,1:T(8,128)(2,1)}, u32[]{:S(2)}, u32[]{:S(2)}) collective-permute-start(bf16[256,4096]{0,1:T(8,128)(2,1)} %copy.299), channel_id=1, source_target_pairs={{1,0},{0,1},{3,2},{2,3},{5,4},{4,5},{7,6},{6,7},{9,8},{8,9},{11,10... | collective-permute-start | bytes 6291464 | tf_op jit(solution)/shard_map/ppermute | solution.py:37
  72.3 26.6 %collective-permute-start.12 = (bf16[512,576]{0,1:T(8,128)(2,1)}, bf16[512,576]{0,1:T(8,128)(2,1)}, u32[]{:S(2)}, u32[]{:S(2)}) collective-permute-start(bf16[512,576]{0,1:T(8,128)(2,1)} %pad_maximum_fusion.27), channel_id=1, source_target_pairs={{0,4},{2,6},{4,0},{6,2},{8,12},{10,14},{12,8},{14,10},{16,20},{18,... | collective-permute-start | bytes 1769480 | tf_op jit(solution)/shard_map/ppermute | solution.py:137
  81.3 23.1 %collective-permute-start.4 = (bf16[128,3072]{1,0:T(8,128)(2,1)}, bf16[128,3072]{1,0:T(8,128)(2,1)}, u32[]{:S(2)}, u32[]{:S(2)}) collective-permute-start(bf16[128,3072]{1,0:T(8,128)(2,1)} %slice.908), channel_id=1, source_target_pairs={{0,1},{1,0},{2,3},{3,2},{4,5},{5,4},{6,7},{7,6},{8,9},{9,8},{10,11... | collective-permute-start | bytes 2359304 | tf_op jit(solution)/shard_map/ppermute | solution.py:42
  93.9 73.3 %all-to-all-start = ((bf16[8,128,2048]{2,1,0:T(8,128)(2,1)}), bf16[8,128,2048]{2,1,0:T(8,128)(2,1)}, u32[]{:S(2)}, u32[]{:S(2)}) async-start(bf16[8,128,2048]{2,1,0:T(8,128)(2,1)} %pad_maximum_fusion), calls=%async_computation | async-start | bytes 8388608 | tf_op jit(solution)/shard_map/all_to_all | solution.py:425
  98.6 153.3 %all-gather.9.cloned.1.call-start = ((), (), s32[]{:S(2)}) async-start(), calls=%async_computation.11 | async-start | bytes 8650752 | tf_op jit(solution)/shard_map/all_gather | solution.py:491
  163.3 65.1 %collective-permute-start.21 = (bf16[128,2048]{1,0:T(8,128)(2,1)S(1)}, bf16[128,2048]{1,0:T(8,128)(2,1)}, u32[]{:S(2)}, u32[]{:S(2)}) collective-permute-start(bf16[128,2048]{1,0:T(8,128)(2,1)S(1)} %bitcast.443), channel_id=1, source_target_pairs={{1,0},{0,1},{3,2},{2,3},{5,4},{4,5},{7,6},{6,7},{9,8},{8,9},{11,10... | collective-permute-start | bytes 1572872 | tf_op jit(solution)/shard_map/ppermute | solution.py:37
  167.2 53.8 %collective-permute-start.24 = (bf16[128,2048]{1,0:T(8,128)(2,1)S(1)}, bf16[128,2048]{1,0:T(8,128)(2,1)}, u32[]{:S(2)}, u32[]{:S(2)}) collective-permute-start(bf16[128,2048]{1,0:T(8,128)(2,1)S(1)} %multiply_convert_fusion.10), channel_id=1, source_target_pairs={{0,16},{2,18},{4,20},{6,22},{8,24},{10,26},{12,28},{14,30},{16,0},... | collective-permute-start | bytes 1572872 | tf_op jit(solution)/shard_map/ppermute | solution.py:137
  169.4 34.2 %collective-permute-start.18 = (bf16[128,2048]{1,0:T(8,128)(2,1)S(1)}, bf16[128,2048]{1,0:T(8,128)(2,1)}, u32[]{:S(2)}, u32[]{:S(2)}) collective-permute-start(bf16[128,2048]{1,0:T(8,128)(2,1)S(1)} %multiply_convert_fusion.10), channel_id=1, source_target_pairs={{1,0},{0,1},{3,2},{2,3},{5,4},{4,5},{7,6},{6,7},{9,8},{8,9},{11,10... | collective-permute-start | bytes 1572872 | tf_op jit(solution)/shard_map/ppermute | solution.py:37
  176.2 62.7 %all-to-all-start.2 = ((bf16[8,64,2048]{2,1,0:T(8,128)(2,1)}), bf16[8,64,2048]{2,1,0:T(8,128)(2,1)S(1)}, u32[]{:S(2)}, u32[]{:S(2)}) async-start(bf16[8,64,2048]{2,1,0:T(8,128)(2,1)} %bitcast.455), calls=%async_computation.2 | async-start | bytes 4194304 | tf_op jit(solution)/shard_map/all_to_all | solution.py:425
  234.7 34.6 %collective-permute-start.22 = (bf16[256,4224]{1,0:T(8,128)(2,1)}, bf16[256,4224]{1,0:T(8,128)(2,1)}, u32[]{:S(2)}, u32[]{:S(2)}) collective-permute-start(bf16[256,4224]{1,0:T(8,128)(2,1)} %pad_maximum_fusion.5), channel_id=1, source_target_pairs={{1,0},{0,1},{3,2},{2,3},{5,4},{4,5},{7,6},{6,7},{9,8},{8,9},{11,10... | collective-permute-start | bytes 6488072 | tf_op jit(solution)/shard_map/ppermute | solution.py:37
  238.6 478.2 %collective-permute-start.20 = (f32[128,2048]{1,0:T(8,128)}, f32[128,2048]{1,0:T(8,128)}, u32[]{:S(2)}, u32[]{:S(2)}) collective-permute-start(f32[128,2048]{1,0:T(8,128)} %slice.611), channel_id=1, source_target_pairs={{0,1},{1,0},{2,3},{3,2},{4,5},{5,4},{6,7},{7,6},{8,9},{9,8},{10,11... | collective-permute-start | bytes 3145736 | tf_op jit(solution)/shard_map/ppermute | solution.py:42
  238.9 44.4 %all-to-all-start.1 = ((bf16[8,64,2048]{2,1,0:T(8,128)(2,1)}), bf16[8,64,2048]{2,1,0:T(8,128)(2,1)}, u32[]{:S(2)}, u32[]{:S(2)}) async-start(bf16[8,64,2048]{2,1,0:T(8,128)(2,1)} %bitcast.454), calls=%async_computation.1 | async-start | bytes 4194304 | tf_op jit(solution)/shard_map/all_to_all | solution.py:425
  273.4 37.2 %collective-permute-start.46 = (bf16[128,3840]{1,0:T(8,128)(2,1)}, bf16[128,3840]{1,0:T(8,128)(2,1)}, u32[]{:S(2)}, u32[]{:S(2)}) collective-permute-start(bf16[128,3840]{1,0:T(8,128)(2,1)} %pad_maximum_fusion.15), channel_id=1, source_target_pairs={{0,4},{2,6},{4,0},{6,2},{8,12},{10,14},{12,8},{14,10},{16,20},{18,... | collective-permute-start | bytes 2949128 | tf_op jit(solution)/shard_map/ppermute | solution.py:137
  279.1 69.8 %collective-permute-start.45 = (bf16[128,6656]{1,0:T(8,128)(2,1)}, bf16[128,6656]{1,0:T(8,128)(2,1)}, u32[]{:S(2)}, u32[]{:S(2)}) collective-permute-start(bf16[128,6656]{1,0:T(8,128)(2,1)} %pad_maximum_fusion.7), channel_id=1, source_target_pairs={{0,2},{2,0},{4,6},{6,4},{8,10},{10,8},{12,14},{14,12},{16,18},{18,... | collective-permute-start | bytes 5111816 | tf_op jit(solution)/shard_map/ppermute | solution.py:137
  283.2 57.2 %all-to-all-start.3 = ((bf16[8,64,2048]{2,1,0:T(8,128)(2,1)}), bf16[8,64,2048]{2,1,0:T(8,128)(2,1)S(1)}, u32[]{:S(2)}, u32[]{:S(2)}) async-start(bf16[8,64,2048]{2,1,0:T(8,128)(2,1)} %bitcast.492), calls=%async_computation.3 | async-start | bytes 4194304 | tf_op jit(solution)/shard_map/all_to_all | solution.py:425
  348.5 54.5 %collective-permute-start.23 = (f32[128,1024]{1,0:T(8,128)}, f32[128,1024]{1,0:T(8,128)}, u32[]{:S(2)}, u32[]{:S(2)}) collective-permute-start(f32[128,1024]{1,0:T(8,128)} %get-tuple-element.252), channel_id=1, source_target_pairs={{1,0},{0,1},{3,2},{2,3},{5,4},{4,5},{7,6},{6,7},{9,8},{8,9},{11,10... | collective-permute-start | bytes 1572872 | tf_op jit(solution)/shard_map/ppermute | solution.py:112
  351.6 37.5 %all-to-all-start.4 = ((bf16[8,64,2048]{2,1,0:T(8,128)(2,1)}), bf16[8,64,2048]{2,1,0:T(8,128)(2,1)}, u32[]{:S(2)}, u32[]{:S(2)}) async-start(bf16[8,64,2048]{2,1,0:T(8,128)(2,1)} %bitcast.490), calls=%async_computation.4 | async-start | bytes 4194304 | tf_op jit(solution)/shard_map/all_to_all | solution.py:425
  356.0 167.2 %reduce-scatter.5.cloned.1.call-start = ((), (), s32[]{:S(2)}) async-start(), calls=%async_computation.9 | async-start | bytes 3244032 | tf_op jit(solution)/shard_map/reduce_scatter | solution.py:488
  356.0 36.8 %collective-permute-start.72 = (bf16[256,6656]{1,0:T(8,128)(2,1)S(1)}, bf16[256,6656]{1,0:T(8,128)(2,1)}, u32[]{:S(2)}, u32[]{:S(2)}) collective-permute-start(bf16[256,6656]{1,0:T(8,128)(2,1)S(1)} %pad_maximum_fusion.3), channel_id=1, source_target_pairs={{1,0},{0,1},{3,2},{2,3},{5,4},{4,5},{7,6},{6,7},{9,8},{8,9},{11,10... | collective-permute-start | bytes 10223624 | tf_op jit(solution)/shard_map/ppermute | solution.py:37
  371.3 458.4 %reduce-scatter.3.cloned.1.call-start = ((), (), s32[]{:S(2)}) async-start(), calls=%async_computation.8 | async-start | bytes 6488064 | tf_op jit(solution)/shard_map/reduce_scatter | solution.py:488
  392.0 35.7 %collective-permute-start.25 = (bf16[128,2048]{1,0:T(8,128)(2,1)}, bf16[128,2048]{1,0:T(8,128)(2,1)}, u32[]{:S(2)}, u32[]{:S(2)}) collective-permute-start(bf16[128,2048]{1,0:T(8,128)(2,1)} %fusion.75), channel_id=1, source_target_pairs={{0,16},{2,18},{4,20},{6,22},{8,24},{10,26},{12,28},{14,30},{16,0},... | collective-permute-start | bytes 1572872 | tf_op jit(solution)/shard_map/ppermute | solution.py:137
  438.7 88.5 %all-to-all-start.5 = ((bf16[8,128,2048]{2,1,0:T(8,128)(2,1)}), bf16[8,128,2048]{2,1,0:T(8,128)(2,1)}, u32[]{:S(2)}, u32[]{:S(2)}) async-start(bf16[8,128,2048]{2,1,0:T(8,128)(2,1)} %pad_maximum_fusion.1), calls=%async_computation.5 | async-start | bytes 8388608 | tf_op jit(solution)/shard_map/all_to_all | solution.py:425
  454.2 62.7 %collective-permute-start.47 = (bf16[128,3072]{0,1:T(8,128)(2,1)}, bf16[128,3072]{0,1:T(8,128)(2,1)}, u32[]{:S(2)}, u32[]{:S(2)}) collective-permute-start(bf16[128,3072]{0,1:T(8,128)(2,1)} %pad_maximum_fusion.17), channel_id=1, source_target_pairs={{0,4},{2,6},{4,0},{6,2},{8,12},{10,14},{12,8},{14,10},{16,20},{18,... | collective-permute-start | bytes 2359304 | tf_op jit(solution)/shard_map/ppermute | solution.py:137
  490.1 29.2 %collective-permute-start.50 = (bf16[16,1,128,512]{3,2,0,1:T(8,128)(2,1)}, bf16[16,1,128,512]{3,2,0,1:T(8,128)(2,1)}, u32[]{:S(2)}, u32[]{:S(2)}) collective-permute-start(bf16[16,1,128,512]{3,2,0,1:T(8,128)(2,1)} %broadcast_select_fusion), channel_id=1, source_target_pairs={{0,1},{1,0},{2,3},{3,2},{4,5},{5,4},{6,7},{7,6},{8,9},{9,8},{10,11... | collective-permute-start | bytes 6291464 | tf_op jit(solution)/shard_map/ppermute | solution.py:42
  506.3 181.1 %collective-permute-start.29 = (bf16[128,3072]{0,1:T(8,128)(2,1)S(1)}, bf16[128,3072]{0,1:T(8,128)(2,1)}, u32[]{:S(2)}, u32[]{:S(2)}) collective-permute-start(bf16[128,3072]{0,1:T(8,128)(2,1)S(1)} %bitcast.460), channel_id=1, source_target_pairs={{1,0},{0,1},{3,2},{2,3},{5,4},{4,5},{7,6},{6,7},{9,8},{8,9},{11,10... | collective-permute-start | bytes 2359304 | tf_op jit(solution)/shard_map/ppermute | solution.py:37
  580.9 39.6 %collective-permute-start.30 = (bf16[512,576]{0,1:T(8,128)(2,1)}, bf16[512,576]{0,1:T(8,128)(2,1)}, u32[]{:S(2)}, u32[]{:S(2)}) collective-permute-start(bf16[512,576]{0,1:T(8,128)(2,1)} %get-tuple-element.233), channel_id=1, source_target_pairs={{0,2},{2,0},{4,6},{6,4},{8,10},{10,8},{12,14},{14,12},{16,18},{18,... | collective-permute-start | bytes 1769480 | tf_op jit(solution)/shard_map/ppermute | solution.py:137
  597.8 22.8 %collective-permute-start.34 = (bf16[512,576]{0,1:T(8,128)(2,1)}, bf16[512,576]{0,1:T(8,128)(2,1)}, u32[]{:S(2)}, u32[]{:S(2)}) collective-permute-start(bf16[512,576]{0,1:T(8,128)(2,1)} %get-tuple-element.234), channel_id=1, source_target_pairs={{0,4},{2,6},{4,0},{6,2},{8,12},{10,14},{12,8},{14,10},{16,20},{18,... | collective-permute-start | bytes 1769480 | tf_op jit(solution)/shard_map/ppermute | solution.py:137
  599.0 25.5 %collective-permute-start.48 = (bf16[128,2560]{0,1:T(8,128)(2,1)}, bf16[128,2560]{0,1:T(8,128)(2,1)}, u32[]{:S(2)}, u32[]{:S(2)}) collective-permute-start(bf16[128,2560]{0,1:T(8,128)(2,1)} %pad_maximum_fusion.22), channel_id=1, source_target_pairs={{0,2},{2,0},{4,6},{6,4},{8,10},{10,8},{12,14},{14,12},{16,18},{18,... | collective-permute-start | bytes 1966088 | tf_op jit(solution)/shard_map/ppermute | solution.py:137
  620.5 78.8 %collective-permute-start.68 = (bf16[256,3072]{0,1:T(8,128)(2,1)}, bf16[256,3072]{0,1:T(8,128)(2,1)}, u32[]{:S(2)}, u32[]{:S(2)}) collective-permute-start(bf16[256,3072]{0,1:T(8,128)(2,1)} %pad_maximum_fusion.10), channel_id=1, source_target_pairs={{1,0},{0,1},{3,2},{2,3},{5,4},{4,5},{7,6},{6,7},{9,8},{8,9},{11,10... | collective-permute-start | bytes 4718600 | tf_op jit(solution)/shard_map/ppermute | solution.py:37
  624.5 19.5 %collective-permute-start.31 = (bf16[256,576]{0,1:T(8,128)(2,1)S(1)}, bf16[256,576]{0,1:T(8,128)(2,1)S(1)}, u32[]{:S(2)}, u32[]{:S(2)}) collective-permute-start(bf16[256,576]{0,1:T(8,128)(2,1)S(1)} %slice.910), channel_id=1, source_target_pairs={{0,4},{2,6},{4,0},{6,2},{8,12},{10,14},{12,8},{14,10},{16,20},{18,... | collective-permute-start | bytes 884744 | tf_op jit(solution)/shard_map/ppermute | solution.py:137
  644.0 173.1 %collective-permute-start.76 = (bf16[704,2048]{1,0:T(8,128)(2,1)}, bf16[704,2048]{1,0:T(8,128)(2,1)}, u32[]{:S(2)}, u32[]{:S(2)}) collective-permute-start(bf16[704,2048]{1,0:T(8,128)(2,1)} %dynamic-slice_convert_fusion), channel_id=1, source_target_pairs={{0,1},{1,0},{2,3},{3,2},{4,5},{5,4},{6,7},{7,6},{8,9},{9,8},{10,11... | collective-permute-start | bytes 8650760 | tf_op jit(solution)/shard_map/ppermute | solution.py:42
  684.9 112.3 %collective-permute-start.75 = (bf16[1024,1408]{1,0:T(8,128)(2,1)}, bf16[1024,1408]{1,0:T(8,128)(2,1)}, u32[]{:S(2)}, u32[]{:S(2)}) collective-permute-start(bf16[1024,1408]{1,0:T(8,128)(2,1)} %dynamic-slice_convert_fusion.1), channel_id=1, source_target_pairs={{0,1},{1,0},{2,3},{3,2},{4,5},{5,4},{6,7},{7,6},{8,9},{9,8},{10,11... | collective-permute-start | bytes 8650760 | tf_op jit(solution)/shard_map/ppermute | solution.py:42
  699.3 25.6 %collective-permute-start.28 = (bf16[128,2048]{1,0:T(8,128)(2,1)}, bf16[128,2048]{1,0:T(8,128)(2,1)}, u32[]{:S(2)}, u32[]{:S(2)}) collective-permute-start(bf16[128,2048]{1,0:T(8,128)(2,1)} %fusion.74), channel_id=1, source_target_pairs={{0,16},{2,18},{4,20},{6,22},{8,24},{10,26},{12,28},{14,30},{16,0},... | collective-permute-start | bytes 1572872 | tf_op jit(solution)/shard_map/ppermute | solution.py:137
  716.8 30.5 %collective-permute-start.51 = (bf16[256,2560]{0,1:T(8,128)(2,1)}, bf16[256,2560]{0,1:T(8,128)(2,1)}, u32[]{:S(2)}, u32[]{:S(2)}) collective-permute-start(bf16[256,2560]{0,1:T(8,128)(2,1)} %pad_maximum_fusion.12), channel_id=1, source_target_pairs={{1,0},{0,1},{3,2},{2,3},{5,4},{4,5},{7,6},{6,7},{9,8},{8,9},{11,10... | collective-permute-start | bytes 3932168 | tf_op jit(solution)/shard_map/ppermute | solution.py:37
  716.9 25.6 %collective-permute-start.64 = (bf16[8,1,128,512]{3,2,0,1:T(8,128)(2,1)S(1)}, bf16[8,1,128,512]{3,2,0,1:T(8,128)(2,1)S(1)}, u32[]{:S(2)}, u32[]{:S(2)}) collective-permute-start(bf16[8,1,128,512]{3,2,0,1:T(8,128)(2,1)S(1)} %copy-done.86), channel_id=1, source_target_pairs={{0,2},{2,0},{4,6},{6,4},{8,10},{10,8},{12,14},{14,12},{16,18},{18,... | collective-permute-start | bytes 3145736 | tf_op jit(solution)/shard_map/ppermute | solution.py:137
  742.5 62.3 %collective-permute-start.74 = (bf16[1024,1408]{1,0:T(8,128)(2,1)}, bf16[1024,1408]{1,0:T(8,128)(2,1)}, u32[]{:S(2)}, u32[]{:S(2)}) collective-permute-start(bf16[1024,1408]{1,0:T(8,128)(2,1)} %dynamic-slice_convert_fusion.2), channel_id=1, source_target_pairs={{0,1},{1,0},{2,3},{3,2},{4,5},{5,4},{6,7},{7,6},{8,9},{9,8},{10,11... | collective-permute-start | bytes 8650760 | tf_op jit(solution)/shard_map/ppermute | solution.py:42
  747.3 25.3 %collective-permute-start.69 = (bf16[4,1,64,2048]{3,2,0,1:T(8,128)(2,1)}, bf16[4,1,64,2048]{3,2,0,1:T(8,128)(2,1)S(1)}, u32[]{:S(2)}, u32[]{:S(2)}) collective-permute-start(bf16[4,1,64,2048]{3,2,0,1:T(8,128)(2,1)} %dynamic-slice_bitcast_fusion), channel_id=1, source_target_pairs={{0,2},{2,0},{4,6},{6,4},{8,10},{10,8},{12,14},{14,12},{16,18},{18,... | collective-permute-start | bytes 3145736 | tf_op jit(solution)/shard_map/ppermute | solution.py:137
  751.6 31.2 %collective-permute-start.65 = (bf16[4,1,128,512]{3,2,0,1:T(8,128)(2,1)S(1)}, bf16[4,1,128,512]{3,2,0,1:T(8,128)(2,1)S(1)}, u32[]{:S(2)}, u32[]{:S(2)}) collective-permute-start(bf16[4,1,128,512]{3,2,0,1:T(8,128)(2,1)S(1)} %copy-done.101), channel_id=1, source_target_pairs={{0,4},{2,6},{4,0},{6,2},{8,12},{10,14},{12,8},{14,10},{16,20},{18,... | collective-permute-start | bytes 1572872 | tf_op jit(solution)/shard_map/ppermute | solution.py:137
  781.5 43.2 %collective-permute-start.52 = (bf16[4,1,96,1024]{3,2,0,1:T(8,128)(2,1)}, bf16[4,1,96,1024]{3,2,0,1:T(8,128)(2,1)}, u32[]{:S(2)}, u32[]{:S(2)}) collective-permute-start(bf16[4,1,96,1024]{3,2,0,1:T(8,128)(2,1)} %dynamic-slice_bitcast_fusion.3), channel_id=1, source_target_pairs={{0,4},{2,6},{4,0},{6,2},{8,12},{10,14},{12,8},{14,10},{16,20},{18,... | collective-permute-start | bytes 2359304 | tf_op jit(solution)/shard_map/ppermute | solution.py:137
  793.8 33.4 %collective-permute-start.56 = (bf16[4,1,96,1024]{3,2,0,1:T(8,128)(2,1)}, bf16[4,1,96,1024]{3,2,0,1:T(8,128)(2,1)S(1)}, u32[]{:S(2)}, u32[]{:S(2)}) collective-permute-start(bf16[4,1,96,1024]{3,2,0,1:T(8,128)(2,1)} %dynamic-slice_bitcast_fusion.2), channel_id=1, source_target_pairs={{0,2},{2,0},{4,6},{6,4},{8,10},{10,8},{12,14},{14,12},{16,18},{18,... | collective-permute-start | bytes 2359304 | tf_op jit(solution)/shard_map/ppermute | solution.py:137
  797.2 26.5 %collective-permute-start.70 = (bf16[2,1,64,2048]{3,2,0,1:T(8,128)(2,1)S(1)}, bf16[2,1,64,2048]{3,2,0,1:T(8,128)(2,1)S(1)}, u32[]{:S(2)}, u32[]{:S(2)}) collective-permute-start(bf16[2,1,64,2048]{3,2,0,1:T(8,128)(2,1)S(1)} %dynamic-slice_bitcast_fusion.4), channel_id=1, source_target_pairs={{0,8},{2,10},{4,12},{6,14},{8,0},{10,2},{12,4},{14,6},{16,24},{18,... | collective-permute-start | bytes 1572872 | tf_op jit(solution)/shard_map/ppermute | solution.py:137
  827.6 20.2 %collective-permute-start.57 = (bf16[2,1,96,1024]{3,2,1,0:T(8,128)(2,1)S(1)}, bf16[2,1,96,1024]{3,2,1,0:T(8,128)(2,1)S(1)}, u32[]{:S(2)}, u32[]{:S(2)}) collective-permute-start(bf16[2,1,96,1024]{3,2,1,0:T(8,128)(2,1)S(1)} %dynamic-slice_bitcast_fusion.6), channel_id=1, source_target_pairs={{0,8},{2,10},{4,12},{6,14},{8,0},{10,2},{12,4},{14,6},{16,24},{18,... | collective-permute-start | bytes 1179656 | tf_op jit(solution)/shard_map/ppermute | solution.py:137
  (239 other events, 2830.9 us)
Sparse Core Ops, SparseCore 0:
  9.7 18.6 all-gather.6
  29.9 17.1 all-gather.10
  151.5 17.3 all-gather.8
  371.4 107.7 reduce-scatter.4
  482.7 127.0 reduce-scatter.2

commit v3 on v2

--- a/solution.py
+++ b/solution.py
@@ -4,6 +4,7 @@
 import jax
 import jax.numpy as jnp
 from jax import lax
+from jax.experimental.layout import Layout, with_layout_constraint
 from jax.sharding import PartitionSpec as P
 
 D = 2048
@@ -265,7 +266,7 @@
     return out, top + jnp.log(total), heads.reshape(heads.shape[0], H * DV).astype(BF)
 
 
-def attend_back(query, keys, seen, up_key, up_value, out, log_total, grad_heads, cos, sin, beside):
+def attend_back(query, keys, seen, up_key, up_value, out, log_total, grad_heads, cos, sin):
     rows = query.shape[1]
     scores = jnp.einsum("htr,kr->htk", query, keys, preferred_element_type=F32) * SCALE
     probs = jnp.exp(jnp.where(seen, scores, MASKED) - log_total)
@@ -278,14 +279,13 @@
     grad_query = jnp.einsum("htk,kr->htr", grad_scores, keys, preferred_element_type=F32)
     grad_keys = jnp.einsum("htk,htr->kr", grad_scores, query, preferred_element_type=F32)
     values_part = jnp.einsum("htk,htr->kr", probs.astype(BF), grad_out, preferred_element_type=F32)
-    values_part, beside = lax.optimization_barrier((values_part, beside))
     grad_keys = grad_keys + jnp.pad(values_part, ((0, 0), (0, DR)))
     grad_latent = grad_query[:, :, :R].astype(BF)
     nope = jnp.einsum("htr,rhd->thd", grad_latent, up_key, preferred_element_type=F32)
     first, second = grad_query[:, :, R : R + DR // 2], grad_query[:, :, R + DR // 2 :]
     rotary = jnp.concatenate([first * cos + second * sin, second * cos - first * sin], axis=2)
     grad_q = jnp.concatenate([nope, rotary.transpose(1, 0, 2)], axis=2).reshape(rows, H * DQ)
-    return grad_q.astype(BF), grad_latent, grad_keys, beside
+    return grad_q.astype(BF), grad_latent, grad_keys
 
 
 def rms_norm(values, gain):
@@ -362,6 +362,7 @@
     half_ctx = n_ctx // 2
     capacity = min(rows, 4 * rows * TOP // (3 * n_ctx))
     after = Order()
+    partner = functools.partial(ctx_swap, mask=half_ctx)
     order_a, order_b = spread_orders()
     reduce_a, reduce_b = order_a[::-1], order_b[::-1]
 
@@ -401,23 +402,27 @@
         [latent, (first * cos - second * sin).astype(BF), (first * sin + second * cos).astype(BF)],
         axis=1,
     )
-    keys_a = ctx_spread(own_keys[:block], order_a)
-    keys_b = ctx_spread(own_keys[block:], order_b)
+    keys_a = ctx_spread(own_keys[:block], order_a[:1])
+    keys_b = ctx_spread(own_keys[block:], order_b[:1])
+    cot_other = partner(after(cot, keys_a, keys_b))
+    tables = partner(after(jnp.concatenate([routes[0].astype(F32), gate_weights[0]], axis=1), own_keys))
+    keys_a = ctx_spread(keys_a, order_a[1:])
+    keys_b = ctx_spread(keys_b, order_b[1:])
     tok_all = wt_rows(after(tok, own_keys))
     cot_all = wt_rows(after(cot, own_keys))
-    kv_up = wt_gather(after(w_kv_up, own_keys), 0)
-    one_part = my_part(rms_norm(tok_all.astype(F32), gain_one).astype(BF), 1)
+    kv_up = with_layout_constraint(wt_gather(after(w_kv_up, own_keys), 0), Layout((0, 1)))
+    one_all = rms_norm(tok_all.astype(F32), gain_one).astype(BF)
+    one_part = my_part(one_all, 1)
     query = wt_sum_rows(contract(one_part, w_query, 1, 0), BF)
     up3 = kv_up.reshape(R, H, DN + DV)
     up_key, up_value = up3[:, :, :DN], up3[:, :, DN:]
     query_nope, query_cat = query_parts(query, cos, sin, up_key)
 
-    partner = functools.partial(ctx_swap, mask=half_ctx)
     route_own = routes[0]
     gate_own = gate_weights[0]
     place_own, high_own, low_own = route_matrices(route_own, gate_own, capacity)
     place_other, high_other, low_other = route_matrices(
-        partner(route_own.astype(F32)).astype(jnp.int32), partner(gate_own), capacity
+        tables[:, :TOP].astype(jnp.int32), tables[:, TOP:], capacity
     )
     groups = [list(range(half_ctx)), list(range(half_ctx, n_ctx))]
 
@@ -427,7 +432,6 @@
     def slots(x):
         return x.astype(BF).reshape(half_ctx, capacity, D)
 
-    cot_other = partner(cot)
     rows_grad = jnp.concatenate(
         [
             slots(contract(high_own, cot, 1, 0) + contract(low_own, cot, 1, 0)),
@@ -453,39 +457,7 @@
 
     two_all = wt_rows(normed_two)
     two_part = my_part(two_all, 1)
-    shared_gate, shared_up = wt_sum_parts(
-        [contract(two_part, w_shared_gate, 1, 0), contract(two_part, w_shared_up, 1, 0)]
-    )
-    act, slope = silu_parts(shared_gate)
-    hidden = (act * shared_up).astype(BF)
-    shared_out = wt_sum_rows(contract(hidden, w_shared_down, 1, 0))
-    grad_hidden = contract(cot_all, w_shared_down, 1, 1)
-    grad_gate, grad_up, hidden_all = wt_all_columns(
-        [(grad_hidden * shared_up * slope).astype(BF), (grad_hidden * act).astype(BF), hidden]
-    )
-    shared_back = wt_own_rows(
-        contract(grad_gate, w_shared_gate, 1, 1) + contract(grad_up, w_shared_up, 1, 1)
-    )
-
-    def pair_send(chunked, other, bit, *others):
-        mine = (c // bit) % 2
-        view = chunked.reshape(rows, half_ctx // bit, 2, -1)
-        keep = jnp.where(mine == 0, view[:, :, 0], view[:, :, 1]).reshape(rows, -1)
-        sent = jnp.where(mine == 0, view[:, :, 1], view[:, :, 0]).reshape(rows, -1)
-        got = ctx_swap(after(jnp.concatenate([sent, other], axis=1), *others), bit)
-        return jnp.concatenate([jnp.concatenate([keep, other], axis=1), got], axis=0), keep.shape[1]
-
-    def pair_grad(sent, *others):
-        both, wide = sent
-        both = wt_rows(after(both, *others))
-        columns, partners = both[:, :wide], both[:, wide:]
-        columns = my_part(columns.reshape(-1, half_ctx, n_wt, wide // (half_ctx * n_wt)), 2).reshape(-1, wide // n_wt)
-        grad = contract(columns, partners, 0, 0).astype(BF)
-        return grad.reshape(half_ctx, -1, partners.shape[1])
-
-    def scatter_sum(x, bit):
-        sides = [[i for i in range(n_ctx) if i // bit % 2 == side] for side in range(2)]
-        return lax.psum_scatter(x, "ctx", scatter_dimension=0, axis_index_groups=sides, tiled=True)[0].astype(F32)
+    shared_terms = [contract(two_part, w, 1, 0) for w in (w_shared_gate, w_shared_up)]
 
     gate_matrix = lax.all_gather(w_expert_gate[0], "wt", axis=0, tiled=True)
     up_matrix = lax.all_gather(w_expert_up[0], "wt", axis=0, tiled=True)
@@ -502,18 +474,49 @@
         return (gate_act * up).astype(BF), grad_gate_pre, grad_up_pre, slots(grad_in)
 
     hidden_1, grad_gate_1, grad_up_1, grad_in_1 = expert(rows_own, grad_own)
+    hidden_2, grad_gate_2, grad_up_2, grad_in_2 = expert(after(rows_other, grad_in_1), grad_other)
     back_own = swap_blocks(grad_in_1).reshape(-1, D)
-    hidden_2, grad_gate_2, grad_up_2, grad_in_2 = expert(after(rows_other, grad_in_1), grad_other)
-    sent_gate_up = pair_send(
-        normed_two, jnp.concatenate([grad_gate[:rows], grad_up[:rows]], axis=1), reduce_a[0], grad_in_1
-    )
-    sent_down = pair_send(cot, hidden_all[:rows], reduce_b[0], grad_in_1)
     grad_in_2, back_own = lax.optimization_barrier((grad_in_2, back_own))
     back_other = swap_blocks(grad_in_2).reshape(-1, D)
-    grads_gate_up = pair_grad(sent_gate_up, grad_in_2)
-    grads_down = pair_grad(sent_down, grad_in_2)
-    sums_gate_up = scatter_sum(grads_gate_up, reduce_a[0])
-    sums_down = scatter_sum(grads_down, reduce_b[0])
+
+    shared_gate, shared_up = wt_sum_parts([after(x, grad_in_2) for x in shared_terms])
+    act, slope = silu_parts(shared_gate)
+    hidden = (act * shared_up).astype(BF)
+    shared_out = wt_sum_rows(contract(hidden, w_shared_down, 1, 0))
+    grad_hidden = contract(cot_all, w_shared_down, 1, 1)
+    grad_gate, grad_up, hidden_all = wt_all_columns(
+        [(grad_hidden * shared_up * slope).astype(BF), (grad_hidden * act).astype(BF), hidden]
+    )
+    shared_back = wt_own_rows(
+        contract(grad_gate, w_shared_gate, 1, 1) + contract(grad_up, w_shared_up, 1, 1)
+    )
+
+    def pair_send(chunked, other, bit, *others):
+        mine = (c // bit) % 2
+        view = chunked.reshape(rows, half_ctx // bit, 2, -1)
+        low, high = view[:, :, 0].reshape(rows, -1), view[:, :, 1].reshape(rows, -1)
+        keep = jnp.where(mine == 0, low, high)
+        sent = jnp.where(mine == 0, high, low)
+        got = ctx_swap(after(jnp.concatenate([sent] + other, axis=1), *others), bit)
+        return jnp.concatenate([jnp.concatenate([keep] + other, axis=1), got], axis=0)
+
+    def pair_grad(both, deep, *others):
+        both = wt_rows(after(both, *others))
+        wide = both.shape[1] - deep
+        columns, partners = both[:, :wide], both[:, wide:]
+        columns = my_part(columns.reshape(-1, half_ctx, n_wt, wide // (half_ctx * n_wt)), 2).reshape(-1, wide // n_wt)
+        grad = contract(columns, partners, 0, 0).astype(BF)
+        return grad.reshape(half_ctx, -1, deep)
+
+    def scatter_sum(x, bit):
+        sides = [[i for i in range(n_ctx) if i // bit % 2 == side] for side in range(2)]
+        return lax.psum_scatter(x, "ctx", scatter_dimension=0, axis_index_groups=sides, tiled=True)[0].astype(F32)
+
+    hidden_wide = grad_gate.shape[1]
+    sent_gate_up = pair_send(normed_two, [grad_gate[:rows], grad_up[:rows]], reduce_a[0], back_other)
+    sent_down = pair_send(cot, [hidden_all[:rows]], reduce_b[0], back_other)
+    sums_down = scatter_sum(pair_grad(sent_down, hidden_wide), reduce_b[0])
+    sums_gate_up = scatter_sum(pair_grad(sent_gate_up, 2 * hidden_wide), reduce_a[0])
     produced = jnp.concatenate(
         [slots(contract(after(x, grad_in_2), down_matrix, 1, 0)) for x in (hidden_1, hidden_2)], axis=1
     )
@@ -534,22 +537,29 @@
     grad_attn_own = grad_residual.astype(BF)
     grad_attn = wt_rows(grad_attn_own)
     grad_heads = wt_own_rows(contract(grad_attn, w_out, 1, 1).astype(BF))
-    sent_out = pair_send(grad_attn_own, heads_out, reduce_b[0], grad_heads)
+    sent_out = pair_send(grad_attn_own, [heads_out], reduce_b[0], grad_heads)
 
     out_rows = swap_blocks(after(produced, grad_routed))
 
-    grad_query, grad_query_latent, grad_keys, out_rows = attend_back(
-        query_cat, keys, seen, up_key, up_value, out_latent, log_total, grad_heads, cos, sin, out_rows
-    )
+    grad_query, grad_query_latent, grad_keys = attend_back(
+        query_cat, keys, seen, up_key, up_value, out_latent, log_total, grad_heads, cos, sin
+    )
+    grad_keys = after(grad_keys, out_rows)
     out_own, out_other = out_rows[:, :capacity].reshape(-1, D), out_rows[:, capacity:].reshape(-1, D)
     grad_keys_a, grad_keys_b = jnp.split(grad_keys, 2, axis=0)
+    first_a, first_b = (ctx_unspread(x, o[-1:]) for x, o in ((grad_keys_a, order_a), (grad_keys_b, order_b)))
+    steps = [lax.optimization_barrier((first_a, first_b))]
+    for number in range(2, len(order_a) + 1):
+        step = tuple(
+            ctx_unspread(x, order[-number : 1 - number])
+            for x, order in zip(steps[-1], (order_a, order_b))
+        )
+        steps.append(lax.optimization_barrier(step))
     sent_query = [
-        pair_send(grad_query, one_own[:, part * (D // 2) : (part + 1) * (D // 2)], order[0], grad_keys_a)
+        pair_send(grad_query, [one_own[:, part * (D // 2) : (part + 1) * (D // 2)]], order[0], *steps[1])
         for part, order in ((0, reduce_a), (1, reduce_b))
     ]
-    grad_keys = jnp.concatenate(
-        [ctx_unspread(grad_keys_a, order_a), ctx_unspread(grad_keys_b, order_b)], axis=0
-    )
+    grad_keys = jnp.concatenate(steps[-1], axis=0)
     routed = (
         contract(high_own, out_own, 0, 0)
         + contract(low_own, out_own, 0, 0)
@@ -558,21 +568,29 @@
         ).astype(F32)
     )
     mixed_out = (residual + shared_out + routed).astype(BF)
-    rows_own, rows_other, grad_own, grad_other = (
-        after(x, grad_keys_a) for x in (rows_own, rows_other, grad_own, grad_other)
-    )
-    rows_in = jnp.concatenate([rows_own, rows_other], axis=0)
-    expert_hidden = jnp.concatenate([hidden_1, hidden_2], axis=0)
-    rows_grad = jnp.concatenate([grad_own, grad_other], axis=0)
-    grad_w_expert_gate = expert_sum(contract(rows_in, jnp.concatenate([grad_gate_1, grad_gate_2], axis=0), 0, 0))
-    grad_w_expert_up = expert_sum(contract(rows_in, jnp.concatenate([grad_up_1, grad_up_2], axis=0), 0, 0))
-    grad_w_expert_down = expert_sum(contract(expert_hidden, rows_grad, 0, 0))
+    def expert_sum(former, latter):
+        former = after(jnp.concatenate(former, axis=0), grad_keys)
+        latter = jnp.concatenate(latter, axis=0)
+        w = lax.axis_index("wt")
+        sums = [
+            wt_to(contract(part_of(former, (w + way) % n_wt, 1), latter, 0, 0).astype(BF), way)
+            for way in range(1, n_wt)
+        ]
+        total = contract(after(my_part(former, 1), *sums), latter, 0, 0)
+        for got in sums:
+            total = total + got.astype(F32)
+        return total[None]
+
+    rows_in = rows_own, rows_other
+    grad_w_expert_gate = expert_sum(rows_in, (grad_gate_1, grad_gate_2))
+    grad_w_expert_up = expert_sum(rows_in, (grad_up_1, grad_up_2))
+    grad_w_expert_down = expert_sum((hidden_1, hidden_2), (grad_own, grad_other))
 
     grad_up_key = jnp.einsum(
-        "thd,htr->hdr", query_nope, grad_query_latent, preferred_element_type=F32
+        "thd,htr->hdr", query_nope, after(grad_query_latent, grad_keys), preferred_element_type=F32
     )
     grad_up_value = jnp.einsum(
-        "thv,htr->hvr", grad_heads.reshape(rows, H, DV), out_latent.astype(BF), preferred_element_type=F32
+        "thv,htr->hvr", after(grad_heads, grad_keys).reshape(rows, H, DV), out_latent.astype(BF), preferred_element_type=F32
     )
     up_grads = jnp.concatenate([grad_up_key, grad_up_value], axis=1).astype(BF)
     up_grads = up_grads.reshape(n_ctx, n_wt, -1, R)
@@ -583,9 +601,9 @@
     sum_kv_up = Reduction(own_up.astype(BF).reshape(n_ctx, -1, R), reduce_a, after)
 
     query_all = wt_rows(grad_query)
-    sum_out = Reduction(pair_grad(sent_out, grad_keys_a), reduce_b[1:], after).send()
+    sums_out = scatter_sum(pair_grad(sent_out, heads_out.shape[1], grad_keys), reduce_b[0])
     sums_query = [
-        Reduction(pair_grad(sent, grad_keys), order[1:], after).send()
+        Reduction(pair_grad(sent, D // 2, grad_keys), order[1:], after).send()
         for sent, order in zip(sent_query, (reduce_a, reduce_b))
     ]
     sum_kv_up.send(grad_keys)
@@ -597,7 +615,9 @@
         [grad_latent, first * cos + second * sin, second * cos - first * sin], axis=1
     ).astype(BF)
     grad_kv_all = wt_rows(grad_kv)
-    sum_kv_down = Reduction(pair_grad(pair_send(one_own, grad_kv, reduce_b[0], grad_kv)), reduce_b[1:], after)
+    one_columns = my_part(one_all.reshape(-1, n_ctx, n_wt, D // (n_ctx * n_wt)), 2).reshape(-1, D // n_wt)
+    kv_down_terms = contract(one_columns, grad_kv_all, 0, 0).astype(BF).reshape(n_ctx, -1, KW)
+    kv_down_terms = lax.all_to_all(kv_down_terms, "ctx", 0, 0, tiled=True)
     grad_one = wt_own_rows(one_back + contract(grad_kv_all, w_kv_down, 1, 1))
     grad_inputs, grad_gain_attn = rms_back(inputs, gain_one, grad_one)
     grad_tokens = grad_residual + grad_inputs
@@ -609,18 +629,15 @@
         ],
         axis=2,
     )
-    own_gain = my_part(gain_grads, 1)
-    for step in range(1, n_wt):
-        w = lax.axis_index("wt")
-        own_gain = own_gain + wt_to(part_of(gain_grads, (w + step) % n_wt, 1), step)
-    gain_total = after.seal(ctx_reduce(own_gain.reshape(n_ctx, 1, -1), reduce_b, F32)[0])
+    gain_grads = lax.all_to_all(gain_grads.reshape(n_ctx * n_wt, -1), ("ctx", "wt"), 0, 0, tiled=True)
+    gain_total = after.seal(jnp.sum(gain_grads, axis=0))
     wide = D // (n_ctx * n_wt)
-    grad_w_kv_down = sum_kv_down.result()
+    grad_w_kv_down = jnp.sum(kv_down_terms.astype(F32), axis=0)
     grad_w_query = jnp.concatenate([part.result().T for part in sums_query], axis=0)
     grad_w_kv_up = sum_kv_up.result().T
     grad_w_shared_gate, grad_w_shared_up = jnp.split(sums_gate_up, 2, axis=1)
     grad_w_shared_down = sums_down.T
-    grad_w_out = sum_out.result().T
+    grad_w_out = sums_out.T
 
     return (
         mixed_out[None],

time: 879 us -> 835 us (0.950)
  local copies, waits for them, and re-layouts: 144 us -> 120 us
  matrix products: 264 us -> 287 us
  waiting for transfers between devices: 201 us -> 180 us
  starting transfers between devices: 116 us -> 99.4 us
    ppermute x48 -> x36, starting transfers between devices: 80.5 us -> 48.5 us  [ctx_swap(): return lax.ppermute(x, 'ctx', [(i, i ^ mask) for i in range(count)])]
    all_to_all x6, waiting for transfers between devices: 29.3 us -> 2.54 us  [swap_blocks(): return lax.all_to_all(x, 'ctx', 0, 0, axis_index_groups=groups, tiled=True)]
    broadcast_in_dim x3 -> x0, other arithmetic: 17.6 us -> none  [expert_sum(): return total[None]]
    dot_general x47 -> x50, matrix products: 196 us -> 212 us  [contract(): lax.dot_general(former, latter, (((former_dim,), (latter_dim,)), ((), ())...]
    all_to_all x0 -> x2, waiting for transfers between devices: none -> 13.5 us  [the longest x1 12.2 us: per_device(): kv_down_terms = lax.all_to_all(kv_down_terms, 'ctx', 0, 0, tiled=True)]
    all_to_all x0 -> x2, starting transfers between devices: none -> 11.8 us  [the longest x1 5.99 us: per_device(): lax.all_to_all(gain_grads.reshape(n_ctx * n_wt, -1), ('ctx', 'wt'), 0, 0,...]
    ppermute x48 -> x36, waiting for transfers between devices: 169 us -> 162 us  [ctx_swap(): return lax.ppermute(x, 'ctx', [(i, i ^ mask) for i in range(count)])]
    unnamed x417 -> x413, local copies, waits for them, and re-layouts: 42.2 us -> 39.9 us
  transfers between devices with their start and end apart: 88 -> 77, of which waited for: 33 -> 28; matrix products, arithmetic and copies ran while one was open for 57% -> 58% of each run, Pallas kernels for 0% -> 0%
where the time goes in v3:
time: 835 us; the launch traced here: 824 us
  matrix products  287 us (34%)
  waiting for transfers between devices  180 us (22%)
  local copies, waits for them, and re-layouts  120 us (14%)
  other arithmetic  106 us (13%)
  starting transfers between devices  99.4 us (12%)
  between operations  32.5 us (4%)
    dot_general x50, matrix products, contract(): lax.dot_general(former, latter, (((former_dim,), (latter_dim,)), ((), ())...  212 us
    ppermute x36, waiting for transfers between devices, ctx_swap(): return lax.ppermute(x, 'ctx', [(i, i ^ mask) for i in range(count)])  162 us
    ppermute x36, starting transfers between devices, ctx_swap(): return lax.ppermute(x, 'ctx', [(i, i ^ mask) for i in range(count)])  48.5 us
    unnamed x413, local copies, waits for them, and re-layouts  39.9 us
    all_to_all x6, starting transfers between devices, swap_blocks(): return lax.all_to_all(x, 'ctx', 0, 0, axis_index_groups=groups, tiled=True)  33 us
  transfers between devices with their start and end apart: 77, of which 28 were waited for; matrix products, arithmetic and copies ran while one was open for 58% of the time, Pallas kernels for 0%

profile of v3, /device:TPU:0, one launch (start us, length us, event | category | flops | bytes accessed | tf_op | source)
XLA Modules:
  0.0 824.3 jit_solution(4755274241417363246)
XLA Ops:
  28.6 30.7 %collective-permute-done.9 = bf16[64,576]{0,1:T(8,128)(2,1)S(1)} collective-permute-done((bf16[64,576]{0,1:T(8,128)(2,1)S(1)}, bf16[64,576]{0,1:T(8,128)(2,1)S(1)}, u32[]{:S(2)}, u32[]{:S(2)}) %collective-permute-start.9) | collective-permute-done | bytes 73760 | tf_op jit(solution)/shard_map/ppermute | solution.py:138
  94.2 4.9 concatenate.286
  123.9 10.4 %fusion.3 = (f32[16,128]{1,0:T(8,128)S(1)}, f32[16,128,2048]{2,1,0:T(8,128)S(1)}) fusion(pred[128,2048]{1,0:T(8,128)(4,1)S(1)} %copy-done.98, bf16[2048,576]{0,1:T(8,128)(2,1)} %concatenate.286, bf16[16,128,64]{2,1,0:T(8,128)(2,1)S(1)} %maximum_bitcast_fusion, bf16[16,128,512]{2,1,0:T(8,128)(2,1)} %convolution_convert_fusion.11), kind=kOutput, calls=%fused_computation.10 | convolution fusion | flops 4849137664 | bytes 21766144 | tf_op jit(solution)/shard_map/htr,kr->htk/dot_general | solution.py:259
  140.1 8.5 %fusion.87 = (bf16[16,128,512]{2,1,0:T(8,128)(2,1)}, f32[16,128,512]{2,1,0:T(8,128)}) fusion(f32[16,128]{1,0:T(8,128)S(1)} %fusion, bf16[2048,576]{0,1:T(8,128)(2,1)} %concatenate.286, f32[16,128,2048]{2,1,0:T(8,128)S(1)} %get-tuple-element.348, f32[16,128]{1,0:T(8,128)S(1)} %get-tuple-element.347, pred[128,2048]{1,0:T(8,128)(4,1)S(1)} %copy-done.98), kind=kOutput, calls=%fused_computation.156 | convolution fusion | flops 4313841664 | bytes 25444352 | tf_op jit(solution)/shard_map/htk,kr->htr/dot_general | solution.py:264
  170.9 5.0 all-to-all-start.2
  177.4 4.8 fusion.232
  182.2 8.3 %fusion.37 = f32[512,1408]{1,0:T(8,128)} fusion(bf16[512,2048]{1,0:T(8,128)(2,1)} %bitcast.468, bf16[1,1408,2048]{2,1,0:T(8,128)(2,1)} %all-gather.7.cloned.1.call-done), kind=kOutput, calls=%fused_computation.43 | convolution fusion | flops 2952790016 | bytes 10747904 | tf_op jit(solution)/shard_map/dot_general | solution.py:28
  191.8 18.4 %collective-permute-done.18 = bf16[128,2048]{1,0:T(8,128)(2,1)S(1)} collective-permute-done((bf16[128,2048]{1,0:T(8,128)(2,1)S(1)}, bf16[128,2048]{1,0:T(8,128)(2,1)S(1)}, u32[]{:S(2)}, u32[]{:S(2)}) %collective-permute-start.18) | collective-permute-done | bytes 524320 | tf_op jit(solution)/shard_map/ppermute | solution.py:138
  212.3 6.0 fusion.173
  221.6 7.4 all-to-all-start.1
  229.0 8.3 %fusion.23 = f32[512,1408]{1,0:T(8,128)} fusion(bf16[512,2048]{1,0:T(8,128)(2,1)} %bitcast.37, bf16[1,2048,1408]{2,1,0:T(8,128)(2,1)} %all-gather.11.cloned.1.call-done), kind=kOutput, calls=%fused_computation.29 | convolution fusion | flops 2952790016 | bytes 10747904 | tf_op jit(solution)/shard_map/dot_general | solution.py:28
  237.4 10.5 %multiply_convert_fusion.2 = (bf16[512,1408]{1,0:T(8,128)(2,1)}, bf16[512,1408]{1,0:T(8,128)(2,1)S(1)}, bf16[512,1408]{1,0:T(8,128)(2,1)S(1)}) fusion(f32[512,1408]{1,0:T(8,128)} %fusion.23, f32[512,1408]{1,0:T(8,128)} %fusion.37, bf16[512,2048]{1,0:T(8,128)(2,1)} %bitcast.37, bf16[1,2048,1408]{2,1,0:T(8,128)(2,1)} %all-gather.9.cloned.1.call-done), kind=kOutput, calls=%fused_computation.82 | convolution fusion | flops 2963603456 | bytes 17956864 | tf_op jit(solution)/shard_map/dot_general | solution.py:28
  257.7 5.3 all-to-all-start.3
  263.0 6.6 fusion.27
  269.6 8.5 %fusion.19 = f32[512,1408]{1,0:T(8,128)} fusion(bf16[512,2048]{1,0:T(8,128)(2,1)} %bitcast.32, bf16[1,2048,1408]{2,1,0:T(8,128)(2,1)} %all-gather.11.cloned.1.call-done), kind=kOutput, calls=%fused_computation.25 | convolution fusion | flops 2952790016 | bytes 10747904 | tf_op jit(solution)/shard_map/dot_general | solution.py:28
  278.2 6.8 multiply_convert_fusion.3
  288.5 7.4 add_convert_fusion.1
  322.0 5.0 pad_maximum_fusion.4
  328.8 5.4 all-to-all-start.4
  334.2 7.4 fusion.48
  341.6 7.5 fusion.51
  371.0 17.9 %collective-permute-done.21 = bf16[128,2048]{1,0:T(8,128)(2,1)} collective-permute-done((bf16[128,2048]{1,0:T(8,128)(2,1)}, bf16[128,2048]{1,0:T(8,128)(2,1)}, u32[]{:S(2)}, u32[]{:S(2)}) %collective-permute-start.21) | collective-permute-done | bytes 524320 | tf_op jit(solution)/shard_map/ppermute | solution.py:138
  402.5 5.2 all-to-all-start.5
  421.4 10.0 %fusion.41 = f32[2048,512]{0,1:T(8,128)} fusion(bf16[16,128,512]{2,1,0:T(8,128)(2,1)} %get-tuple-element.352, f32[16,128,2048]{2,1,0:T(8,128)S(1)} %bitcast.421, f32[16,128]{1,0:T(8,128)S(1)} %copy-done.150, pred[128,2048]{1,0:T(8,128)(4,1)S(1)} %copy-done.99), kind=kOutput, calls=%fused_computation.69 | convolution fusion | flops 4311744512 | bytes 23339008 | tf_op jit(solution)/shard_map/htk,htr->kr/dot_general | solution.py:281
  431.4 11.3 %multiply_convert_fusion = bf16[16,128,2048]{2,1,0:T(8,128)(2,1)S(1)} fusion(f32[16,128,2048]{2,1,0:T(8,128)} %copy-done.10, f32[16,128]{1,0:T(8,128)S(1)} %get-tuple-element.351, f32[16,128]{1,0:T(8,128)S(1)} %copy-done.150, pred[128,2048]{1,0:T(8,128)(4,1)S(1)} %copy-done.99, bf16[16,128,512]{2,1,0:T(8,128)(2,1)} %get-tuple-element.352, ...), kind=kOutput, calls=%fused_computation.2 | convolution fusion | flops 4324327424 | bytes 29638656 | tf_op jit(solution)/shard_map/htr,kr->htk/dot_general | solution.py:277
  442.8 10.1 %bitcast_add_fusion = f32[2048,576]{0,1:T(8,128)} fusion(f32[2048,512]{0,1:T(8,128)} %fusion.41, bf16[16,128,2048]{2,1,0:T(8,128)(2,1)S(1)} %multiply_convert_fusion, bf16[16,128,64]{2,1,0:T(8,128)(2,1)S(1)} %copy-done.110, bf16[16,128,512]{2,1,0:T(8,128)(2,1)S(1)} %copy-done.60), kind=kOutput, calls=%fused_computation.50 | convolution fusion | flops 4837736448 | bytes 19660800 | tf_op jit(solution)/shard_map/htk,htr->kr/dot_general | solution.py:280
  463.3 5.3 collective-permute-start.29
  474.9 6.2 collective-permute-done.29
  504.1 7.1 collective-permute-done.34
  518.8 7.5 collective-permute-done.36
  538.1 8.4 %collective-permute-done.59 = bf16[128,6656]{1,0:T(8,128)(2,1)} collective-permute-done((bf16[128,6656]{1,0:T(8,128)(2,1)}, bf16[128,6656]{1,0:T(8,128)(2,1)}, u32[]{:S(2)}, u32[]{:S(2)}) %collective-permute-start.59) | collective-permute-done | bytes 1703968 | tf_op jit(solution)/shard_map/ppermute | solution.py:138
  555.2 8.5 %fusion.68 = f32[16,128,576]{1,2,0:T(8,128)S(1)} fusion(bf16[16,128,2048]{2,1,0:T(8,128)(2,1)} %copy-done.179, bf16[2048,576]{0,1:T(8,128)(2,1)} %concatenate.286), kind=kOutput, calls=%fused_computation.116 | convolution fusion | flops 4831838208 | bytes 15466496 | tf_op jit(solution)/shard_map/htk,kr->htr/dot_general | solution.py:279
  580.9 7.6 convolution_convert_fusion
  606.9 7.6 convolution_convert_fusion.2
  617.1 5.5 convolution_convert_fusion.3
  624.3 5.4 convolution_convert_fusion.4
  650.7 5.2 fusion.102
  667.9 6.0 all-to-all-start.6
  674.6 5.7 fusion.111
  681.6 5.8 all-to-all-start.7
  704.8 12.2 %all-to-all-done.7 = bf16[16,64,576]{2,1,0:T(8,128)(2,1)S(1)} async-done(((bf16[16,64,576]{2,1,0:T(8,128)(2,1)}), bf16[16,64,576]{2,1,0:T(8,128)(2,1)S(1)}, u32[]{:S(2)}, u32[]{:S(2)}) %all-to-all-start.7) | async-done | bytes 1179680 | tf_op jit(solution)/shard_map/all_to_all | solution.py:620
  717.9 14.9 %collective-permute-done.47 = bf16[4,1,96,1024]{3,2,0,1:T(8,128)(2,1)} collective-permute-done((bf16[4,1,96,1024]{3,2,0,1:T(8,128)(2,1)}, bf16[4,1,96,1024]{3,2,0,1:T(8,128)(2,1)}, u32[]{:S(2)}, u32[]{:S(2)}) %collective-permute-start.47) | collective-permute-done | bytes 786464 | tf_op jit(solution)/shard_map/ppermute | solution.py:138
  750.9 9.4 %add_bitcast_fusion = f32[1,704,2048]{2,1,0:T(8,128)} fusion(bf16[704,2048]{1,0:T(8,128)(2,1)} %collective-permute-done.41, bf16[1024,704]{1,0:T(8,128)(2,1)} %broadcast_select_fusion.3, bf16[512,2048]{1,0:T(8,128)(2,1)} %bitcast.465, bf16[512,2048]{1,0:T(8,128)(2,1)} %bitcast.469), kind=kOutput, calls=%fused_computation.47 | convolution fusion | flops 2964062208 | bytes 14286848 | tf_op jit(solution)/shard_map/dot_general | solution.py:28
  760.4 6.9 add_bitcast_fusion.1
  768.4 6.7 add_bitcast_fusion.2
  783.3 6.6 collective-permute-done.55
  798.9 5.2 collective-permute-done.56
  805.4 6.8 collective-permute-done.57
  (826 shorter events, 393.4 us)
Async XLA Ops:
  7.3 174.9 %all-gather.7.cloned.1.call-start = ((), (), s32[]{:S(2)}) async-start(), calls=%async_computation.14 | async-start | bytes 8650752 | tf_op jit(solution)/shard_map/all_gather | solution.py:464
  8.0 221.0 %all-gather.11.cloned.1.call-start = ((), (), s32[]{:S(2)}) async-start(), calls=%async_computation.16 | async-start | bytes 8650752 | tf_op jit(solution)/shard_map/all_gather | solution.py:462
  22.9 62.0 %collective-permute-start.16 = (bf16[128,2048]{1,0:T(8,128)(2,1)S(1)}, bf16[128,2048]{1,0:T(8,128)(2,1)S(1)}, u32[]{:S(2)}, u32[]{:S(2)}) collective-permute-start(bf16[128,2048]{1,0:T(8,128)(2,1)S(1)} %bitcast.424), channel_id=1, source_target_pairs={{0,16},{2,18},{4,20},{6,22},{8,24},{10,26},{12,28},{14,30},{16,0},... | collective-permute-start | bytes 1572872 | tf_op jit(solution)/shard_map/ppermute | solution.py:138
  22.9 57.5 %collective-permute-start.3 = (bf16[128,2048]{1,0:T(8,128)(2,1)S(1)}, bf16[128,2048]{1,0:T(8,128)(2,1)S(1)}, u32[]{:S(2)}, u32[]{:S(2)}) collective-permute-start(bf16[128,2048]{1,0:T(8,128)(2,1)S(1)} %bitcast.416), channel_id=1, source_target_pairs={{1,0},{0,1},{3,2},{2,3},{5,4},{4,5},{7,6},{6,7},{9,8},{8,9},{11,10... | collective-permute-start | bytes 1572872 | tf_op jit(solution)/shard_map/ppermute | solution.py:38
  23.0 86.8 %collective-permute-start.2 = (bf16[256,4096]{1,0:T(8,128)(2,1)}, bf16[256,4096]{1,0:T(8,128)(2,1)}, u32[]{:S(2)}, u32[]{:S(2)}) collective-permute-start(bf16[256,4096]{1,0:T(8,128)(2,1)} %param.28), channel_id=1, source_target_pairs={{1,0},{0,1},{3,2},{2,3},{5,4},{4,5},{7,6},{6,7},{9,8},{8,9},{11,10... | collective-permute-start | bytes 6291464 | tf_op jit(solution)/shard_map/ppermute | solution.py:38
  24.4 34.9 %collective-permute-start.9 = (bf16[64,576]{0,1:T(8,128)(2,1)S(1)}, bf16[64,576]{0,1:T(8,128)(2,1)S(1)}, u32[]{:S(2)}, u32[]{:S(2)}) collective-permute-start(bf16[64,576]{0,1:T(8,128)(2,1)S(1)} %get-tuple-element.328), channel_id=1, source_target_pairs={{0,16},{2,18},{4,20},{6,22},{8,24},{10,26},{12,28},{14,30},{16,0},... | collective-permute-start | bytes 221192 | tf_op jit(solution)/shard_map/ppermute | solution.py:138
  27.3 34.1 %collective-permute-start.5 = (bf16[64,576]{0,1:T(8,128)(2,1)S(1)}, bf16[64,576]{0,1:T(8,128)(2,1)S(1)}, u32[]{:S(2)}, u32[]{:S(2)}) collective-permute-start(bf16[64,576]{0,1:T(8,128)(2,1)S(1)} %get-tuple-element.329), channel_id=1, source_target_pairs={{0,16},{2,18},{4,20},{6,22},{8,24},{10,26},{12,28},{14,30},{16,0},... | collective-permute-start | bytes 221192 | tf_op jit(solution)/shard_map/ppermute | solution.py:138
  74.1 20.1 %collective-permute-start.12 = (bf16[512,576]{0,1:T(8,128)(2,1)}, bf16[512,576]{0,1:T(8,128)(2,1)}, u32[]{:S(2)}, u32[]{:S(2)}) collective-permute-start(bf16[512,576]{0,1:T(8,128)(2,1)} %pad_maximum_fusion.47), channel_id=1, source_target_pairs={{0,4},{2,6},{4,0},{6,2},{8,12},{10,14},{12,8},{14,10},{16,20},{18,... | collective-permute-start | bytes 1769480 | tf_op jit(solution)/shard_map/ppermute | solution.py:138
  79.1 15.2 %collective-permute-start.8 = (bf16[512,576]{0,1:T(8,128)(2,1)}, bf16[512,576]{0,1:T(8,128)(2,1)}, u32[]{:S(2)}, u32[]{:S(2)}) collective-permute-start(bf16[512,576]{0,1:T(8,128)(2,1)} %pad_maximum_fusion.46), channel_id=1, source_target_pairs={{0,2},{2,0},{4,6},{6,4},{8,10},{10,8},{12,14},{14,12},{16,18},{18,... | collective-permute-start | bytes 1769480 | tf_op jit(solution)/shard_map/ppermute | solution.py:138
  88.9 80.0 %all-to-all-start = ((bf16[8,128,2048]{2,1,0:T(8,128)(2,1)}), bf16[8,128,2048]{2,1,0:T(8,128)(2,1)}, u32[]{:S(2)}, u32[]{:S(2)}) async-start(bf16[8,128,2048]{2,1,0:T(8,128)(2,1)} %pad_maximum_fusion.2), calls=%async_computation | async-start | bytes 8388608 | tf_op jit(solution)/shard_map/all_to_all | solution.py:430
  93.7 143.7 %all-gather.9.cloned.1.call-start = ((), (), s32[]{:S(2)}) async-start(), calls=%async_computation.15 | async-start | bytes 8650752 | tf_op jit(solution)/shard_map/all_gather | solution.py:463
  163.2 150.3 %collective-permute-start.23 = (bf16[128,2048]{1,0:T(8,128)(2,1)S(1)}, bf16[128,2048]{1,0:T(8,128)(2,1)}, u32[]{:S(2)}, u32[]{:S(2)}) collective-permute-start(bf16[128,2048]{1,0:T(8,128)(2,1)S(1)} %bitcast.425), channel_id=1, source_target_pairs={{1,0},{0,1},{3,2},{2,3},{5,4},{4,5},{7,6},{6,7},{9,8},{8,9},{11,10... | collective-permute-start | bytes 1572872 | tf_op jit(solution)/shard_map/ppermute | solution.py:38
  170.9 50.6 %all-to-all-start.2 = ((bf16[8,64,2048]{2,1,0:T(8,128)(2,1)}), bf16[8,64,2048]{2,1,0:T(8,128)(2,1)}, u32[]{:S(2)}, u32[]{:S(2)}) async-start(bf16[8,64,2048]{2,1,0:T(8,128)(2,1)} %bitcast.435), calls=%async_computation.2 | async-start | bytes 4194304 | tf_op jit(solution)/shard_map/all_to_all | solution.py:430
  177.4 32.8 %collective-permute-start.18 = (bf16[128,2048]{1,0:T(8,128)(2,1)S(1)}, bf16[128,2048]{1,0:T(8,128)(2,1)S(1)}, u32[]{:S(2)}, u32[]{:S(2)}) collective-permute-start(bf16[128,2048]{1,0:T(8,128)(2,1)S(1)} %multiply_convert_fusion.11), channel_id=1, source_target_pairs={{0,16},{2,18},{4,20},{6,22},{8,24},{10,26},{12,28},{14,30},{16,0},... | collective-permute-start | bytes 1572872 | tf_op jit(solution)/shard_map/ppermute | solution.py:138
  221.6 36.1 %all-to-all-start.1 = ((bf16[8,64,2048]{2,1,0:T(8,128)(2,1)}), bf16[8,64,2048]{2,1,0:T(8,128)(2,1)}, u32[]{:S(2)}, u32[]{:S(2)}) async-start(bf16[8,64,2048]{2,1,0:T(8,128)(2,1)} %bitcast.436), calls=%async_computation.1 | async-start | bytes 4194304 | tf_op jit(solution)/shard_map/all_to_all | solution.py:430
  257.7 38.2 %all-to-all-start.3 = ((bf16[8,64,2048]{2,1,0:T(8,128)(2,1)}), bf16[8,64,2048]{2,1,0:T(8,128)(2,1)}, u32[]{:S(2)}, u32[]{:S(2)}) async-start(bf16[8,64,2048]{2,1,0:T(8,128)(2,1)} %bitcast.458), calls=%async_computation.3 | async-start | bytes 4194304 | tf_op jit(solution)/shard_map/all_to_all | solution.py:430
  321.4 27.6 %collective-permute-start.24 = (bf16[256,4224]{1,0:T(8,128)(2,1)}, bf16[256,4224]{1,0:T(8,128)(2,1)}, u32[]{:S(2)}, u32[]{:S(2)}) collective-permute-start(bf16[256,4224]{1,0:T(8,128)(2,1)} %pad_maximum_fusion.18), channel_id=1, source_target_pairs={{1,0},{0,1},{3,2},{2,3},{5,4},{4,5},{7,6},{6,7},{9,8},{8,9},{11,10... | collective-permute-start | bytes 6488072 | tf_op jit(solution)/shard_map/ppermute | solution.py:38
  328.8 31.4 %all-to-all-start.4 = ((bf16[8,64,2048]{2,1,0:T(8,128)(2,1)}), bf16[8,64,2048]{2,1,0:T(8,128)(2,1)}, u32[]{:S(2)}, u32[]{:S(2)}) async-start(bf16[8,64,2048]{2,1,0:T(8,128)(2,1)} %bitcast.456), calls=%async_computation.4 | async-start | bytes 4194304 | tf_op jit(solution)/shard_map/all_to_all | solution.py:430
  363.2 25.7 %collective-permute-start.21 = (bf16[128,2048]{1,0:T(8,128)(2,1)}, bf16[128,2048]{1,0:T(8,128)(2,1)}, u32[]{:S(2)}, u32[]{:S(2)}) collective-permute-start(bf16[128,2048]{1,0:T(8,128)(2,1)} %fusion.61), channel_id=1, source_target_pairs={{0,16},{2,18},{4,20},{6,22},{8,24},{10,26},{12,28},{14,30},{16,0},... | collective-permute-start | bytes 1572872 | tf_op jit(solution)/shard_map/ppermute | solution.py:138
  370.4 42.8 %collective-permute-start.61 = (bf16[128,3840]{1,0:T(8,128)(2,1)}, bf16[128,3840]{1,0:T(8,128)(2,1)}, u32[]{:S(2)}, u32[]{:S(2)}) collective-permute-start(bf16[128,3840]{1,0:T(8,128)(2,1)} %pad_maximum_fusion.38), channel_id=1, source_target_pairs={{0,4},{2,6},{4,0},{6,2},{8,12},{10,14},{12,8},{14,10},{16,20},{18,... | collective-permute-start | bytes 2949128 | tf_op jit(solution)/shard_map/ppermute | solution.py:138
  402.5 55.2 %all-to-all-start.5 = ((bf16[8,128,2048]{2,1,0:T(8,128)(2,1)}), bf16[8,128,2048]{2,1,0:T(8,128)(2,1)}, u32[]{:S(2)}, u32[]{:S(2)}) async-start(bf16[8,128,2048]{2,1,0:T(8,128)(2,1)} %pad_maximum_fusion.3), calls=%async_computation.5 | async-start | bytes 8388608 | tf_op jit(solution)/shard_map/all_to_all | solution.py:430
  407.7 190.5 %reduce-scatter.8.cloned.1.call-start = ((), (), s32[]{:S(2)}) async-start(), calls=%async_computation.13 | async-start | bytes 3244032 | tf_op jit(solution)/shard_map/reduce_scatter | solution.py:513
  415.0 37.9 %collective-permute-start.62 = (bf16[256,3840]{1,0:T(8,128)(2,1)S(1)}, bf16[256,3840]{1,0:T(8,128)(2,1)}, u32[]{:S(2)}, u32[]{:S(2)}) collective-permute-start(bf16[256,3840]{1,0:T(8,128)(2,1)S(1)} %pad_maximum_fusion.19), channel_id=1, source_target_pairs={{1,0},{0,1},{3,2},{2,3},{5,4},{4,5},{7,6},{6,7},{9,8},{8,9},{11,10... | collective-permute-start | bytes 5898248 | tf_op jit(solution)/shard_map/ppermute | solution.py:38
  463.3 17.7 %collective-permute-start.29 = (bf16[512,576]{0,1:T(8,128)(2,1)}, bf16[512,576]{0,1:T(8,128)(2,1)}, u32[]{:S(2)}, u32[]{:S(2)}) collective-permute-start(bf16[512,576]{0,1:T(8,128)(2,1)} %get-tuple-element.289), channel_id=1, source_target_pairs={{0,2},{2,0},{4,6},{6,4},{8,10},{10,8},{12,14},{14,12},{16,18},{18,... | collective-permute-start | bytes 1769480 | tf_op jit(solution)/shard_map/ppermute | solution.py:138
  474.8 338.3 %reduce-scatter.4.cloned.1.call-start = ((), (), s32[]{:S(2)}) async-start(), calls=%async_computation.11 | async-start | bytes 2359296 | tf_op jit(solution)/shard_map/reduce_scatter | solution.py:513
  491.3 24.6 %collective-permute-start.42 = (bf16[128,3072]{0,1:T(8,128)(2,1)}, bf16[128,3072]{0,1:T(8,128)(2,1)S(1)}, u32[]{:S(2)}, u32[]{:S(2)}) collective-permute-start(bf16[128,3072]{0,1:T(8,128)(2,1)} %pad_maximum_fusion.39), channel_id=1, source_target_pairs={{0,4},{2,6},{4,0},{6,2},{8,12},{10,14},{12,8},{14,10},{16,20},{18,... | collective-permute-start | bytes 2359304 | tf_op jit(solution)/shard_map/ppermute | solution.py:138
  501.5 45.0 %collective-permute-start.59 = (bf16[128,6656]{1,0:T(8,128)(2,1)}, bf16[128,6656]{1,0:T(8,128)(2,1)}, u32[]{:S(2)}, u32[]{:S(2)}) collective-permute-start(bf16[128,6656]{1,0:T(8,128)(2,1)} %pad_maximum_fusion.28), channel_id=1, source_target_pairs={{0,2},{2,0},{4,6},{6,4},{8,10},{10,8},{12,14},{14,12},{16,18},{18,... | collective-permute-start | bytes 5111816 | tf_op jit(solution)/shard_map/ppermute | solution.py:138
  530.0 20.8 %collective-permute-start.58 = (bf16[256,3072]{0,1:T(8,128)(2,1)}, bf16[256,3072]{0,1:T(8,128)(2,1)}, u32[]{:S(2)}, u32[]{:S(2)}) collective-permute-start(bf16[256,3072]{0,1:T(8,128)(2,1)} %pad_maximum_fusion.31), channel_id=1, source_target_pairs={{1,0},{0,1},{3,2},{2,3},{5,4},{4,5},{7,6},{6,7},{9,8},{8,9},{11,10... | collective-permute-start | bytes 4718600 | tf_op jit(solution)/shard_map/ppermute | solution.py:38
  536.9 137.1 %collective-permute-start.20 = (f32[128,2048]{1,0:T(8,128)}, f32[128,2048]{1,0:T(8,128)}, u32[]{:S(2)}, u32[]{:S(2)}) collective-permute-start(f32[128,2048]{1,0:T(8,128)} %slice.614), channel_id=1, source_target_pairs={{0,1},{1,0},{2,3},{3,2},{4,5},{5,4},{6,7},{7,6},{8,9},{9,8},{10,11... | collective-permute-start | bytes 3145736 | tf_op jit(solution)/shard_map/ppermute | solution.py:43
  549.1 26.1 %collective-permute-start.60 = (bf16[256,6656]{1,0:T(8,128)(2,1)S(1)}, bf16[256,6656]{1,0:T(8,128)(2,1)}, u32[]{:S(2)}, u32[]{:S(2)}) collective-permute-start(bf16[256,6656]{1,0:T(8,128)(2,1)S(1)} %pad_maximum_fusion.7), channel_id=1, source_target_pairs={{1,0},{0,1},{3,2},{2,3},{5,4},{4,5},{7,6},{6,7},{9,8},{8,9},{11,10... | collective-permute-start | bytes 10223624 | tf_op jit(solution)/shard_map/ppermute | solution.py:38
  555.1 259.7 %reduce-scatter.6.cloned.1.call-start = ((), (), s32[]{:S(2)}) async-start(), calls=%async_computation.12 | async-start | bytes 6488064 | tf_op jit(solution)/shard_map/reduce_scatter | solution.py:513
  568.3 82.1 %collective-permute-start.28 = (bf16[128,3072]{0,1:T(8,128)(2,1)}, bf16[128,3072]{0,1:T(8,128)(2,1)}, u32[]{:S(2)}, u32[]{:S(2)}) collective-permute-start(bf16[128,3072]{0,1:T(8,128)(2,1)} %bitcast.58), channel_id=1, source_target_pairs={{1,0},{0,1},{3,2},{2,3},{5,4},{4,5},{7,6},{6,7},{9,8},{8,9},{11,10... | collective-permute-start | bytes 2359304 | tf_op jit(solution)/shard_map/ppermute | solution.py:38
  594.3 80.1 %collective-permute-start.22 = (bf16[128,2048]{1,0:T(8,128)(2,1)}, bf16[128,2048]{1,0:T(8,128)(2,1)}, u32[]{:S(2)}, u32[]{:S(2)}) collective-permute-start(bf16[128,2048]{1,0:T(8,128)(2,1)} %fusion.60), channel_id=1, source_target_pairs={{0,16},{2,18},{4,20},{6,22},{8,24},{10,26},{12,28},{14,30},{16,0},... | collective-permute-start | bytes 1572872 | tf_op jit(solution)/shard_map/ppermute | solution.py:138
  602.5 53.5 %collective-permute-start.43 = (bf16[128,2560]{0,1:T(8,128)(2,1)}, bf16[128,2560]{0,1:T(8,128)(2,1)}, u32[]{:S(2)}, u32[]{:S(2)}) collective-permute-start(bf16[128,2560]{0,1:T(8,128)(2,1)} %pad_maximum_fusion.44), channel_id=1, source_target_pairs={{0,2},{2,0},{4,6},{6,4},{8,10},{10,8},{12,14},{14,12},{16,18},{18,... | collective-permute-start | bytes 1966088 | tf_op jit(solution)/shard_map/ppermute | solution.py:138
  644.7 19.1 %collective-permute-start.44 = (bf16[128,2560]{0,1:T(8,128)(2,1)S(1)}, bf16[128,2560]{0,1:T(8,128)(2,1)S(1)}, u32[]{:S(2)}, u32[]{:S(2)}) collective-permute-start(bf16[128,2560]{0,1:T(8,128)(2,1)S(1)} %copy-done.107), channel_id=1, source_target_pairs={{0,4},{2,6},{4,0},{6,2},{8,12},{10,14},{12,8},{14,10},{16,20},{18,... | collective-permute-start | bytes 1966088 | tf_op jit(solution)/shard_map/ppermute | solution.py:138
  650.4 89.2 %collective-permute-start.41 = (bf16[704,2048]{1,0:T(8,128)(2,1)}, bf16[704,2048]{1,0:T(8,128)(2,1)}, u32[]{:S(2)}, u32[]{:S(2)}) collective-permute-start(bf16[704,2048]{1,0:T(8,128)(2,1)} %convolution_convert_fusion.4), channel_id=1, source_target_pairs={{0,1},{1,0},{2,3},{3,2},{4,5},{5,4},{6,7},{7,6},{8,9},{9,8},{10,11... | collective-permute-start | bytes 8650760 | tf_op jit(solution)/shard_map/ppermute | solution.py:43
  663.8 23.7 %collective-permute-start.46 = (bf16[256,2560]{0,1:T(8,128)(2,1)}, bf16[256,2560]{0,1:T(8,128)(2,1)}, u32[]{:S(2)}, u32[]{:S(2)}) collective-permute-start(bf16[256,2560]{0,1:T(8,128)(2,1)} %pad_maximum_fusion.33), channel_id=1, source_target_pairs={{1,0},{0,1},{3,2},{2,3},{5,4},{4,5},{7,6},{6,7},{9,8},{8,9},{11,10... | collective-permute-start | bytes 3932168 | tf_op jit(solution)/shard_map/ppermute | solution.py:38
  666.3 76.3 %collective-permute-start.40 = (bf16[1024,1408]{1,0:T(8,128)(2,1)}, bf16[1024,1408]{1,0:T(8,128)(2,1)}, u32[]{:S(2)}, u32[]{:S(2)}) collective-permute-start(bf16[1024,1408]{1,0:T(8,128)(2,1)} %convolution_convert_fusion.2), channel_id=1, source_target_pairs={{0,1},{1,0},{2,3},{3,2},{4,5},{5,4},{6,7},{7,6},{8,9},{9,8},{10,11... | collective-permute-start | bytes 8650760 | tf_op jit(solution)/shard_map/ppermute | solution.py:43
  674.0 70.5 %collective-permute-start.39 = (bf16[1024,1408]{1,0:T(8,128)(2,1)}, bf16[1024,1408]{1,0:T(8,128)(2,1)}, u32[]{:S(2)}, u32[]{:S(2)}) collective-permute-start(bf16[1024,1408]{1,0:T(8,128)(2,1)} %convolution_convert_fusion.3), channel_id=1, source_target_pairs={{0,1},{1,0},{2,3},{3,2},{4,5},{5,4},{6,7},{7,6},{8,9},{9,8},{10,11... | collective-permute-start | bytes 8650760 | tf_op jit(solution)/shard_map/ppermute | solution.py:43
  674.4 20.8 %collective-permute-start.50 = (bf16[256,2560]{0,1:T(8,128)(2,1)}, bf16[256,2560]{0,1:T(8,128)(2,1)}, u32[]{:S(2)}, u32[]{:S(2)}) collective-permute-start(bf16[256,2560]{0,1:T(8,128)(2,1)} %copy-done.29), channel_id=1, source_target_pairs={{1,0},{0,1},{3,2},{2,3},{5,4},{4,5},{7,6},{6,7},{9,8},{8,9},{11,10... | collective-permute-start | bytes 3932168 | tf_op jit(solution)/shard_map/ppermute | solution.py:38
  681.6 35.4 %all-to-all-start.7 = ((bf16[16,64,576]{2,1,0:T(8,128)(2,1)}), bf16[16,64,576]{2,1,0:T(8,128)(2,1)S(1)}, u32[]{:S(2)}, u32[]{:S(2)}) async-start(bf16[16,64,576]{2,1,0:T(8,128)(2,1)} %bitcast.442), calls=%async_computation.7 | async-start | bytes 2621440 | tf_op jit(solution)/shard_map/all_to_all | solution.py:620
  695.2 37.6 %collective-permute-start.47 = (bf16[4,1,96,1024]{3,2,0,1:T(8,128)(2,1)}, bf16[4,1,96,1024]{3,2,0,1:T(8,128)(2,1)}, u32[]{:S(2)}, u32[]{:S(2)}) collective-permute-start(bf16[4,1,96,1024]{3,2,0,1:T(8,128)(2,1)} %dynamic-slice_bitcast_fusion.2), channel_id=1, source_target_pairs={{0,4},{2,6},{4,0},{6,2},{8,12},{10,14},{12,8},{14,10},{16,20},{18,... | collective-permute-start | bytes 2359304 | tf_op jit(solution)/shard_map/ppermute | solution.py:138
  701.2 34.3 %collective-permute-start.51 = (bf16[4,1,96,1024]{3,2,0,1:T(8,128)(2,1)}, bf16[4,1,96,1024]{3,2,0,1:T(8,128)(2,1)}, u32[]{:S(2)}, u32[]{:S(2)}) collective-permute-start(bf16[4,1,96,1024]{3,2,0,1:T(8,128)(2,1)} %dynamic-slice_bitcast_fusion.1), channel_id=1, source_target_pairs={{0,2},{2,0},{4,6},{6,4},{8,10},{10,8},{12,14},{14,12},{16,18},{18,... | collective-permute-start | bytes 2359304 | tf_op jit(solution)/shard_map/ppermute | solution.py:138
  732.8 42.4 %collective-permute-start.54 = (bf16[8,1,128,512]{3,2,0,1:T(8,128)(2,1)}, bf16[8,1,128,512]{3,2,0,1:T(8,128)(2,1)}, u32[]{:S(2)}, u32[]{:S(2)}) collective-permute-start(bf16[8,1,128,512]{3,2,0,1:T(8,128)(2,1)} %dynamic-slice_bitcast_fusion), channel_id=1, source_target_pairs={{0,2},{2,0},{4,6},{6,4},{8,10},{10,8},{12,14},{14,12},{16,18},{18,... | collective-permute-start | bytes 3145736 | tf_op jit(solution)/shard_map/ppermute | solution.py:138
  735.5 42.3 %collective-permute-start.48 = (bf16[2,1,96,1024]{3,2,0,1:T(8,128)(2,1)S(1)}, bf16[2,1,96,1024]{3,2,0,1:T(8,128)(2,1)}, u32[]{:S(2)}, u32[]{:S(2)}) collective-permute-start(bf16[2,1,96,1024]{3,2,0,1:T(8,128)(2,1)S(1)} %dynamic-slice_bitcast_fusion.5), channel_id=1, source_target_pairs={{0,8},{2,10},{4,12},{6,14},{8,0},{10,2},{12,4},{14,6},{16,24},{18,... | collective-permute-start | bytes 1179656 | tf_op jit(solution)/shard_map/ppermute | solution.py:138
  739.6 42.4 %collective-permute-start.52 = (bf16[2,1,96,1024]{3,2,1,0:T(8,128)(2,1)}, bf16[2,1,96,1024]{3,2,1,0:T(8,128)(2,1)}, u32[]{:S(2)}, u32[]{:S(2)}) collective-permute-start(bf16[2,1,96,1024]{3,2,1,0:T(8,128)(2,1)} %dynamic-slice_bitcast_fusion.4), channel_id=1, source_target_pairs={{0,8},{2,10},{4,12},{6,14},{8,0},{10,2},{12,4},{14,6},{16,24},{18,... | collective-permute-start | bytes 1179656 | tf_op jit(solution)/shard_map/ppermute | solution.py:138
  779.0 16.6 %collective-permute-start.49 = (bf16[1,1,96,1024]{3,2,0,1:T(8,128)(2,1)S(1)}, bf16[1,1,96,1024]{3,2,0,1:T(8,128)(2,1)S(1)}, u32[]{:S(2)}, u32[]{:S(2)}) collective-permute-start(bf16[1,1,96,1024]{3,2,0,1:T(8,128)(2,1)S(1)} %constant_dynamic-slice_fusion.2), channel_id=1, source_target_pairs={{0,16},{2,18},{4,20},{6,22},{8,24},{10,26},{12,28},{14,30},{16,0},... | collective-permute-start | bytes 589832 | tf_op jit(solution)/shard_map/ppermute | solution.py:138
  783.2 15.6 %collective-permute-start.53 = (bf16[1,1,96,1024]{3,2,1,0:T(8,128)(2,1)S(1)}, bf16[1,1,96,1024]{3,2,1,0:T(8,128)(2,1)S(1)}, u32[]{:S(2)}, u32[]{:S(2)}) collective-permute-start(bf16[1,1,96,1024]{3,2,1,0:T(8,128)(2,1)S(1)} %constant_dynamic-slice_fusion.1), channel_id=1, source_target_pairs={{0,16},{2,18},{4,20},{6,22},{8,24},{10,26},{12,28},{14,30},{16,0},... | collective-permute-start | bytes 589832 | tf_op jit(solution)/shard_map/ppermute | solution.py:138
  (227 other events, 2327.0 us)
Sparse Core Ops, SparseCore 0:
  9.7 21.9 all-gather.6
  33.2 17.4 all-gather.10
  159.1 15.4 all-gather.8
  474.9 82.6 reduce-scatter.7
  560.9 68.2 reduce-scatter.3
  632.7 145.2 reduce-scatter.5
